TPU v7x, 512 devices: a whole 4x4x16 slice. The times are simulated.
512 devices in a mesh: wide: 64 (over z, y), narrow: 8 (over x, core).
Axes of the slice: x: 4, y: 4, z: 16, core: 2. Of those that a mesh axis runs over, the one named last changes fastest.
Arguments:
- density: bfloat16 [32, 262144], P(None, ('wide', 'narrow')), may hold values from -6 to 6
- panels: float32 [7, 262144], P(None, ('wide', 'narrow')), as said below
- near_mask: int32 [2048, 8], P(('wide', 'narrow')), may hold values from 0 to 1, as said below
- source_basis: bfloat16 [64, 262144], P(None, ('wide', 'narrow')), may hold values from -0.5 to 0.5
- leaf_transfer: bfloat16 [2048, 64, 64], P(('wide', 'narrow')), may hold values from -0.375 to 0.375
- cluster_coupling: bfloat16 [512, 512, 64], P(('wide', 'narrow')), may hold values from -0.25 to 0.25
- out_leaf: int32 [32768], P(('wide', 'narrow')), may hold values from 0 to 3
- out_wide: int32 [32768, 1], P(('wide', 'narrow')), may hold values from 0 to 63; in each aligned block of 64 rows (0 to 63, 64 to 127, ...) at most 2 rows name the same one
- out_target: int32 [32768], P(('wide', 'narrow')), may hold values from 0 to 3
- coupling: bfloat16 [32768, 64, 64], P(('wide', 'narrow')), may hold values from -0.1875 to 0.1875
- target_basis: bfloat16 [64, 262144], P(None, ('wide', 'narrow')), may hold values from -0.75 to 0.75
Outputs:
- first_pass: bfloat16 [32, 262144], P(None, ('wide', 'narrow'))
- second_pass: bfloat16 [32, 262144], P(None, ('wide', 'narrow'))
Inputs may be any that keep to these rules, and one draw needn't show every extreme that they name: `panels`: rows 0 to 2 hold panel positions, rows 3 to 5 unit normals, row 6 panel areas between 0.05 and 0.4. near_mask[g, c] is 0 wherever c % 4 and g % 4 differ by more than 1, and 1 where c = g % 4. `out_wide`: among the 64 coupling blocks of one device no wide index is named more than 2 times, and some wide index is named exactly 2 times.
All inputs are finite; a program needn't handle non-finite values.
Results may differ from a plain program's by a relative error of at most 0.012.
Values may be sent and summed in bfloat16 or wider, within the bound.
No kernel may reach another device: no remote copies, remote signals or barrier semaphores. Data moves between devices by JAX's collectives and lax.ppermute only.
A program may use at most 64 MiB of HBM per device.

v0:
```python
import math

import jax
import jax.numpy as jnp
from jax import lax
from jax.sharding import PartitionSpec as P

LEAF_SIZE = 128
RANK = 64
RIGHT_SIDES = 32


SMOOTHING = 0.0625


def partner(block, axis, distance):
    count = lax.axis_size(axis)
    route = []
    for low in range(count):
        high = low | 1 << distance
        if high != low and high < count:
            route += [(low, high), (high, low)]
    return lax.ppermute(block, axis, route)


def kernel_block(target_pos, source_geom):
    offsets = target_pos[:, :, None] - source_geom[0:3, None, :]
    squared = jnp.sum(offsets * offsets, axis=0) + SMOOTHING
    normal_dot = jnp.sum(source_geom[3:6, None, :] * offsets, axis=0)
    return source_geom[6][None, :] * normal_dot / (4.0 * math.pi * squared * jnp.sqrt(squared))


def nearby_field(own_geom, source_geom, source_density, near_mask):
    leaf_count = near_mask.shape[0]
    target_pos = jnp.transpose(own_geom[0:3].reshape(3, leaf_count, LEAF_SIZE), (1, 0, 2))
    weights = jnp.repeat(near_mask.astype(jnp.bfloat16), LEAF_SIZE, axis=1)

    def leaf_near(inputs):
        position, weight_row = inputs
        kernel = kernel_block(position, source_geom).astype(jnp.bfloat16) * weight_row[None, :]
        return lax.dot_general(
            source_density, kernel, (((1,), (1,)), ((), ())), preferred_element_type=jnp.float32
        )

    blocks = lax.map(leaf_near, (target_pos, weights))
    return jnp.transpose(blocks, (1, 0, 2)).reshape(RIGHT_SIDES, leaf_count * LEAF_SIZE)


def shards(
    density,
    panels,
    near_mask,
    source_basis,
    leaf_transfer,
    cluster_coupling,
    out_leaf,
    out_wide,
    out_target,
    coupling,
    target_basis,
):
    leaf_count = near_mask.shape[0]
    out_count = out_leaf.shape[0]
    row_width = RIGHT_SIDES * RANK
    partner_geom = partner(panels, "narrow", 0)
    source_geom = jnp.concatenate([panels, partner_geom], axis=1)
    coupling_rows = cluster_coupling[0]

    def fold_cluster(pieces):
        count = pieces.shape[0]
        slab = coupling_rows.reshape(count, RANK, RANK)
        return jnp.einsum("mrk,mkj->rj", pieces, slab, preferred_element_type=jnp.float32)

    def apply_operator(values):
        coeffs = jnp.einsum(
            "rls,kls->lrk",
            values.reshape(RIGHT_SIDES, leaf_count, LEAF_SIZE),
            source_basis.reshape(RANK, leaf_count, LEAF_SIZE),
            preferred_element_type=jnp.float32,
        ).astype(jnp.bfloat16)
        cluster = jnp.einsum(
            "lrk,lkj->rj", coeffs, leaf_transfer, preferred_element_type=jnp.float32
        ).astype(jnp.bfloat16)
        downward = fold_cluster(lax.all_gather(cluster[None], "narrow", axis=0, tiled=True))
        picked = jnp.take(coeffs, out_leaf, axis=0)
        products = jnp.einsum(
            "erk,ekj->erj", picked, coupling, preferred_element_type=jnp.float32
        ).reshape(out_count, row_width)
        wide_count = lax.axis_size("wide")
        destination = out_wide[:, 0] * leaf_count + out_target
        outgoing = jax.ops.segment_sum(products, destination, num_segments=wide_count * leaf_count)
        received = lax.all_to_all(
            outgoing.reshape(wide_count, leaf_count, row_width),
            "wide",
            split_axis=0,
            concat_axis=0,
            tiled=True,
        )
        leaf_field = jnp.sum(received, axis=0)
        spread = jnp.einsum(
            "rk,ljk->lrj",
            downward,
            leaf_transfer.astype(jnp.float32),
            precision=lax.Precision.HIGHEST,
        )
        leaf_field = (leaf_field.reshape(leaf_count, RIGHT_SIDES, RANK) + spread).astype(
            jnp.bfloat16
        )
        far_part = jnp.einsum(
            "lrk,kls->rls",
            leaf_field,
            target_basis.reshape(RANK, leaf_count, LEAF_SIZE),
            preferred_element_type=jnp.float32,
        ).reshape(RIGHT_SIDES, leaf_count * LEAF_SIZE)
        partner_values = partner(values, "narrow", 0)
        source_density = jnp.concatenate([values, partner_values], axis=1)
        near_part = nearby_field(panels, source_geom, source_density, near_mask)
        return (0.5 * values.astype(jnp.float32) + near_part + far_part).astype(jnp.bfloat16)

    first_pass = apply_operator(density)
    second_pass = apply_operator(first_pass)
    return (first_pass, second_pass)


def solution(mesh):
    in_specs = (
        P(None, ("wide", "narrow")),
        P(None, ("wide", "narrow")),
        P(("wide", "narrow"), None),
        P(None, ("wide", "narrow")),
        P(("wide", "narrow"), None, None),
        P(("wide", "narrow"), None, None),
        P(("wide", "narrow")),
        P(("wide", "narrow"), None),
        P(("wide", "narrow")),
        P(("wide", "narrow"), None, None),
        P(None, ("wide", "narrow")),
    )
    out_specs = (P(None, ("wide", "narrow")), P(None, ("wide", "narrow")))
    return jax.shard_map(shards, mesh=mesh, in_specs=in_specs, out_specs=out_specs, check_vma=False)
```

profile of v0, /device:TPU:4, one launch (start us, length us, event | category | flops | bytes accessed | tf_op | source)
XLA Modules:
  0.0 244.8 jit_solution(11260027841969366444)
XLA Ops:
  0.6 0.7 compare_select_fusion
  1.4 0.7 compare_and_fusion
  2.1 1.0 convolution_convert_fusion.1
  3.0 0.7 gather_fusion
  3.8 0.5 fusion.26
  4.2 1.2 reshape.107
  5.4 2.4 scatter_custom_fusion
  7.8 1.7 reshape.77
  9.5 18.9 %all-to-all-start = ((f32[64,4,2048]{2,1,0:T(4,128)}), f32[64,4,2048]{2,1,0:T(4,128)S(1)}, u32[]{:S(2)}, u32[]{:S(2)}) async-start(f32[64,4,2048]{2,1,0:T(4,128)} %reshape.77), calls=%async_computation | async-start | bytes 4194304 | tf_op jit(solution)/shard_map/all_to_all | solution.py:92
  28.4 1.9 collective-permute-start.1
  30.3 2.4 collective-permute-start
  33.1 11.5 %all-gather = bf16[256,64]{1,0:T(8,128)(2,1)S(1)} all-gather(bf16[32,64]{1,0:T(8,128)(2,1)S(1)} %fusion.18), channel_id=2, replica_groups=mesh['wide'=64,'narrow'=8] {'narrow'}, dimensions={0}, use_global_device_ids=true | all-gather | bytes 36864 | tf_op jit(solution)/shard_map/all_gather | solution.py:84
  44.9 1.4 pad_maximum_fusion
  46.3 6.6 %while.20 = (s32[]{:T(128)}, f32[4,32,128]{2,1,0:T(8,128)S(1)}, f32[7,1024]{1,0:T(8,128)S(1)}, f32[4,3,128]{2,1,0:T(4,128)S(1)}, bf16[4,1024]{1,0:T(4,128)(2,1)S(1)}, /*index=5*/bf16[32,1024]{1,0:T(8,128)(2,1)}, s32[]{:T(128)}) while((s32[]{:T(128)}, f32[4,32,128]{2,1,0:T(8,128)S(1)}, f32[7,1024]{1,0:T(8,128)S(1)}, ...), condition=%wide.region_3.4_spmd, body=%wide.region_0.3_spmd.sunk | while | flops 11010050 | bytes 2275929 | solution.py:45
  46.8 1.2 fusion.92
  48.4 1.2 fusion.92
  50.0 1.2 fusion.92
  51.7 1.2 fusion.92
  52.9 75.7 %all-to-all-done = f32[64,4,2048]{2,1,0:T(4,128)S(1)} async-done(((f32[64,4,2048]{2,1,0:T(4,128)}), f32[64,4,2048]{2,1,0:T(4,128)S(1)}, u32[]{:S(2)}, u32[]{:S(2)}) %all-to-all-start) | async-done | bytes 2097184 | tf_op jit(solution)/shard_map/all_to_all | solution.py:92
  129.3 1.0 convolution_bitcast_fusion.4
  130.3 1.0 convolution_convert_fusion
  131.3 0.7 gather_fusion.1
  132.0 0.5 fusion.24
  132.5 1.2 reshape.115
  133.6 2.4 scatter_custom_fusion.1
  136.0 1.7 reshape.84
  137.7 5.8 %all-to-all-start.1 = ((f32[64,4,2048]{2,1,0:T(4,128)}), f32[64,4,2048]{2,1,0:T(4,128)S(1)}, u32[]{:S(2)}, u32[]{:S(2)}) async-start(f32[64,4,2048]{2,1,0:T(4,128)} %reshape.84), calls=%async_computation.1 | async-start | bytes 4194304 | tf_op jit(solution)/shard_map/all_to_all | solution.py:92
  143.5 1.9 collective-permute-start.2
  145.6 11.5 %all-gather.1 = bf16[256,64]{1,0:T(8,128)(2,1)S(1)} all-gather(bf16[32,64]{1,0:T(8,128)(2,1)S(1)} %fusion.19), channel_id=3, replica_groups=mesh['wide'=64,'narrow'=8] {'narrow'}, dimensions={0}, use_global_device_ids=true | all-gather | bytes 36864 | tf_op jit(solution)/shard_map/all_gather | solution.py:84
  157.4 3.2 %while.21 = (s32[]{:T(128)}, f32[4,32,128]{2,1,0:T(8,128)S(1)}, f32[7,1024]{1,0:T(8,128)S(1)}, f32[4,3,128]{2,1,0:T(4,128)S(1)}, bf16[4,1024]{1,0:T(4,128)(2,1)S(1)}, /*index=5*/bf16[32,1024]{1,0:T(8,128)(2,1)S(1)}, s32[]{:T(128)}) while((s32[]{:T(128)}, f32[4,32,128]{2,1,0:T(8,128)S(1)}, f32[7,1024]{1,0:T(8,128)S(1)}, ...), condition=%wide.region_9.11_spmd, body=%wide.region_6.10_spmd.sunk | while | flops 11010050 | bytes 2275929 | solution.py:45
  160.7 82.6 %all-to-all-done.1 = f32[64,4,2048]{2,1,0:T(4,128)S(1)} async-done(((f32[64,4,2048]{2,1,0:T(4,128)}), f32[64,4,2048]{2,1,0:T(4,128)S(1)}, u32[]{:S(2)}, u32[]{:S(2)}) %all-to-all-start.1) | async-done | bytes 2097184 | tf_op jit(solution)/shard_map/all_to_all | solution.py:92
  244.2 0.6 fusion.32
  (91 shorter events, 7.4 us)
Async XLA Ops:
  0.6 3.1 %copy-start = (bf16[64,64,64]{2,1,0:T(8,128)(2,1)S(1)}, bf16[64,64,64]{2,1,0:T(8,128)(2,1)}, u32[]{:S(2)}) copy-start(bf16[64,64,64]{2,1,0:T(8,128)(2,1)} %param.26) | copy-start | bytes 1572868
  3.7 1.6 copy-start.8
  3.8 1.6 copy-start.9
  9.5 18.9 %copy-start.3 = (bf16[32,512]{1,0:T(8,128)(2,1)S(1)}, bf16[32,512]{1,0:T(8,128)(2,1)}, u32[]{:S(2)}) copy-start(bf16[32,512]{1,0:T(8,128)(2,1)} %param.17) | copy-start | bytes 98308
  9.5 20.8 %copy-start.6 = (f32[7,512]{1,0:T(8,128)S(1)}, f32[7,512]{1,0:T(8,128)}, u32[]{:S(2)}) copy-start(f32[7,512]{1,0:T(8,128)} %param.18) | copy-start | bytes 43012
  9.5 23.3 %copy-start.5 = (bf16[1,512,64]{1,2,0:T(8,128)(2,1)S(1)}, bf16[1,512,64]{1,2,0:T(8,128)(2,1)}, u32[]{:S(2)}) copy-start(bf16[1,512,64]{1,2,0:T(8,128)(2,1)} %param.22) | copy-start | bytes 196612
  9.5 23.4 %copy-start.7 = (s32[4,8]{1,0:T(4,128)S(1)}, s32[4,8]{1,0:T(4,128)}, u32[]{:S(2)}) copy-start(s32[4,8]{1,0:T(4,128)} %param.19) | copy-start | bytes 388
  9.5 23.4 %copy-start.1 = (bf16[4,64,64]{2,1,0:T(8,128)(2,1)S(1)}, bf16[4,64,64]{2,1,0:T(8,128)(2,1)}, u32[]{:S(2)}) copy-start(bf16[4,64,64]{2,1,0:T(8,128)(2,1)} %param.21) | copy-start | bytes 98308
  9.5 119.1 %all-to-all-start = ((f32[64,4,2048]{2,1,0:T(4,128)}), f32[64,4,2048]{2,1,0:T(4,128)S(1)}, u32[]{:S(2)}, u32[]{:S(2)}) async-start(f32[64,4,2048]{2,1,0:T(4,128)} %reshape.77), calls=%async_computation | async-start | bytes 4194304 | tf_op jit(solution)/shard_map/all_to_all | solution.py:92
  28.4 16.6 %collective-permute-start.1 = (bf16[32,512]{1,0:T(8,128)(2,1)S(1)}, bf16[32,512]{1,0:T(8,128)(2,1)}, u32[]{:S(2)}, u32[]{:S(2)}) collective-permute-start(bf16[32,512]{1,0:T(8,128)(2,1)S(1)} %copy-done.3), channel_id=1, source_target_pairs={{0,1},{1,0},{2,3},{3,2},{4,5},{5,4},{6,7},{7,6},{8,9},{9,8},{10,11... | collective-permute-start | bytes 98312 | tf_op jit(solution)/shard_map/ppermute | solution.py:23
  30.3 14.6 %collective-permute-start = (f32[7,512]{1,0:T(8,128)S(1)}, f32[7,512]{1,0:T(8,128)S(1)}, u32[]{:S(2)}, u32[]{:S(2)}) collective-permute-start(f32[7,512]{1,0:T(8,128)S(1)} %copy-done.6), channel_id=1, source_target_pairs={{0,1},{1,0},{2,3},{3,2},{4,5},{5,4},{6,7},{7,6},{8,9},{9,8},{10,11... | collective-permute-start | bytes 43016 | tf_op jit(solution)/shard_map/ppermute | solution.py:23
  130.3 113.8 %copy-start.2 = (bf16[32,512]{1,0:T(8,128)(2,1)}, bf16[32,512]{1,0:T(8,128)(2,1)S(1)}, u32[]{:S(2)}) copy-start(bf16[32,512]{1,0:T(8,128)(2,1)S(1)} %fusion.33) | copy-start | bytes 98308
  137.7 105.6 %all-to-all-start.1 = ((f32[64,4,2048]{2,1,0:T(4,128)}), f32[64,4,2048]{2,1,0:T(4,128)S(1)}, u32[]{:S(2)}, u32[]{:S(2)}) async-start(f32[64,4,2048]{2,1,0:T(4,128)} %reshape.84), calls=%async_computation.1 | async-start | bytes 4194304 | tf_op jit(solution)/shard_map/all_to_all | solution.py:92
  143.5 13.8 %collective-permute-start.2 = (bf16[32,512]{1,0:T(8,128)(2,1)S(1)}, bf16[32,512]{1,0:T(8,128)(2,1)S(1)}, u32[]{:S(2)}, u32[]{:S(2)}) collective-permute-start(bf16[32,512]{1,0:T(8,128)(2,1)S(1)} %fusion.33), channel_id=1, source_target_pairs={{0,1},{1,0},{2,3},{3,2},{4,5},{5,4},{6,7},{7,6},{8,9},{9,8},{10,11... | collective-permute-start | bytes 98312 | tf_op jit(solution)/shard_map/ppermute | solution.py:23
  160.7 83.4 %copy-start.4 = (bf16[64,512]{1,0:T(8,128)(2,1)S(1)}, bf16[64,512]{1,0:T(8,128)(2,1)}, u32[]{:S(2)}) copy-start(bf16[64,512]{1,0:T(8,128)(2,1)} %param.27) | copy-start | bytes 196612
where the time goes:
time: 246 us; the launch traced here: 245 us
  waiting for transfers between devices  158 us (64%)
  starting transfers between devices  31 us (13%)
  blocking collectives  23.1 us (9%)
  other arithmetic  11.7 us (5%)
  matrix products  11.7 us (5%)
  local copies, waits for them, and re-layouts  7.87 us (3%)
    all_to_all x2, waiting for transfers between devices, apply_operator(): lax.all_to_all(outgoing.reshape(wide_count, leaf_count, row_width), 'wide...  158 us
    all_to_all x2, starting transfers between devices, apply_operator(): lax.all_to_all(outgoing.reshape(wide_count, leaf_count, row_width), 'wide...  24.7 us
    all_gather x2, blocking collectives, apply_operator(): lax.all_gather(cluster[None], 'narrow', axis=0, tiled=True)  23.1 us
    dot_general x8, matrix products, leaf_near(): lax.dot_general(source_density, kernel, (((1,), (1,)), ((), ())), preferr...  6.4 us
    ppermute x3, starting transfers between devices, partner(): return lax.ppermute(block, axis, route)  6.25 us
  transfers between devices with their start and end apart: 5, of which 2 were waited for; matrix products, arithmetic and copies ran while one was open for 5% of the time, Pallas kernels for 0%

commit v1 on v0

v1 whole, which is shorter than its diff:
```python
import math

import jax
import jax.numpy as jnp
import numpy as np
from jax import lax
from jax.experimental import pallas as pl
from jax.experimental.pallas import tpu as pltpu
from jax.sharding import Mesh, PartitionSpec as P

LEAF_SIZE = 128
RANK = 64
RIGHT_SIDES = 32
LEAVES = 4
OUTS = 64
SMOOTHING = 0.0625
NZ, NY, NX, NC = 16, 4, 4, 2
NARROW = NX * NC
SLOTS = 2 * NZ
ROWS = 16
CHUNK = SLOTS * ROWS + SLOTS
EMPTY = 4
F32, BF16 = jnp.float32, jnp.bfloat16
NT = (((1,), (1,)), ((), ()))


def call(body, name, out_shape, in_spaces, scratch=()):
    return pl.pallas_call(
        body,
        out_shape=out_shape,
        in_specs=[pl.BlockSpec(memory_space=space) for space in in_spaces],
        out_specs=[pl.BlockSpec(memory_space=pltpu.VMEM)] * len(out_shape),
        scratch_shapes=list(scratch),
        compiler_params=pltpu.CompilerParams(vmem_limit_bytes=32 * 1024 * 1024),
        name=name,
    )


VM, SM = pltpu.VMEM, pltpu.SMEM


def dot(a, b, dims=None):
    if dims is None:
        return jnp.dot(a, b, preferred_element_type=F32)
    return lax.dot_general(a, b, dims, preferred_element_type=F32)


def pack(block):
    return jnp.concatenate([block[:ROWS], block[ROWS:]], axis=1)


def leaf_cols(leaf):
    return slice(leaf * LEAF_SIZE, (leaf + 1) * LEAF_SIZE)


def outgoing(value_ref, code_ref, basis_ref, transfer_ref, coupling_ref, send_ref, cluster_ref, coeff_ref, count_ref):
    cluster = jnp.zeros((RIGHT_SIDES, RANK), F32)
    for leaf in range(LEAVES):
        coeff = dot(value_ref[:, leaf_cols(leaf)], basis_ref[:, leaf_cols(leaf)], NT).astype(BF16)
        coeff_ref[leaf * RIGHT_SIDES : (leaf + 1) * RIGHT_SIDES, :] = coeff
        cluster += dot(coeff, transfer_ref[leaf])
    wide_cluster = jnp.concatenate([cluster, jnp.zeros_like(cluster)], axis=1).astype(BF16)
    for peer in range(NARROW):
        cluster_ref[peer] = wide_cluster
    for peer in range(NY):
        send_ref[peer] = jnp.concatenate(
            [jnp.zeros((SLOTS * ROWS, 128), BF16), jnp.full((SLOTS, 128), EMPTY, BF16)], axis=0
        )
    for wide in range(NZ * NY):
        count_ref[wide] = 0
    rows = lax.broadcasted_iota(jnp.int32, (SLOTS, 128), 0)
    for block in range(OUTS):
        code = code_ref[block]
        wide = code // 16
        target = (code // 4) % 4
        source = code % 4
        turn = count_ref[wide]
        count_ref[wide] = turn + 1
        peer = wide % NY
        slot = (wide // NY) * 2 + turn
        coeff = coeff_ref[pl.ds(pl.multiple_of(source * RIGHT_SIDES, RIGHT_SIDES), RIGHT_SIDES), :]
        product = dot(coeff, coupling_ref[block])
        send_ref[peer, pl.ds(pl.multiple_of(slot * ROWS, ROWS), ROWS), :] = pack(product).astype(BF16)
        ids = send_ref[peer, SLOTS * ROWS :, :]
        send_ref[peer, SLOTS * ROWS :, :] = jnp.where(rows == slot, target.astype(F32), ids.astype(F32)).astype(BF16)


def first_body(value_ref, code_ref, basis_ref, transfer_ref, coupling_ref, send_ref, cluster_ref, coeff_ref, count_ref):
    outgoing(value_ref, code_ref, basis_ref, transfer_ref, coupling_ref, send_ref, cluster_ref, coeff_ref, count_ref)


def merge_body(recv_ref, out_ref):
    ids = [recv_ref[src, SLOTS * ROWS :, :].astype(F32) for src in range(NY)]
    for z in range(NZ):
        total = [jnp.zeros((ROWS, 128), F32) for _ in range(LEAVES)]
        for src in range(NY):
            for turn in range(2):
                slot = z * 2 + turn
                block = recv_ref[src, slot * ROWS : (slot + 1) * ROWS, :].astype(F32)
                row = jnp.broadcast_to(ids[src][slot : slot + 1, :], (ROWS, 128))
                for leaf in range(LEAVES):
                    total[leaf] += jnp.where(row == leaf, block, 0.0)
        for leaf in range(LEAVES):
            out_ref[z, leaf * ROWS : (leaf + 1) * ROWS, :] = total[leaf].astype(BF16)


def kernel_body(own_ref, other_ref, mask_ref, kernel_ref):
    columns = jnp.transpose(
        jnp.concatenate([own_ref[0:3, :], jnp.zeros((5, LEAVES * LEAF_SIZE), F32)], axis=0)
    )
    for leaf in range(LEAVES):
        place = [columns[leaf_cols(leaf), axis : axis + 1] for axis in range(3)]
        for side, ref in enumerate((own_ref, other_ref)):
            for near in range(max(leaf - 1, 0), min(leaf + 2, LEAVES)):
                source = [ref[row : row + 1, leaf_cols(near)] for row in range(7)]
                offset = [place[axis] - source[axis] for axis in range(3)]
                squared = offset[0] * offset[0] + offset[1] * offset[1] + offset[2] * offset[2] + SMOOTHING
                along = offset[0] * source[3] + offset[1] * source[4] + offset[2] * source[5]
                inverse = lax.rsqrt(squared)
                kernel = (source[6] * (1.0 / (4.0 * math.pi))) * along * (inverse * inverse * inverse)
                keep = mask_ref[leaf, side * LEAVES + near] != 0
                first = side * LEAVES * LEAF_SIZE
                kernel_ref[leaf_cols(leaf), first + near * LEAF_SIZE : first + (near + 1) * LEAF_SIZE] = jnp.where(
                    keep, kernel, 0.0
                ).astype(BF16)


def near_body(value_ref, other_ref, kernel_ref, group_ref, rows_ref, transfer_ref, base_ref, spread_ref):
    for leaf in range(LEAVES):
        low, high = max(leaf - 1, 0) * LEAF_SIZE, min(leaf + 2, LEAVES) * LEAF_SIZE
        width = LEAVES * LEAF_SIZE
        near = dot(value_ref[:, low:high], kernel_ref[leaf_cols(leaf), low:high], NT)
        near += dot(other_ref[:, low:high], kernel_ref[leaf_cols(leaf), width + low : width + high], NT)
        base_ref[:, leaf_cols(leaf)] = near + 0.5 * value_ref[:, leaf_cols(leaf)].astype(F32)
    down = jnp.zeros((RIGHT_SIDES, RANK), F32)
    for peer in range(NARROW):
        down += dot(group_ref[peer, :, :RANK], rows_ref[0, peer * RANK : (peer + 1) * RANK, :])
    high = down.astype(BF16)
    low = (down - high.astype(F32)).astype(BF16)
    for leaf in range(LEAVES):
        spread = dot(high, transfer_ref[leaf], NT) + dot(low, transfer_ref[leaf], NT)
        spread_ref[leaf * ROWS : (leaf + 1) * ROWS, :] = pack(spread)


def finish(recv_ref, spread_ref, base_ref, target_ref, out_ref):
    field = spread_ref[...]
    for src in range(NZ):
        field += recv_ref[src].astype(F32)
    field = field.astype(BF16)
    lower = lax.broadcasted_iota(jnp.int32, (ROWS, 128), 1) < RANK
    for leaf in range(LEAVES):
        block = field[leaf * ROWS : (leaf + 1) * ROWS, :].astype(F32)
        tall = jnp.concatenate([jnp.where(lower, block, 0.0), jnp.where(lower, 0.0, block)], axis=0).astype(BF16)
        basis = target_ref[:, leaf_cols(leaf)]
        far = dot(tall, jnp.concatenate([basis, basis], axis=0))
        out_ref[:, leaf_cols(leaf)] = (base_ref[:, leaf_cols(leaf)] + far).astype(BF16)


def middle_body(
    recv_ref, spread_ref, base_ref, target_ref, code_ref, basis_ref, transfer_ref, coupling_ref,
    out_ref, send_ref, cluster_ref, coeff_ref, count_ref,
):
    finish(recv_ref, spread_ref, base_ref, target_ref, out_ref)
    outgoing(out_ref, code_ref, basis_ref, transfer_ref, coupling_ref, send_ref, cluster_ref, coeff_ref, count_ref)


def last_body(recv_ref, spread_ref, base_ref, target_ref, out_ref):
    finish(recv_ref, spread_ref, base_ref, target_ref, out_ref)


def shape(*dims, dtype=BF16):
    return jax.ShapeDtypeStruct(dims, dtype)


def shards(
    density, panels, near_mask, source_basis, leaf_transfer, cluster_coupling,
    out_leaf, out_wide, out_target, coupling, target_basis,
):
    panels_here = LEAVES * LEAF_SIZE
    swap = [(0, 1), (1, 0)]
    code = out_wide[:, 0] * 16 + out_target * 4 + out_leaf
    work = [pltpu.VMEM((LEAVES * RIGHT_SIDES, RANK), BF16), pltpu.SMEM((NZ * NY,), jnp.int32)]
    sends = [shape(NY, CHUNK, 128), shape(NARROW, RIGHT_SIDES, 128)]
    values = shape(RIGHT_SIDES, panels_here)

    def exchange(block, axis):
        return lax.all_to_all(block, axis, 0, 0, tiled=True)

    merge = call(merge_body, "merge", [shape(NZ, LEAVES * ROWS, 128)], [VM])
    nearby = call(
        near_body, "nearby",
        [shape(RIGHT_SIDES, panels_here, dtype=F32), shape(LEAVES * ROWS, 128, dtype=F32)], [VM] * 6,
    )

    other_panels = lax.ppermute(panels, "c", swap)
    other = lax.ppermute(density, "c", swap)
    send, cluster = call(first_body, "first", sends, [VM, SM, VM, VM, VM], work)(
        density, code, source_basis, leaf_transfer, coupling
    )
    arrived = exchange(send, "y")
    group = exchange(cluster, ("x", "c"))
    merged = merge(arrived)[0]
    received = exchange(merged, "z")
    kernel = call(kernel_body, "kernel", [shape(panels_here, 2 * panels_here)], [VM, VM, SM])(
        panels, other_panels, near_mask
    )[0]
    base, spread = nearby(density, other, kernel, group, cluster_coupling, leaf_transfer)
    first_pass, send, cluster = call(
        middle_body, "middle", [values] + sends, [VM, VM, VM, VM, SM, VM, VM, VM], work
    )(received, spread, base, target_basis, code, source_basis, leaf_transfer, coupling)

    arrived = exchange(send, "y")
    group = exchange(cluster, ("x", "c"))
    other = lax.ppermute(first_pass, "c", swap)
    merged = merge(arrived)[0]
    received = exchange(merged, "z")
    base, spread = nearby(first_pass, other, kernel, group, cluster_coupling, leaf_transfer)
    second_pass = call(last_body, "last", [values], [VM] * 4)(received, spread, base, target_basis)[0]
    return (first_pass, second_pass)


def solution(mesh):
    grid = Mesh(np.asarray(mesh.devices).reshape(NZ, NY, NX, NC), ("z", "y", "x", "c"))
    every = ("z", "y", "x", "c")
    cols, rows = P(None, every), P(every)
    in_specs = (cols, cols, rows, cols, rows, rows, rows, rows, rows, rows, cols)
    return jax.shard_map(shards, mesh=grid, in_specs=in_specs, out_specs=(cols, cols), check_vma=False)
```

time: 246 us -> 115 us (0.47)
  the two profiles are of different devices: /device:TPU:4 before, /device:TPU:64 now
where the time goes in v1:
time: 115 us; the launch traced here: 114 us
  waiting for transfers between devices  36.2 us (31%)
  starting transfers between devices  36.1 us (31%)
  blocking collectives  24.7 us (21%)
  Pallas kernels  11.6 us (10%)
  local copies, waits for them, and re-layouts  3.82 us (3%)
    all_to_all x4, waiting for transfers between devices, exchange(): return lax.all_to_all(block, axis, 0, 0, tiled=True)  34.3 us
    all_to_all x4, starting transfers between devices, exchange(): return lax.all_to_all(block, axis, 0, 0, tiled=True)  29.9 us
    all_to_all x2, blocking collectives, exchange(): return lax.all_to_all(block, axis, 0, 0, tiled=True)  24.7 us
    unnamed x27, local copies, waits for them, and re-layouts  3.82 us
    pallas_call x1, Pallas kernels, shards(): call(middle_body, 'middle', [values] + sends, [VM, VM, VM, VM, SM, VM, VM...  2.93 us
    pallas_call x1, Pallas kernels, shards(): call(first_body, 'first', sends, [VM, SM, VM, VM, VM], work)  2.76 us
    ppermute x1, starting transfers between devices, shards(): other_panels = lax.ppermute(panels, 'c', swap)  2.41 us
  transfers between devices with their start and end apart: 7, of which 6 were waited for; matrix products, arithmetic and copies ran while one was open for 0% of the time, Pallas kernels for 5%

profile of v1, /device:TPU:64, one launch (start us, length us, event | category | flops | bytes accessed | tf_op | source)
XLA Modules:
  0.0 113.9 jit_solution(2726666185887156233)
XLA Ops:
  0.6 0.7 fusion.code_ref
  1.3 1.2 %copy-done = bf16[64,64,64]{2,1,0:T(8,128)(2,1)S(1)} copy-done((bf16[64,64,64]{2,1,0:T(8,128)(2,1)S(1)}, bf16[64,64,64]{2,1,0:T(8,128)(2,1)}, u32[]{:S(2)}) %copy-start) | copy-done | bytes 524312
  2.6 0.8 copy-done.2
  3.4 0.8 copy-done.4
  4.2 0.8 copy-done.7
  5.0 2.8 %first.1 = (bf16[4,544,128]{2,1,0:T(8,128)(2,1)S(1)}, bf16[8,32,128]{2,1,0:T(8,128)(2,1)}) custom-call(bf16[32,512]{1,0:T(8,128)(2,1)S(1)} %copy-done.7, s32[64]{0:T(128)S(1)} %fusion.code_ref, bf16[64,512]{1,0:T(8,128)(2,1)S(1)} %copy-done.4, bf16[4,64,64]{2,1,0:T(8,128)(2,1)S(1)} %copy-done.2, bf16[64,64,64]{2,1,0:T(8,128)(2,1)S(1)} %copy-done), custom_call_target="tpu_custom_call" | custom-call | tf_op jit(solution)/shard_map/first/pallas_call | solution.py:197
  7.7 14.1 %all_to_all.30.recv_ref = bf16[4,544,128]{2,1,0:T(8,128)(2,1)S(1)} all-to-all(bf16[4,544,128]{2,1,0:T(8,128)(2,1)S(1)} %get-tuple-element.11), channel_id=1, replica_groups=mesh['z'=16,'y'=4,'x'=4,'c'=2] {'y'}, dimensions={0} | all-to-all | bytes 1114112 | tf_op jit(solution)/shard_map/all_to_all | solution.py:187
  21.8 4.3 %all-to-all-start.2 = ((bf16[8,32,128]{2,1,0:T(8,128)(2,1)}), bf16[8,32,128]{2,1,0:T(8,128)(2,1)S(1)}, u32[]{:S(2)}, u32[]{:S(2)}) async-start(bf16[8,32,128]{2,1,0:T(8,128)(2,1)} %get-tuple-element.12), calls=%async_computation.2 | async-start | bytes 131072 | tf_op jit(solution)/shard_map/all_to_all | solution.py:187
  26.1 1.1 merge.2
  27.2 4.5 %all-to-all-done.2.group_ref = bf16[8,32,128]{2,1,0:T(8,128)(2,1)S(1)} async-done(((bf16[8,32,128]{2,1,0:T(8,128)(2,1)}), bf16[8,32,128]{2,1,0:T(8,128)(2,1)S(1)}, u32[]{:S(2)}, u32[]{:S(2)}) %all-to-all-start.2) | async-done | bytes 65568 | tf_op jit(solution)/shard_map/all_to_all | solution.py:187
  31.7 14.8 %all-to-all-start.1 = ((bf16[16,64,128]{2,1,0:T(8,128)(2,1)}), bf16[16,64,128]{2,1,0:T(8,128)(2,1)S(1)}, u32[]{:S(2)}, u32[]{:S(2)}) async-start(bf16[16,64,128]{2,1,0:T(8,128)(2,1)} %merge.2), calls=%async_computation.1 | async-start | bytes 524288 | tf_op jit(solution)/shard_map/all_to_all | solution.py:187
  46.5 1.9 %collective-permute-start = (bf16[32,512]{1,0:T(8,128)(2,1)S(1)}, bf16[32,512]{1,0:T(8,128)(2,1)S(1)}, u32[]{:S(2)}, u32[]{:S(2)}) collective-permute-start(bf16[32,512]{1,0:T(8,128)(2,1)S(1)} %copy-done.8), channel_id=1, source_target_pairs={{0,1},{1,0},{2,3},{3,2},{4,5},{5,4},{6,7},{7,6},{8,9},{9,8},{10,11... | collective-permute-start | bytes 98312 | tf_op jit(solution)/shard_map/ppermute | solution.py:196
  48.5 2.4 %collective-permute-start.1 = (f32[7,512]{1,0:T(8,128)S(1)}, f32[7,512]{1,0:T(8,128)S(1)}, u32[]{:S(2)}, u32[]{:S(2)}) collective-permute-start(f32[7,512]{1,0:T(8,128)S(1)} %copy-done.10), channel_id=1, source_target_pairs={{0,1},{1,0},{2,3},{3,2},{4,5},{5,4},{6,7},{7,6},{8,9},{9,8},{10,11... | collective-permute-start | bytes 43016 | tf_op jit(solution)/shard_map/ppermute | solution.py:195
  50.9 0.1 copy.13.rows_ref
  51.0 0.0 copy-start.1
  51.0 0.7 collective-permute-done.1.other_ref
  51.7 1.7 %kernel.1.kernel_ref = bf16[512,1024]{1,0:T(8,128)(2,1)S(1)} custom-call(f32[7,512]{1,0:T(8,128)S(1)} %copy-done.10, f32[7,512]{1,0:T(8,128)S(1)} %collective-permute-done.1.other_ref, s32[4,8]{1,0:T(4,128)S(1)} %copy-done.11), custom_call_target="tpu_custom_call" | custom-call | tf_op jit(solution)/shard_map/kernel/pallas_call | solution.py:204
  53.4 0.0 copy-start.5
  53.4 0.0 copy-start.6
  53.5 0.6 nearby.2
  54.1 10.7 %all-to-all-done.1.recv_ref = bf16[16,64,128]{2,1,0:T(8,128)(2,1)S(1)} async-done(((bf16[16,64,128]{2,1,0:T(8,128)(2,1)}), bf16[16,64,128]{2,1,0:T(8,128)(2,1)S(1)}, u32[]{:S(2)}, u32[]{:S(2)}) %all-to-all-start.1) | async-done | bytes 262176 | tf_op jit(solution)/shard_map/all_to_all | solution.py:187
  64.9 2.9 %middle.1 = (bf16[32,512]{1,0:T(8,128)(2,1)}, bf16[4,544,128]{2,1,0:T(8,128)(2,1)S(1)}, bf16[8,32,128]{2,1,0:T(8,128)(2,1)}) custom-call(bf16[16,64,128]{2,1,0:T(8,128)(2,1)S(1)} %all-to-all-done.1.recv_ref, f32[64,128]{1,0:T(8,128)S(1)} %get-tuple-element.13.spread_ref, f32[32,512]{1,0:T(8,128)S(1)} %get-tuple-element.14.base_ref, ...), custom_call_target="tpu_custom_call" | custom-call | tf_op jit(solution)/shard_map/middle/pallas_call | solution.py:208
  67.8 10.6 %all_to_all.31.recv_ref = bf16[4,544,128]{2,1,0:T(8,128)(2,1)S(1)} all-to-all(bf16[4,544,128]{2,1,0:T(8,128)(2,1)S(1)} %get-tuple-element.16), channel_id=1, replica_groups=mesh['z'=16,'y'=4,'x'=4,'c'=2] {'y'}, dimensions={0} | all-to-all | bytes 1114112 | tf_op jit(solution)/shard_map/all_to_all | solution.py:187
  78.4 3.3 %all-to-all-start.5 = ((bf16[8,32,128]{2,1,0:T(8,128)(2,1)}), bf16[8,32,128]{2,1,0:T(8,128)(2,1)S(1)}, u32[]{:S(2)}, u32[]{:S(2)}) async-start(bf16[8,32,128]{2,1,0:T(8,128)(2,1)} %get-tuple-element.17), calls=%async_computation.5 | async-start | bytes 131072 | tf_op jit(solution)/shard_map/all_to_all | solution.py:187
  81.8 1.1 merge.3
  82.9 4.5 %all-to-all-done.5.group_ref = bf16[8,32,128]{2,1,0:T(8,128)(2,1)S(1)} async-done(((bf16[8,32,128]{2,1,0:T(8,128)(2,1)}), bf16[8,32,128]{2,1,0:T(8,128)(2,1)S(1)}, u32[]{:S(2)}, u32[]{:S(2)}) %all-to-all-start.5) | async-done | bytes 65568 | tf_op jit(solution)/shard_map/all_to_all | solution.py:187
  87.3 7.5 %all-to-all-start.4 = ((bf16[16,64,128]{2,1,0:T(8,128)(2,1)}), bf16[16,64,128]{2,1,0:T(8,128)(2,1)S(1)}, u32[]{:S(2)}, u32[]{:S(2)}) async-start(bf16[16,64,128]{2,1,0:T(8,128)(2,1)} %merge.3), calls=%async_computation.4 | async-start | bytes 524288 | tf_op jit(solution)/shard_map/all_to_all | solution.py:187
  94.8 1.9 %collective-permute-start.2 = (bf16[32,512]{1,0:T(8,128)(2,1)S(1)}, bf16[32,512]{1,0:T(8,128)(2,1)S(1)}, u32[]{:S(2)}, u32[]{:S(2)}) collective-permute-start(bf16[32,512]{1,0:T(8,128)(2,1)S(1)} %copy-done.9), channel_id=1, source_target_pairs={{0,1},{1,0},{2,3},{3,2},{4,5},{5,4},{6,7},{7,6},{8,9},{9,8},{10,11... | collective-permute-start | bytes 98312 | tf_op jit(solution)/shard_map/ppermute | solution.py:214
  96.7 1.2 %collective-permute-done.2.other_ref = bf16[32,512]{1,0:T(8,128)(2,1)S(1)} collective-permute-done((bf16[32,512]{1,0:T(8,128)(2,1)S(1)}, bf16[32,512]{1,0:T(8,128)(2,1)S(1)}, u32[]{:S(2)}, u32[]{:S(2)}) %collective-permute-start.2) | collective-permute-done | bytes 32800 | tf_op jit(solution)/shard_map/ppermute | solution.py:214
  97.9 0.6 nearby.3
  98.6 14.6 %all-to-all-done.4.recv_ref = bf16[16,64,128]{2,1,0:T(8,128)(2,1)S(1)} async-done(((bf16[16,64,128]{2,1,0:T(8,128)(2,1)}), bf16[16,64,128]{2,1,0:T(8,128)(2,1)S(1)}, u32[]{:S(2)}, u32[]{:S(2)}) %all-to-all-start.4) | async-done | bytes 262176 | tf_op jit(solution)/shard_map/all_to_all | solution.py:187
  113.2 0.8 last.1
  (20 shorter events, 0.0 us)
Async XLA Ops:
  1.3 1.2 %copy-start = (bf16[64,64,64]{2,1,0:T(8,128)(2,1)S(1)}, bf16[64,64,64]{2,1,0:T(8,128)(2,1)}, u32[]{:S(2)}) copy-start(bf16[64,64,64]{2,1,0:T(8,128)(2,1)} %coupling_ref.3) | copy-start | bytes 1572868
  2.5 0.8 copy-start.2
  3.4 0.8 copy-start.4
  4.2 0.8 copy-start.7
  21.8 9.9 %all-to-all-start.2 = ((bf16[8,32,128]{2,1,0:T(8,128)(2,1)}), bf16[8,32,128]{2,1,0:T(8,128)(2,1)S(1)}, u32[]{:S(2)}, u32[]{:S(2)}) async-start(bf16[8,32,128]{2,1,0:T(8,128)(2,1)} %get-tuple-element.12), calls=%async_computation.2 | async-start | bytes 131072 | tf_op jit(solution)/shard_map/all_to_all | solution.py:187
  27.2 19.3 %copy-start.8 = (bf16[32,512]{1,0:T(8,128)(2,1)S(1)}, bf16[32,512]{1,0:T(8,128)(2,1)}, u32[]{:S(2)}) copy-start(bf16[32,512]{1,0:T(8,128)(2,1)} %value_ref.3) | copy-start | bytes 98308
  27.2 21.2 %copy-start.10 = (f32[7,512]{1,0:T(8,128)S(1)}, f32[7,512]{1,0:T(8,128)}, u32[]{:S(2)}) copy-start(f32[7,512]{1,0:T(8,128)} %own_ref.1) | copy-start | bytes 43012
  27.2 23.7 %copy-start.12 = (bf16[1,512,64]{1,2,0:T(8,128)(2,1)S(1)}, bf16[1,512,64]{1,2,0:T(8,128)(2,1)}, u32[]{:S(2)}) copy-start(bf16[1,512,64]{1,2,0:T(8,128)(2,1)} %param.16) | copy-start | bytes 196612
  31.7 33.1 %all-to-all-start.1 = ((bf16[16,64,128]{2,1,0:T(8,128)(2,1)}), bf16[16,64,128]{2,1,0:T(8,128)(2,1)S(1)}, u32[]{:S(2)}, u32[]{:S(2)}) async-start(bf16[16,64,128]{2,1,0:T(8,128)(2,1)} %merge.2), calls=%async_computation.1 | async-start | bytes 524288 | tf_op jit(solution)/shard_map/all_to_all | solution.py:187
  46.5 5.2 %copy-start.11 = (s32[4,8]{1,0:T(4,128)S(1)}, s32[4,8]{1,0:T(4,128)}, u32[]{:S(2)}) copy-start(s32[4,8]{1,0:T(4,128)} %mask_ref.1) | copy-start | bytes 388
  46.5 6.9 %collective-permute-start = (bf16[32,512]{1,0:T(8,128)(2,1)S(1)}, bf16[32,512]{1,0:T(8,128)(2,1)S(1)}, u32[]{:S(2)}, u32[]{:S(2)}) collective-permute-start(bf16[32,512]{1,0:T(8,128)(2,1)S(1)} %copy-done.8), channel_id=1, source_target_pairs={{0,1},{1,0},{2,3},{3,2},{4,5},{5,4},{6,7},{7,6},{8,9},{9,8},{10,11... | collective-permute-start | bytes 98312 | tf_op jit(solution)/shard_map/ppermute | solution.py:196
  48.5 3.2 %collective-permute-start.1 = (f32[7,512]{1,0:T(8,128)S(1)}, f32[7,512]{1,0:T(8,128)S(1)}, u32[]{:S(2)}, u32[]{:S(2)}) collective-permute-start(f32[7,512]{1,0:T(8,128)S(1)} %copy-done.10), channel_id=1, source_target_pairs={{0,1},{1,0},{2,3},{3,2},{4,5},{5,4},{6,7},{7,6},{8,9},{9,8},{10,11... | collective-permute-start | bytes 43016 | tf_op jit(solution)/shard_map/ppermute | solution.py:195
  50.9 2.6 %copy-start.3 = (bf16[4,64,64]{2,1,0:T(8,128)(2,1)S(1)}, bf16[4,64,64]{2,1,0:T(8,128)(2,1)}, u32[]{:S(2)}) copy-start(bf16[4,64,64]{2,1,0:T(8,128)(2,1)} %transfer_ref.7) | copy-start | bytes 98308
  51.0 13.8 %copy-start.1 = (bf16[64,64,64]{2,1,0:T(8,128)(2,1)S(1)}, bf16[64,64,64]{2,1,0:T(8,128)(2,1)}, u32[]{:S(2)}) copy-start(bf16[64,64,64]{2,1,0:T(8,128)(2,1)} %coupling_ref.3) | copy-start | bytes 1572868
  53.4 11.4 %copy-start.5 = (bf16[64,512]{1,0:T(8,128)(2,1)S(1)}, bf16[64,512]{1,0:T(8,128)(2,1)}, u32[]{:S(2)}) copy-start(bf16[64,512]{1,0:T(8,128)(2,1)} %basis_ref.3) | copy-start | bytes 196612
  53.4 11.4 %copy-start.6 = (bf16[64,512]{1,0:T(8,128)(2,1)S(1)}, bf16[64,512]{1,0:T(8,128)(2,1)}, u32[]{:S(2)}) copy-start(bf16[64,512]{1,0:T(8,128)(2,1)} %target_ref.3) | copy-start | bytes 196612
  78.4 8.9 %all-to-all-start.5 = ((bf16[8,32,128]{2,1,0:T(8,128)(2,1)}), bf16[8,32,128]{2,1,0:T(8,128)(2,1)S(1)}, u32[]{:S(2)}, u32[]{:S(2)}) async-start(bf16[8,32,128]{2,1,0:T(8,128)(2,1)} %get-tuple-element.17), calls=%async_computation.5 | async-start | bytes 131072 | tf_op jit(solution)/shard_map/all_to_all | solution.py:187
  82.9 11.9 %copy-start.9 = (bf16[32,512]{1,0:T(8,128)(2,1)S(1)}, bf16[32,512]{1,0:T(8,128)(2,1)}, u32[]{:S(2)}) copy-start(bf16[32,512]{1,0:T(8,128)(2,1)} %get-tuple-element.9.value_ref) | copy-start | bytes 98308
  87.3 25.8 %all-to-all-start.4 = ((bf16[16,64,128]{2,1,0:T(8,128)(2,1)}), bf16[16,64,128]{2,1,0:T(8,128)(2,1)S(1)}, u32[]{:S(2)}, u32[]{:S(2)}) async-start(bf16[16,64,128]{2,1,0:T(8,128)(2,1)} %merge.3), calls=%async_computation.4 | async-start | bytes 524288 | tf_op jit(solution)/shard_map/all_to_all | solution.py:187
  94.8 3.1 %collective-permute-start.2 = (bf16[32,512]{1,0:T(8,128)(2,1)S(1)}, bf16[32,512]{1,0:T(8,128)(2,1)S(1)}, u32[]{:S(2)}, u32[]{:S(2)}) collective-permute-start(bf16[32,512]{1,0:T(8,128)(2,1)S(1)} %copy-done.9), channel_id=1, source_target_pairs={{0,1},{1,0},{2,3},{3,2},{4,5},{5,4},{6,7},{7,6},{8,9},{9,8},{10,11... | collective-permute-start | bytes 98312 | tf_op jit(solution)/shard_map/ppermute | solution.py:214

commit v2 on v1

v2 whole, which is shorter than its diff:
```python
import math

import jax
import jax.numpy as jnp
import numpy as np
from jax import lax
from jax.experimental import pallas as pl
from jax.experimental.pallas import tpu as pltpu
from jax.sharding import Mesh, PartitionSpec as P

LEAF_SIZE = 128
RANK = 64
RIGHT_SIDES = 32
LEAVES = 4
OUTS = 64
SMOOTHING = 0.0625
NA, NB, NY, NX, NC = 8, 2, 4, 4, 2
PEERS = NB * NY
SLOTS = 2 * NA
ROWS = 16
CHUNK = SLOTS * ROWS + SLOTS
EMPTY = 4
F32, BF16 = jnp.float32, jnp.bfloat16
NT = (((1,), (1,)), ((), ()))


def call(body, name, out_shape, in_spaces, scratch=(), out_spaces=None):
    return pl.pallas_call(
        body,
        out_shape=out_shape,
        in_specs=[pl.BlockSpec(memory_space=space) for space in in_spaces],
        out_specs=[pl.BlockSpec(memory_space=space) for space in out_spaces or [pltpu.VMEM] * len(out_shape)],
        scratch_shapes=list(scratch),
        compiler_params=pltpu.CompilerParams(vmem_limit_bytes=32 * 1024 * 1024),
        name=name,
    )


VM, SM = pltpu.VMEM, pltpu.SMEM


def dot(a, b, dims=None):
    if dims is None:
        return jnp.dot(a, b, preferred_element_type=F32)
    return lax.dot_general(a, b, dims, preferred_element_type=F32)


def pack(block):
    return jnp.concatenate([block[:ROWS], block[ROWS:]], axis=1)


def leaf_cols(leaf):
    return slice(leaf * LEAF_SIZE, (leaf + 1) * LEAF_SIZE)


def leaf_coeffs(value_ref, basis_ref, transfer_ref, swap_ref, coeff_ref):
    cluster = jnp.zeros((RIGHT_SIDES, RANK), F32)
    for leaf in range(LEAVES):
        coeff = dot(value_ref[:, leaf_cols(leaf)], basis_ref[:, leaf_cols(leaf)], NT).astype(BF16)
        coeff_ref[leaf * RIGHT_SIDES : (leaf + 1) * RIGHT_SIDES, :] = coeff
        cluster += dot(coeff, transfer_ref[leaf])
    swap_ref[:, : LEAVES * LEAF_SIZE] = value_ref[...]
    swap_ref[:, LEAVES * LEAF_SIZE :] = jnp.concatenate([cluster, jnp.zeros_like(cluster)], axis=1).astype(BF16)


def product(block, place_ref, coupling_ref, coeff_ref, send_ref):
    place = place_ref[block]
    source = place % 4
    slot = (place // 16) % SLOTS
    peer = place // (16 * SLOTS)
    coeff = coeff_ref[pl.ds(pl.multiple_of(source * RIGHT_SIDES, RIGHT_SIDES), RIGHT_SIDES), :]
    packed = pack(dot(coeff, coupling_ref[block])).astype(BF16)
    send_ref[peer, pl.ds(pl.multiple_of(slot * ROWS, ROWS), ROWS), :] = packed


def clear(send_ref):
    for peer in range(PEERS):
        send_ref[peer, : SLOTS * ROWS, :] = jnp.zeros((SLOTS * ROWS, 128), BF16)


def first_body(
    leaf_ref, wide_ref, target_ref, value_hbm, basis_hbm, transfer_hbm, coupling_hbm,
    send_ref, swap_ref, ids_ref, place_ref,
    value_ref, basis_ref, transfer_ref, coupling_ref, coeff_ref, row_ref, count_ref, sems,
):
    copies = [
        pltpu.make_async_copy(value_hbm, value_ref, sems.at[0]),
        pltpu.make_async_copy(basis_hbm, basis_ref, sems.at[1]),
        pltpu.make_async_copy(transfer_hbm, transfer_ref, sems.at[2]),
    ]
    parts = 4
    each = OUTS // parts
    for part in range(parts):
        span = pl.ds(part * each, each)
        copies.append(pltpu.make_async_copy(coupling_hbm.at[span], coupling_ref.at[span], sems.at[3 + part]))
    for copy in copies:
        copy.start()
    for wide in range(NA * PEERS):
        count_ref[wide] = 0
    row_ref[...] = jnp.full((PEERS * SLOTS, 128), EMPTY, F32)
    clear(send_ref)
    for block in range(OUTS):
        wide = wide_ref[block]
        target = target_ref[block]
        turn = count_ref[wide]
        count_ref[wide] = turn + 1
        spot = (wide % PEERS) * SLOTS + (wide // PEERS) * 2 + turn
        place_ref[block] = spot * 16 + target * 4 + leaf_ref[block]
        row_ref[pl.ds(spot, 1), :] = jnp.full((1, 128), target, jnp.int32).astype(F32)
    for peer in range(PEERS):
        ids = row_ref[peer * SLOTS : (peer + 1) * SLOTS, :].astype(BF16)
        ids_ref[peer] = ids
        send_ref[peer, SLOTS * ROWS :, :] = ids
    for copy in copies[:3]:
        copy.wait()
    leaf_coeffs(value_ref, basis_ref, transfer_ref, swap_ref, coeff_ref)
    for part in range(parts):
        copies[3 + part].wait()
        for block in range(part * each, (part + 1) * each):
            product(block, place_ref, coupling_ref, coeff_ref, send_ref)


def merge_body(recv_ref, out_ref):
    ids = [recv_ref[src, SLOTS * ROWS :, :].astype(F32) for src in range(PEERS)]
    for pair in range(NA):
        total = [jnp.zeros((ROWS, 128), F32) for _ in range(LEAVES)]
        for src in range(PEERS):
            for turn in range(2):
                slot = pair * 2 + turn
                block = recv_ref[src, slot * ROWS : (slot + 1) * ROWS, :].astype(F32)
                row = jnp.broadcast_to(ids[src][slot : slot + 1, :], (ROWS, 128))
                for leaf in range(LEAVES):
                    total[leaf] += jnp.where(row == leaf, block, 0.0)
        for leaf in range(LEAVES):
            out_ref[pair, leaf * ROWS : (leaf + 1) * ROWS, :] = total[leaf].astype(BF16)


def kernel_body(own_ref, other_ref, mask_ref, kernel_ref):
    columns = jnp.transpose(
        jnp.concatenate([own_ref[0:3, :], jnp.zeros((5, LEAVES * LEAF_SIZE), F32)], axis=0)
    )
    for leaf in range(LEAVES):
        place = [columns[leaf_cols(leaf), axis : axis + 1] for axis in range(3)]
        for side, ref in enumerate((own_ref, other_ref)):
            for near in range(max(leaf - 1, 0), min(leaf + 2, LEAVES)):
                source = [ref[row : row + 1, leaf_cols(near)] for row in range(7)]
                offset = [place[axis] - source[axis] for axis in range(3)]
                squared = offset[0] * offset[0] + offset[1] * offset[1] + offset[2] * offset[2] + SMOOTHING
                along = offset[0] * source[3] + offset[1] * source[4] + offset[2] * source[5]
                inverse = lax.rsqrt(squared)
                kernel = (source[6] * (1.0 / (4.0 * math.pi))) * along * (inverse * inverse * inverse)
                keep = mask_ref[leaf, side * LEAVES + near] != 0
                first = side * LEAVES * LEAF_SIZE
                kernel_ref[leaf_cols(leaf), first + near * LEAF_SIZE : first + (near + 1) * LEAF_SIZE] = jnp.where(
                    keep, kernel, 0.0
                ).astype(BF16)


def near_body(value_ref, other_ref, kernel_ref, two_ref, four_ref, eight_ref, rows_ref, transfer_ref, base_ref, spread_ref):
    width = LEAVES * LEAF_SIZE
    for leaf in range(LEAVES):
        low, high = max(leaf - 1, 0) * LEAF_SIZE, min(leaf + 2, LEAVES) * LEAF_SIZE
        near = dot(value_ref[:, low:high], kernel_ref[leaf_cols(leaf), low:high], NT)
        near += dot(other_ref[:, low:high], kernel_ref[leaf_cols(leaf), width + low : width + high], NT)
        base_ref[:, leaf_cols(leaf)] = near + 0.5 * value_ref[:, leaf_cols(leaf)].astype(F32)
    me = lax.axis_index("x") * NC + lax.axis_index("c")
    down = jnp.zeros((RIGHT_SIDES, RANK), F32)
    pairs = [two_ref[...], four_ref[...], eight_ref[:, :128], eight_ref[:, 128:]]
    for step, pair in enumerate(pairs):
        rows = [
            rows_ref[0, pl.ds(pl.multiple_of(jnp.bitwise_xor(me, 2 * step + turn) * RANK, RANK), RANK), :]
            for turn in range(2)
        ]
        down += dot(pair, jnp.concatenate(rows, axis=0))
    high = down.astype(BF16)
    low = (down - high.astype(F32)).astype(BF16)
    for leaf in range(LEAVES):
        spread = dot(high, transfer_ref[leaf], NT) + dot(low, transfer_ref[leaf], NT)
        spread_ref[leaf * ROWS : (leaf + 1) * ROWS, :] = pack(spread)


def finish(recv_ref, spread_ref, base_ref, target_ref, out_ref):
    field = spread_ref[...]
    for src in range(NA):
        field += recv_ref[src].astype(F32)
    field = field.astype(BF16)
    lower = lax.broadcasted_iota(jnp.int32, (ROWS, 128), 1) < RANK
    for leaf in range(LEAVES):
        block = field[leaf * ROWS : (leaf + 1) * ROWS, :].astype(F32)
        tall = jnp.concatenate([jnp.where(lower, block, 0.0), jnp.where(lower, 0.0, block)], axis=0).astype(BF16)
        basis = target_ref[:, leaf_cols(leaf)]
        far = dot(tall, jnp.concatenate([basis, basis], axis=0))
        out_ref[:, leaf_cols(leaf)] = (base_ref[:, leaf_cols(leaf)] + far).astype(BF16)


def middle_body(
    recv_ref, spread_ref, base_ref, target_ref, place_ref, ids_ref, basis_ref, transfer_ref, coupling_ref,
    out_ref, send_ref, swap_ref, coeff_ref,
):
    finish(recv_ref, spread_ref, base_ref, target_ref, out_ref)
    clear(send_ref)
    for peer in range(PEERS):
        send_ref[peer, SLOTS * ROWS :, :] = ids_ref[peer]
    leaf_coeffs(out_ref, basis_ref, transfer_ref, swap_ref, coeff_ref)
    for block in range(OUTS):
        product(block, place_ref, coupling_ref, coeff_ref, send_ref)


def last_body(recv_ref, spread_ref, base_ref, target_ref, out_ref):
    finish(recv_ref, spread_ref, base_ref, target_ref, out_ref)


def shape(*dims, dtype=BF16):
    return jax.ShapeDtypeStruct(dims, dtype)


def shards(
    density, panels, near_mask, source_basis, leaf_transfer, cluster_coupling,
    out_leaf, out_wide, out_target, coupling, target_basis,
):
    panels_here = LEAVES * LEAF_SIZE
    values = shape(RIGHT_SIDES, panels_here)
    sends = [shape(PEERS, CHUNK, 128), shape(RIGHT_SIDES, panels_here + 128)]
    coeff_work = pltpu.VMEM((LEAVES * RIGHT_SIDES, RANK), BF16)

    def swap(block, axis, distance):
        count = lax.axis_size(axis)
        return lax.ppermute(block, axis, [(i, i ^ distance) for i in range(count)])

    first = call(
        first_body, "first", sends + [shape(PEERS, SLOTS, 128), shape(OUTS, dtype=jnp.int32)],
        [SM] * 3 + [pl.ANY] * 4,
        [
            pltpu.VMEM((RIGHT_SIDES, panels_here), BF16),
            pltpu.VMEM((RANK, panels_here), BF16),
            pltpu.VMEM((LEAVES, RANK, RANK), BF16),
            pltpu.VMEM((OUTS, RANK, RANK), BF16),
            coeff_work,
            pltpu.VMEM((PEERS * SLOTS, 128), F32),
            pltpu.SMEM((NA * PEERS,), jnp.int32),
            pltpu.SemaphoreType.DMA((7,)),
        ],
        [VM, VM, VM, SM],
    )
    merge = call(merge_body, "merge", [shape(NA, LEAVES * ROWS, 128)], [VM])
    nearby = call(
        near_body, "nearby",
        [shape(RIGHT_SIDES, panels_here, dtype=F32), shape(LEAVES * ROWS, 128, dtype=F32)], [VM] * 8,
    )

    def couple(send):
        arrived = lax.all_to_all(send, ("b", "y"), 0, 0, tiled=True)
        return lax.all_to_all(merge(arrived)[0], "a", 0, 0, tiled=True)

    def local(value, packet, kernel):
        other = swap(packet, "c", 1)
        two = jnp.concatenate([packet[:, panels_here : panels_here + RANK], other[:, panels_here : panels_here + RANK]], axis=1)
        four = swap(two, "x", 1)
        eight = swap(jnp.concatenate([two, four], axis=1), "x", 2)
        return nearby(value, other, kernel, two, four, eight, cluster_coupling, leaf_transfer)

    send, packet, ids, place = first(
        out_leaf, out_wide.reshape(OUTS), out_target, density, source_basis, leaf_transfer, coupling
    )
    received = couple(send)
    kernel = call(kernel_body, "kernel", [shape(panels_here, 2 * panels_here)], [VM, VM, SM])(
        panels, swap(panels, "c", 1), near_mask
    )[0]
    base, spread = local(density, packet, kernel)
    first_pass, send, packet = call(
        middle_body, "middle", [values] + sends, [VM, VM, VM, VM, SM, VM, VM, VM, VM], [coeff_work]
    )(received, spread, base, target_basis, place, ids, source_basis, leaf_transfer, coupling)

    received = couple(send)
    base, spread = local(first_pass, packet, kernel)
    second_pass = call(last_body, "last", [values], [VM] * 4)(received, spread, base, target_basis)[0]
    return (first_pass, second_pass)


def solution(mesh):
    every = ("a", "b", "y", "x", "c")
    grid = Mesh(np.asarray(mesh.devices).reshape(NA, NB, NY, NX, NC), every)
    cols, rows = P(None, every), P(every)
    in_specs = (cols, cols, rows, cols, rows, rows, rows, rows, rows, rows, cols)
    return jax.shard_map(shards, mesh=grid, in_specs=in_specs, out_specs=(cols, cols), check_vma=False)
```

time: 115 us -> 107 us (0.930)
  waiting for transfers between devices: 36.2 us -> 13.1 us
  starting transfers between devices: 36.1 us -> 45.3 us
  blocking collectives: 24.7 us -> 29.9 us
    all_to_all x4 -> x2, waiting for transfers between devices: 34.3 us -> 0.01 us  [couple(): return lax.all_to_all(merge(arrived)[0], 'a', 0, 0, tiled=True)]
    ppermute x3 -> x7, starting transfers between devices: 6.25 us -> 19.4 us  [swap(): return lax.ppermute(block, axis, [(i, i ^ distance) for i in range(count)])]
    ppermute x3 -> x7, waiting for transfers between devices: 1.83 us -> 13.1 us  [swap(): return lax.ppermute(block, axis, [(i, i ^ distance) for i in range(count)])]
    all_to_all x2, blocking collectives: 24.7 us -> 29.9 us  [couple(): arrived = lax.all_to_all(send, ('b', 'y'), 0, 0, tiled=True)]
    all_to_all x4 -> x2, starting transfers between devices: 29.9 us -> 25.9 us  [couple(): return lax.all_to_all(merge(arrived)[0], 'a', 0, 0, tiled=True)]
    unnamed x27 -> x33, local copies, waits for them, and re-layouts: 3.82 us -> 4.64 us
  transfers between devices with their start and end apart: 7 -> 9, of which waited for: 6 -> 6; matrix products, arithmetic and copies ran while one was open for 0% -> 0% of each run, Pallas kernels for 5% -> 3%
where the time goes in v2:
time: 107 us; the launch traced here: 106 us
  starting transfers between devices  45.3 us (42%)
  blocking collectives  29.9 us (28%)
  waiting for transfers between devices  13.1 us (12%)
  Pallas kernels  12.2 us (11%)
  local copies, waits for them, and re-layouts  4.65 us (4%)
    all_to_all x2, blocking collectives, couple(): arrived = lax.all_to_all(send, ('b', 'y'), 0, 0, tiled=True)  29.9 us
    all_to_all x2, starting transfers between devices, couple(): return lax.all_to_all(merge(arrived)[0], 'a', 0, 0, tiled=True)  25.9 us
    ppermute x7, starting transfers between devices, swap(): return lax.ppermute(block, axis, [(i, i ^ distance) for i in range(count)])  19.4 us
    ppermute x7, waiting for transfers between devices, swap(): return lax.ppermute(block, axis, [(i, i ^ distance) for i in range(count)])  13.1 us
    unnamed x33, local copies, waits for them, and re-layouts  4.64 us
    pallas_call x1, Pallas kernels, shards(): first(out_leaf, out_wide.reshape(OUTS), out_target, density, source_basis...  3.85 us
    pallas_call x1, Pallas kernels, shards(): call(middle_body, 'middle', [values] + sends, [VM, VM, VM, VM, SM, VM, VM...  2.38 us
  transfers between devices with their start and end apart: 9, of which 6 were waited for; matrix products, arithmetic and copies ran while one was open for 0% of the time, Pallas kernels for 3%

profile of v2, /device:TPU:64, one launch (start us, length us, event | category | flops | bytes accessed | tf_op | source)
XLA Modules:
  0.0 106.3 jit_solution(18248258771974175944)
XLA Ops:
  0.7 0.6 copy-done.12
  1.3 1.2 %copy-done = bf16[64,64,64]{2,1,0:T(8,128)(2,1)S(1)} copy-done((bf16[64,64,64]{2,1,0:T(8,128)(2,1)S(1)}, bf16[64,64,64]{2,1,0:T(8,128)(2,1)}, u32[]{:S(2)}) %copy-start) | copy-done | bytes 524312
  2.5 0.8 copy-done.2
  3.4 0.8 copy-done.4
  4.2 0.8 copy-done.7
  5.0 3.9 %first.1 = (bf16[8,272,128]{2,1,0:T(8,128)(2,1)S(1)}, bf16[32,640]{1,0:T(8,128)(2,1)S(1)}, bf16[8,16,128]{2,1,0:T(8,128)(2,1)S(1)}, s32[64]{0:T(128)S(1)}) custom-call(s32[64]{0:T(128)S(1)} %copy-done.12, s32[64]{0:T(128)S(1)} %bitcast.1, s32[64]{0:T(128)S(1)} %copy-done.14, bf16[32,512]{1,0:T(8,128)(2,1)S(1)} %copy-done.7, bf16[64,512]{1,0:T(8,128)(2,1)S(1)} %copy-done.4, ...), custom_call_target="tpu_custom_call" | custom-call | tf_op jit(solution)/shard_map/first/pallas_call | solution.py:262
  8.8 16.3 %all_to_all.20.recv_ref = bf16[8,272,128]{2,1,0:T(8,128)(2,1)S(1)} all-to-all(bf16[8,272,128]{2,1,0:T(8,128)(2,1)S(1)} %get-tuple-element.13), channel_id=1, replica_groups=mesh['a'=8,'b'=2,'y'=4,'x'=4,'c'=2] {'b','y'}, dimensions={0} | all-to-all | bytes 1114112 | tf_op jit(solution)/shard_map/all_to_all | solution.py:252
  25.2 1.0 merge.2
  26.2 13.8 %all-to-all-start.1 = ((bf16[8,64,128]{2,1,0:T(8,128)(2,1)}), bf16[8,64,128]{2,1,0:T(8,128)(2,1)S(1)}, u32[]{:S(2)}, u32[]{:S(2)}) async-start(bf16[8,64,128]{2,1,0:T(8,128)(2,1)} %merge.2), calls=%async_computation.1 | async-start | bytes 262144 | tf_op jit(solution)/shard_map/all_to_all | solution.py:253
  40.0 2.0 %collective-permute-start = (bf16[32,640]{1,0:T(8,128)(2,1)S(1)}, bf16[32,640]{1,0:T(8,128)(2,1)S(1)}, u32[]{:S(2)}, u32[]{:S(2)}) collective-permute-start(bf16[32,640]{1,0:T(8,128)(2,1)S(1)} %get-tuple-element.14), channel_id=1, source_target_pairs={{0,1},{1,0},{2,3},{3,2},{4,5},{5,4},{6,7},{7,6},{8,9},{9,8},{10,11... | collective-permute-start | bytes 122888 | tf_op jit(solution)/shard_map/ppermute | solution.py:228
  42.1 1.2 %collective-permute-done.other_ref = bf16[32,640]{1,0:T(8,128)(2,1)S(1)} collective-permute-done((bf16[32,640]{1,0:T(8,128)(2,1)S(1)}, bf16[32,640]{1,0:T(8,128)(2,1)S(1)}, u32[]{:S(2)}, u32[]{:S(2)}) %collective-permute-start) | collective-permute-done | bytes 40992 | tf_op jit(solution)/shard_map/ppermute | solution.py:228
  43.4 3.5 %collective-permute-start.2 = (bf16[32,128]{1,0:T(8,128)(2,1)S(1)}, bf16[32,128]{1,0:T(8,128)(2,1)S(1)}, u32[]{:S(2)}, u32[]{:S(2)}) collective-permute-start(bf16[32,128]{1,0:T(8,128)(2,1)S(1)} %pad_maximum_fusion.2.two_ref), channel_id=1, source_target_pairs={{0,2},{2,0},{4,6},{6,4},{1,3},{3,1},{5,7},{7,5},{8,10},{10,8},{12,... | collective-permute-start | bytes 24584 | tf_op jit(solution)/shard_map/ppermute | solution.py:228
  46.9 2.1 %collective-permute-done.2.four_ref = bf16[32,128]{1,0:T(8,128)(2,1)S(1)} collective-permute-done((bf16[32,128]{1,0:T(8,128)(2,1)S(1)}, bf16[32,128]{1,0:T(8,128)(2,1)S(1)}, u32[]{:S(2)}, u32[]{:S(2)}) %collective-permute-start.2) | collective-permute-done | bytes 8224 | tf_op jit(solution)/shard_map/ppermute | solution.py:228
  49.1 5.1 %collective-permute-start.3 = (bf16[32,256]{1,0:T(8,128)(2,1)S(1)}, bf16[32,256]{1,0:T(8,128)(2,1)S(1)}, u32[]{:S(2)}, u32[]{:S(2)}) collective-permute-start(bf16[32,256]{1,0:T(8,128)(2,1)S(1)} %pad_maximum_fusion), channel_id=1, source_target_pairs={{0,4},{2,6},{4,0},{6,2},{1,5},{3,7},{5,1},{7,3},{8,12},{10,14},{12... | collective-permute-start | bytes 49160 | tf_op jit(solution)/shard_map/ppermute | solution.py:228
  54.2 1.9 %collective-permute-start.1 = (f32[7,512]{1,0:T(8,128)S(1)}, f32[7,512]{1,0:T(8,128)S(1)}, u32[]{:S(2)}, u32[]{:S(2)}) collective-permute-start(f32[7,512]{1,0:T(8,128)S(1)} %copy-done.10), channel_id=1, source_target_pairs={{0,1},{1,0},{2,3},{3,2},{4,5},{5,4},{6,7},{7,6},{8,9},{9,8},{10,11... | collective-permute-start | bytes 43016 | tf_op jit(solution)/shard_map/ppermute | solution.py:228
  56.1 0.1 copy.13.rows_ref
  56.3 1.0 collective-permute-done.1.other_ref
  57.3 1.7 %kernel.1.kernel_ref = bf16[512,1024]{1,0:T(8,128)(2,1)S(1)} custom-call(f32[7,512]{1,0:T(8,128)S(1)} %copy-done.10, f32[7,512]{1,0:T(8,128)S(1)} %collective-permute-done.1.other_ref, s32[4,8]{1,0:T(4,128)S(1)} %copy-done.11), custom_call_target="tpu_custom_call" | custom-call | tf_op jit(solution)/shard_map/kernel/pallas_call | solution.py:266
  59.1 0.6 nearby.2
  59.7 0.1 copy-done.5
  59.9 2.4 %middle.1 = (bf16[32,512]{1,0:T(8,128)(2,1)}, bf16[8,272,128]{2,1,0:T(8,128)(2,1)S(1)}, bf16[32,640]{1,0:T(8,128)(2,1)S(1)}) custom-call(bf16[8,64,128]{2,1,0:T(8,128)(2,1)S(1)} %all-to-all-done.1.recv_ref, f32[64,128]{1,0:T(8,128)S(1)} %get-tuple-element.15.spread_ref, f32[32,512]{1,0:T(8,128)S(1)} %get-tuple-element.16.base_ref, ...), custom_call_target="tpu_custom_call" | custom-call | tf_op jit(solution)/shard_map/middle/pallas_call | solution.py:270
  62.3 13.6 %all_to_all.21.recv_ref = bf16[8,272,128]{2,1,0:T(8,128)(2,1)S(1)} all-to-all(bf16[8,272,128]{2,1,0:T(8,128)(2,1)S(1)} %get-tuple-element.20), channel_id=1, replica_groups=mesh['a'=8,'b'=2,'y'=4,'x'=4,'c'=2] {'b','y'}, dimensions={0} | all-to-all | bytes 1114112 | tf_op jit(solution)/shard_map/all_to_all | solution.py:252
  75.9 1.0 merge.3
  76.9 12.0 %all-to-all-start.3 = ((bf16[8,64,128]{2,1,0:T(8,128)(2,1)}), bf16[8,64,128]{2,1,0:T(8,128)(2,1)S(1)}, u32[]{:S(2)}, u32[]{:S(2)}) async-start(bf16[8,64,128]{2,1,0:T(8,128)(2,1)} %merge.3), calls=%async_computation.3 | async-start | bytes 262144 | tf_op jit(solution)/shard_map/all_to_all | solution.py:253
  88.9 1.9 %collective-permute-start.4 = (bf16[32,640]{1,0:T(8,128)(2,1)S(1)}, bf16[32,640]{1,0:T(8,128)(2,1)S(1)}, u32[]{:S(2)}, u32[]{:S(2)}) collective-permute-start(bf16[32,640]{1,0:T(8,128)(2,1)S(1)} %get-tuple-element.21), channel_id=1, source_target_pairs={{0,1},{1,0},{2,3},{3,2},{4,5},{5,4},{6,7},{7,6},{8,9},{9,8},{10,11... | collective-permute-start | bytes 122888 | tf_op jit(solution)/shard_map/ppermute | solution.py:228
  90.9 1.2 %collective-permute-done.4.other_ref = bf16[32,640]{1,0:T(8,128)(2,1)S(1)} collective-permute-done((bf16[32,640]{1,0:T(8,128)(2,1)S(1)}, bf16[32,640]{1,0:T(8,128)(2,1)S(1)}, u32[]{:S(2)}, u32[]{:S(2)}) %collective-permute-start.4) | collective-permute-done | bytes 40992 | tf_op jit(solution)/shard_map/ppermute | solution.py:228
  92.1 2.5 %collective-permute-start.5 = (bf16[32,128]{1,0:T(8,128)(2,1)S(1)}, bf16[32,128]{1,0:T(8,128)(2,1)S(1)}, u32[]{:S(2)}, u32[]{:S(2)}) collective-permute-start(bf16[32,128]{1,0:T(8,128)(2,1)S(1)} %pad_maximum_fusion.3.two_ref), channel_id=1, source_target_pairs={{0,2},{2,0},{4,6},{6,4},{1,3},{3,1},{5,7},{7,5},{8,10},{10,8},{12,... | collective-permute-start | bytes 24584 | tf_op jit(solution)/shard_map/ppermute | solution.py:228
  94.6 3.0 %collective-permute-done.5.four_ref = bf16[32,128]{1,0:T(8,128)(2,1)S(1)} collective-permute-done((bf16[32,128]{1,0:T(8,128)(2,1)S(1)}, bf16[32,128]{1,0:T(8,128)(2,1)S(1)}, u32[]{:S(2)}, u32[]{:S(2)}) %collective-permute-start.5) | collective-permute-done | bytes 8224 | tf_op jit(solution)/shard_map/ppermute | solution.py:228
  97.7 2.5 %collective-permute-start.6 = (bf16[32,256]{1,0:T(8,128)(2,1)S(1)}, bf16[32,256]{1,0:T(8,128)(2,1)S(1)}, u32[]{:S(2)}, u32[]{:S(2)}) collective-permute-start(bf16[32,256]{1,0:T(8,128)(2,1)S(1)} %pad_maximum_fusion.1), channel_id=1, source_target_pairs={{0,4},{2,6},{4,0},{6,2},{1,5},{3,7},{5,1},{7,3},{8,12},{10,14},{12... | collective-permute-start | bytes 49160 | tf_op jit(solution)/shard_map/ppermute | solution.py:228
  100.2 4.6 %collective-permute-done.6.eight_ref = bf16[32,256]{1,0:T(8,128)(2,1)S(1)} collective-permute-done((bf16[32,256]{1,0:T(8,128)(2,1)S(1)}, bf16[32,256]{1,0:T(8,128)(2,1)S(1)}, u32[]{:S(2)}, u32[]{:S(2)}) %collective-permute-start.6) | collective-permute-done | bytes 16416 | tf_op jit(solution)/shard_map/ppermute | solution.py:228
  104.9 0.6 nearby.3
  105.5 0.8 last.1
  (37 shorter events, 0.5 us)
Async XLA Ops:
  0.6 0.7 copy-start.12
  0.6 0.7 copy-start.13
  0.7 0.7 copy-start.14
  1.3 1.2 %copy-start = (bf16[64,64,64]{2,1,0:T(8,128)(2,1)S(1)}, bf16[64,64,64]{2,1,0:T(8,128)(2,1)}, u32[]{:S(2)}) copy-start(bf16[64,64,64]{2,1,0:T(8,128)(2,1)} %coupling_ref.1) | copy-start | bytes 1572868
  2.5 0.8 copy-start.2
  3.4 0.8 copy-start.4
  4.2 0.8 copy-start.7
  26.2 33.5 %all-to-all-start.1 = ((bf16[8,64,128]{2,1,0:T(8,128)(2,1)}), bf16[8,64,128]{2,1,0:T(8,128)(2,1)S(1)}, u32[]{:S(2)}, u32[]{:S(2)}) async-start(bf16[8,64,128]{2,1,0:T(8,128)(2,1)} %merge.2), calls=%async_computation.1 | async-start | bytes 262144 | tf_op jit(solution)/shard_map/all_to_all | solution.py:253
  40.0 16.1 %copy-start.15 = (bf16[1,512,64]{1,2,0:T(8,128)(2,1)S(1)}, bf16[1,512,64]{1,2,0:T(8,128)(2,1)}, u32[]{:S(2)}) copy-start(bf16[1,512,64]{1,2,0:T(8,128)(2,1)} %param.16) | copy-start | bytes 196612
  40.0 3.2 %collective-permute-start = (bf16[32,640]{1,0:T(8,128)(2,1)S(1)}, bf16[32,640]{1,0:T(8,128)(2,1)S(1)}, u32[]{:S(2)}, u32[]{:S(2)}) collective-permute-start(bf16[32,640]{1,0:T(8,128)(2,1)S(1)} %get-tuple-element.14), channel_id=1, source_target_pairs={{0,1},{1,0},{2,3},{3,2},{4,5},{5,4},{6,7},{7,6},{8,9},{9,8},{10,11... | collective-permute-start | bytes 122888 | tf_op jit(solution)/shard_map/ppermute | solution.py:228
  43.4 10.8 %copy-start.10 = (f32[7,512]{1,0:T(8,128)S(1)}, f32[7,512]{1,0:T(8,128)}, u32[]{:S(2)}) copy-start(f32[7,512]{1,0:T(8,128)} %own_ref.1) | copy-start | bytes 43012
  43.4 5.7 %collective-permute-start.2 = (bf16[32,128]{1,0:T(8,128)(2,1)S(1)}, bf16[32,128]{1,0:T(8,128)(2,1)S(1)}, u32[]{:S(2)}, u32[]{:S(2)}) collective-permute-start(bf16[32,128]{1,0:T(8,128)(2,1)S(1)} %pad_maximum_fusion.2.two_ref), channel_id=1, source_target_pairs={{0,2},{2,0},{4,6},{6,4},{1,3},{3,1},{5,7},{7,5},{8,10},{10,8},{12,... | collective-permute-start | bytes 24584 | tf_op jit(solution)/shard_map/ppermute | solution.py:228
  49.1 8.2 %copy-start.11 = (s32[4,8]{1,0:T(4,128)S(1)}, s32[4,8]{1,0:T(4,128)}, u32[]{:S(2)}) copy-start(s32[4,8]{1,0:T(4,128)} %mask_ref.1) | copy-start | bytes 388
  49.1 9.9 %collective-permute-start.3 = (bf16[32,256]{1,0:T(8,128)(2,1)S(1)}, bf16[32,256]{1,0:T(8,128)(2,1)S(1)}, u32[]{:S(2)}, u32[]{:S(2)}) collective-permute-start(bf16[32,256]{1,0:T(8,128)(2,1)S(1)} %pad_maximum_fusion), channel_id=1, source_target_pairs={{0,4},{2,6},{4,0},{6,2},{1,5},{3,7},{5,1},{7,3},{8,12},{10,14},{12... | collective-permute-start | bytes 49160 | tf_op jit(solution)/shard_map/ppermute | solution.py:228
  54.2 3.1 %collective-permute-start.1 = (f32[7,512]{1,0:T(8,128)S(1)}, f32[7,512]{1,0:T(8,128)S(1)}, u32[]{:S(2)}, u32[]{:S(2)}) collective-permute-start(f32[7,512]{1,0:T(8,128)S(1)} %copy-done.10), channel_id=1, source_target_pairs={{0,1},{1,0},{2,3},{3,2},{4,5},{5,4},{6,7},{7,6},{8,9},{9,8},{10,11... | collective-permute-start | bytes 43016 | tf_op jit(solution)/shard_map/ppermute | solution.py:228
  56.1 2.9 %copy-start.3 = (bf16[4,64,64]{2,1,0:T(8,128)(2,1)S(1)}, bf16[4,64,64]{2,1,0:T(8,128)(2,1)}, u32[]{:S(2)}) copy-start(bf16[4,64,64]{2,1,0:T(8,128)(2,1)} %transfer_ref.5) | copy-start | bytes 98308
  56.3 2.8 %copy-start.8 = (bf16[32,512]{1,0:T(8,128)(2,1)S(1)}, bf16[32,512]{1,0:T(8,128)(2,1)}, u32[]{:S(2)}) copy-start(bf16[32,512]{1,0:T(8,128)(2,1)} %value_ref.1) | copy-start | bytes 98308
  56.3 3.5 %copy-start.1 = (bf16[64,64,64]{2,1,0:T(8,128)(2,1)S(1)}, bf16[64,64,64]{2,1,0:T(8,128)(2,1)}, u32[]{:S(2)}) copy-start(bf16[64,64,64]{2,1,0:T(8,128)(2,1)} %coupling_ref.1) | copy-start | bytes 1572868
  59.0 0.8 copy-start.5
  59.0 0.9 copy-start.6
  76.9 28.6 %all-to-all-start.3 = ((bf16[8,64,128]{2,1,0:T(8,128)(2,1)}), bf16[8,64,128]{2,1,0:T(8,128)(2,1)S(1)}, u32[]{:S(2)}, u32[]{:S(2)}) async-start(bf16[8,64,128]{2,1,0:T(8,128)(2,1)} %merge.3), calls=%async_computation.3 | async-start | bytes 262144 | tf_op jit(solution)/shard_map/all_to_all | solution.py:253
  88.9 3.1 %collective-permute-start.4 = (bf16[32,640]{1,0:T(8,128)(2,1)S(1)}, bf16[32,640]{1,0:T(8,128)(2,1)S(1)}, u32[]{:S(2)}, u32[]{:S(2)}) collective-permute-start(bf16[32,640]{1,0:T(8,128)(2,1)S(1)} %get-tuple-element.21), channel_id=1, source_target_pairs={{0,1},{1,0},{2,3},{3,2},{4,5},{5,4},{6,7},{7,6},{8,9},{9,8},{10,11... | collective-permute-start | bytes 122888 | tf_op jit(solution)/shard_map/ppermute | solution.py:228
  92.1 12.8 %copy-start.9 = (bf16[32,512]{1,0:T(8,128)(2,1)S(1)}, bf16[32,512]{1,0:T(8,128)(2,1)}, u32[]{:S(2)}) copy-start(bf16[32,512]{1,0:T(8,128)(2,1)} %get-tuple-element.11.value_ref) | copy-start | bytes 98308
  92.1 5.5 %collective-permute-start.5 = (bf16[32,128]{1,0:T(8,128)(2,1)S(1)}, bf16[32,128]{1,0:T(8,128)(2,1)S(1)}, u32[]{:S(2)}, u32[]{:S(2)}) collective-permute-start(bf16[32,128]{1,0:T(8,128)(2,1)S(1)} %pad_maximum_fusion.3.two_ref), channel_id=1, source_target_pairs={{0,2},{2,0},{4,6},{6,4},{1,3},{3,1},{5,7},{7,5},{8,10},{10,8},{12,... | collective-permute-start | bytes 24584 | tf_op jit(solution)/shard_map/ppermute | solution.py:228
  97.7 7.1 %collective-permute-start.6 = (bf16[32,256]{1,0:T(8,128)(2,1)S(1)}, bf16[32,256]{1,0:T(8,128)(2,1)S(1)}, u32[]{:S(2)}, u32[]{:S(2)}) collective-permute-start(bf16[32,256]{1,0:T(8,128)(2,1)S(1)} %pad_maximum_fusion.1), channel_id=1, source_target_pairs={{0,4},{2,6},{4,0},{6,2},{1,5},{3,7},{5,1},{7,3},{8,12},{10,14},{12... | collective-permute-start | bytes 49160 | tf_op jit(solution)/shard_map/ppermute | solution.py:228

commit v3 on v2

--- a/solution.py
+++ b/solution.py
@@ -19,6 +19,7 @@
 SLOTS = 2 * NA
 ROWS = 16
 CHUNK = SLOTS * ROWS + SLOTS
+PARTS = 3
 EMPTY = 4
 F32, BF16 = jnp.float32, jnp.bfloat16
 NT = (((1,), (1,)), ((), ()))
@@ -53,14 +54,21 @@
     return slice(leaf * LEAF_SIZE, (leaf + 1) * LEAF_SIZE)
 
 
+def split_parts(value):
+    high = value.astype(BF16)
+    rest = value - high.astype(F32)
+    middle = rest.astype(BF16)
+    return high, middle, (rest - middle.astype(F32)).astype(BF16)
+
+
 def leaf_coeffs(value_ref, basis_ref, transfer_ref, swap_ref, coeff_ref):
     cluster = jnp.zeros((RIGHT_SIDES, RANK), F32)
     for leaf in range(LEAVES):
         coeff = dot(value_ref[:, leaf_cols(leaf)], basis_ref[:, leaf_cols(leaf)], NT).astype(BF16)
         coeff_ref[leaf * RIGHT_SIDES : (leaf + 1) * RIGHT_SIDES, :] = coeff
         cluster += dot(coeff, transfer_ref[leaf])
-    swap_ref[:, : LEAVES * LEAF_SIZE] = value_ref[...]
-    swap_ref[:, LEAVES * LEAF_SIZE :] = jnp.concatenate([cluster, jnp.zeros_like(cluster)], axis=1).astype(BF16)
+    swap_ref[:RIGHT_SIDES, : LEAVES * LEAF_SIZE] = value_ref[...]
+    swap_ref[:RIGHT_SIDES, LEAVES * LEAF_SIZE :] = jnp.concatenate([cluster, jnp.zeros_like(cluster)], axis=1).astype(BF16)
 
 
 def product(block, place_ref, coupling_ref, coeff_ref, send_ref):
@@ -79,20 +87,21 @@
 
 
 def first_body(
-    leaf_ref, wide_ref, target_ref, value_hbm, basis_hbm, transfer_hbm, coupling_hbm,
+    leaf_ref, wide_ref, target_ref, panel_hbm, value_hbm, basis_hbm, transfer_hbm, coupling_hbm,
     send_ref, swap_ref, ids_ref, place_ref,
-    value_ref, basis_ref, transfer_ref, coupling_ref, coeff_ref, row_ref, count_ref, sems,
+    panel_ref, value_ref, basis_ref, transfer_ref, coupling_ref, coeff_ref, row_ref, count_ref, sems,
 ):
     copies = [
         pltpu.make_async_copy(value_hbm, value_ref, sems.at[0]),
         pltpu.make_async_copy(basis_hbm, basis_ref, sems.at[1]),
         pltpu.make_async_copy(transfer_hbm, transfer_ref, sems.at[2]),
+        pltpu.make_async_copy(panel_hbm, panel_ref, sems.at[3]),
     ]
     parts = 4
     each = OUTS // parts
     for part in range(parts):
         span = pl.ds(part * each, each)
-        copies.append(pltpu.make_async_copy(coupling_hbm.at[span], coupling_ref.at[span], sems.at[3 + part]))
+        copies.append(pltpu.make_async_copy(coupling_hbm.at[span], coupling_ref.at[span], sems.at[4 + part]))
     for copy in copies:
         copy.start()
     for wide in range(NA * PEERS):
@@ -111,11 +120,16 @@
         ids = row_ref[peer * SLOTS : (peer + 1) * SLOTS, :].astype(BF16)
         ids_ref[peer] = ids
         send_ref[peer, SLOTS * ROWS :, :] = ids
-    for copy in copies[:3]:
+    for copy in copies[:4]:
         copy.wait()
     leaf_coeffs(value_ref, basis_ref, transfer_ref, swap_ref, coeff_ref)
+    swap_ref[RIGHT_SIDES:, :] = jnp.zeros((PARTS * ROWS, LEAVES * LEAF_SIZE + 128), BF16)
+    panel = jnp.concatenate([panel_ref[...], jnp.zeros((ROWS - 7, LEAVES * LEAF_SIZE), F32)], axis=0)
+    for part, rows in enumerate(split_parts(panel)):
+        start = RIGHT_SIDES + part * ROWS
+        swap_ref[start : start + ROWS, : LEAVES * LEAF_SIZE] = rows
     for part in range(parts):
-        copies[3 + part].wait()
+        copies[4 + part].wait()
         for block in range(part * each, (part + 1) * each):
             product(block, place_ref, coupling_ref, coeff_ref, send_ref)
 
@@ -135,7 +149,13 @@
             out_ref[pair, leaf * ROWS : (leaf + 1) * ROWS, :] = total[leaf].astype(BF16)
 
 
-def kernel_body(own_ref, other_ref, mask_ref, kernel_ref):
+def kernel_body(own_ref, packet_ref, mask_ref, kernel_ref, other_ref):
+    width = LEAVES * LEAF_SIZE
+    start = RIGHT_SIDES
+    high, middle, low = [
+        packet_ref[start + part * ROWS : start + (part + 1) * ROWS, :width].astype(F32) for part in range(PARTS)
+    ]
+    other_ref[...] = (high + (middle + low))[:8]
     columns = jnp.transpose(
         jnp.concatenate([own_ref[0:3, :], jnp.zeros((5, LEAVES * LEAF_SIZE), F32)], axis=0)
     )
@@ -161,7 +181,7 @@
     for leaf in range(LEAVES):
         low, high = max(leaf - 1, 0) * LEAF_SIZE, min(leaf + 2, LEAVES) * LEAF_SIZE
         near = dot(value_ref[:, low:high], kernel_ref[leaf_cols(leaf), low:high], NT)
-        near += dot(other_ref[:, low:high], kernel_ref[leaf_cols(leaf), width + low : width + high], NT)
+        near += dot(other_ref[:RIGHT_SIDES, low:high], kernel_ref[leaf_cols(leaf), width + low : width + high], NT)
         base_ref[:, leaf_cols(leaf)] = near + 0.5 * value_ref[:, leaf_cols(leaf)].astype(F32)
     me = lax.axis_index("x") * NC + lax.axis_index("c")
     down = jnp.zeros((RIGHT_SIDES, RANK), F32)
@@ -220,7 +240,8 @@
 ):
     panels_here = LEAVES * LEAF_SIZE
     values = shape(RIGHT_SIDES, panels_here)
-    sends = [shape(PEERS, CHUNK, 128), shape(RIGHT_SIDES, panels_here + 128)]
+    packet_width = panels_here + 128
+    send_shape = shape(PEERS, CHUNK, 128)
     coeff_work = pltpu.VMEM((LEAVES * RIGHT_SIDES, RANK), BF16)
 
     def swap(block, axis, distance):
@@ -228,9 +249,14 @@
         return lax.ppermute(block, axis, [(i, i ^ distance) for i in range(count)])
 
     first = call(
-        first_body, "first", sends + [shape(PEERS, SLOTS, 128), shape(OUTS, dtype=jnp.int32)],
-        [SM] * 3 + [pl.ANY] * 4,
+        first_body, "first",
         [
+            send_shape, shape(RIGHT_SIDES + PARTS * ROWS, packet_width),
+            shape(PEERS, SLOTS, 128), shape(OUTS, dtype=jnp.int32),
+        ],
+        [SM] * 3 + [pltpu.HBM] * 5,
+        [
+            pltpu.VMEM((7, panels_here), F32),
             pltpu.VMEM((RIGHT_SIDES, panels_here), BF16),
             pltpu.VMEM((RANK, panels_here), BF16),
             pltpu.VMEM((LEAVES, RANK, RANK), BF16),
@@ -238,7 +264,7 @@
             coeff_work,
             pltpu.VMEM((PEERS * SLOTS, 128), F32),
             pltpu.SMEM((NA * PEERS,), jnp.int32),
-            pltpu.SemaphoreType.DMA((7,)),
+            pltpu.SemaphoreType.DMA((8,)),
         ],
         [VM, VM, VM, SM],
     )
@@ -248,31 +274,37 @@
         [shape(RIGHT_SIDES, panels_here, dtype=F32), shape(LEAVES * ROWS, 128, dtype=F32)], [VM] * 8,
     )
 
-    def couple(send):
+    def together(*arrays):
+        return lax.optimization_barrier(arrays)
+
+    def couple(value, send, packet, kernel):
+        columns = slice(panels_here, panels_here + RANK)
         arrived = lax.all_to_all(send, ("b", "y"), 0, 0, tiled=True)
-        return lax.all_to_all(merge(arrived)[0], "a", 0, 0, tiled=True)
-
-    def local(value, packet, kernel):
         other = swap(packet, "c", 1)
-        two = jnp.concatenate([packet[:, panels_here : panels_here + RANK], other[:, panels_here : panels_here + RANK]], axis=1)
+        two = jnp.concatenate([packet[:RIGHT_SIDES, columns], other[:RIGHT_SIDES, columns]], axis=1)
         four = swap(two, "x", 1)
+        arrived, four = together(arrived, four)
+        merged, four = together(merge(arrived)[0], four)
+        received = lax.all_to_all(merged, "a", 0, 0, tiled=True)
         eight = swap(jnp.concatenate([two, four], axis=1), "x", 2)
-        return nearby(value, other, kernel, two, four, eight, cluster_coupling, leaf_transfer)
+        if kernel is None:
+            kernel = call(
+                kernel_body, "kernel", [shape(panels_here, 2 * panels_here)], [VM, VM, SM],
+                [pltpu.VMEM((8, panels_here), F32)],
+            )(panels, other, near_mask)[0]
+        base, spread = nearby(value, other, kernel, two, four, eight, cluster_coupling, leaf_transfer)
+        return received, base, spread, kernel
 
     send, packet, ids, place = first(
-        out_leaf, out_wide.reshape(OUTS), out_target, density, source_basis, leaf_transfer, coupling
-    )
-    received = couple(send)
-    kernel = call(kernel_body, "kernel", [shape(panels_here, 2 * panels_here)], [VM, VM, SM])(
-        panels, swap(panels, "c", 1), near_mask
-    )[0]
-    base, spread = local(density, packet, kernel)
+        out_leaf, out_wide.reshape(OUTS), out_target, panels, density, source_basis, leaf_transfer, coupling
+    )
+    received, base, spread, kernel = couple(density, send, packet, None)
     first_pass, send, packet = call(
-        middle_body, "middle", [values] + sends, [VM, VM, VM, VM, SM, VM, VM, VM, VM], [coeff_work]
+        middle_body, "middle", [values, send_shape, shape(RIGHT_SIDES, packet_width)],
+        [VM, VM, VM, VM, SM, VM, VM, VM, VM], [coeff_work],
     )(received, spread, base, target_basis, place, ids, source_basis, leaf_transfer, coupling)
 
-    received = couple(send)
-    base, spread = local(first_pass, packet, kernel)
+    received, base, spread, kernel = couple(first_pass, send, packet, kernel)
     second_pass = call(last_body, "last", [values], [VM] * 4)(received, spread, base, target_basis)[0]
     return (first_pass, second_pass)
 

time: 107 us -> 96 us (0.90)
  the two profiles are of different devices: /device:TPU:64 before, /device:TPU:14 now
where the time goes in v3:
time: 96 us; the launch traced here: 95 us
  starting transfers between devices  46.4 us (48%)
  waiting for transfers between devices  29.5 us (31%)
  Pallas kernels  12.7 us (13%)
  local copies, waits for them, and re-layouts  5.21 us (5%)
    all_to_all x2, starting transfers between devices, couple(): received = lax.all_to_all(merged, 'a', 0, 0, tiled=True)  19.7 us
    ppermute x6, starting transfers between devices, swap(): return lax.ppermute(block, axis, [(i, i ^ distance) for i in range(count)])  16 us
    all_to_all x2, waiting for transfers between devices, couple(): received = lax.all_to_all(merged, 'a', 0, 0, tiled=True)  15.8 us
    ppermute x6, waiting for transfers between devices, swap(): return lax.ppermute(block, axis, [(i, i ^ distance) for i in range(count)])  13.7 us
    all_to_all x2, starting transfers between devices, couple(): arrived = lax.all_to_all(send, ('b', 'y'), 0, 0, tiled=True)  10.7 us
    unnamed x35, local copies, waits for them, and re-layouts  5.2 us
    pallas_call x1, Pallas kernels, shards(): first(out_leaf, out_wide.reshape(OUTS), out_target, panels, density, sour...  4.17 us
    pallas_call x1, Pallas kernels, shards(): call(middle_body, 'middle', [values, send_shape, shape(RIGHT_SIDES, packe...  2.69 us
  transfers between devices with their start and end apart: 10, of which 8 were waited for; matrix products, arithmetic and copies ran while one was open for 0% of the time, Pallas kernels for 3%

profile of v3, /device:TPU:14, one launch (start us, length us, event | category | flops | bytes accessed | tf_op | source)
XLA Modules:
  0.0 95.0 jit_solution(390677252534035471)
XLA Ops:
  0.7 0.6 copy-done.13
  1.3 1.2 %copy-done = bf16[64,64,64]{2,1,0:T(8,128)(2,1)S(1)} copy-done((bf16[64,64,64]{2,1,0:T(8,128)(2,1)S(1)}, bf16[64,64,64]{2,1,0:T(8,128)(2,1)}, u32[]{:S(2)}) %copy-start) | copy-done | bytes 524312
  2.5 0.8 copy-done.2
  3.4 0.8 copy-done.5
  4.2 0.8 copy-done.7
  5.0 0.7 copy-done.9
  5.7 4.2 %first.1 = (bf16[8,272,128]{2,1,0:T(8,128)(2,1)}, bf16[80,640]{1,0:T(8,128)(2,1)S(1)}, bf16[8,16,128]{2,1,0:T(8,128)(2,1)S(1)}, s32[64]{0:T(128)S(1)}) custom-call(s32[64]{0:T(128)S(1)} %copy-done.13, s32[64]{0:T(128)S(1)} %bitcast.1, s32[64]{0:T(128)S(1)} %copy-done.15, f32[7,512]{1,0:T(8,128)S(1)} %copy-done.9, bf16[32,512]{1,0:T(8,128)(2,1)S(1)} %copy-done.7, ...), custom_call_target="tpu_custom_call" | custom-call | tf_op jit(solution)/shard_map/first/pallas_call | solution.py:298
  9.9 6.3 %all-to-all-start = ((bf16[8,272,128]{2,1,0:T(8,128)(2,1)}), bf16[8,272,128]{2,1,0:T(8,128)(2,1)S(1)}, u32[]{:S(2)}, u32[]{:S(2)}) async-start(bf16[8,272,128]{2,1,0:T(8,128)(2,1)} %get-tuple-element.21), calls=%async_computation | async-start | bytes 1114112 | tf_op jit(solution)/shard_map/all_to_all | solution.py:282
  16.2 1.9 %collective-permute-start = (bf16[80,640]{1,0:T(8,128)(2,1)S(1)}, bf16[80,640]{1,0:T(8,128)(2,1)S(1)}, u32[]{:S(2)}, u32[]{:S(2)}) collective-permute-start(bf16[80,640]{1,0:T(8,128)(2,1)S(1)} %get-tuple-element.22), channel_id=1, source_target_pairs={{0,1},{1,0},{2,3},{3,2},{4,5},{5,4},{6,7},{7,6},{8,9},{9,8},{10,11... | collective-permute-start | bytes 307208 | tf_op jit(solution)/shard_map/ppermute | solution.py:249
  18.1 1.3 %collective-permute-done.packet_ref.other_ref = bf16[80,640]{1,0:T(8,128)(2,1)S(1)} collective-permute-done((bf16[80,640]{1,0:T(8,128)(2,1)S(1)}, bf16[80,640]{1,0:T(8,128)(2,1)S(1)}, u32[]{:S(2)}, u32[]{:S(2)}) %collective-permute-start) | collective-permute-done | bytes 102432 | tf_op jit(solution)/shard_map/ppermute | solution.py:249
  19.4 2.7 %collective-permute-start.1 = (bf16[32,128]{1,0:T(8,128)(2,1)S(1)}, bf16[32,128]{1,0:T(8,128)(2,1)S(1)}, u32[]{:S(2)}, u32[]{:S(2)}) collective-permute-start(bf16[32,128]{1,0:T(8,128)(2,1)S(1)} %pad_maximum_fusion.2.two_ref), channel_id=1, source_target_pairs={{0,2},{2,0},{4,6},{6,4},{1,3},{3,1},{5,7},{7,5},{8,10},{10,8},{12,... | collective-permute-start | bytes 24584 | tf_op jit(solution)/shard_map/ppermute | solution.py:249
  22.2 2.8 %collective-permute-done.1.four_ref = bf16[32,128]{1,0:T(8,128)(2,1)S(1)} collective-permute-done((bf16[32,128]{1,0:T(8,128)(2,1)S(1)}, bf16[32,128]{1,0:T(8,128)(2,1)S(1)}, u32[]{:S(2)}, u32[]{:S(2)}) %collective-permute-start.1) | collective-permute-done | bytes 8224 | tf_op jit(solution)/shard_map/ppermute | solution.py:249
  25.0 1.0 %merge.2 = bf16[8,64,128]{2,1,0:T(8,128)(2,1)} custom-call(bf16[8,272,128]{2,1,0:T(8,128)(2,1)S(1)} %all-to-all-done.recv_ref), custom_call_target="tpu_custom_call" | custom-call | tf_op jit(solution)/shard_map/merge/pallas_call | solution.py:287
  26.0 14.3 %all-to-all-start.1 = ((bf16[8,64,128]{2,1,0:T(8,128)(2,1)}), bf16[8,64,128]{2,1,0:T(8,128)(2,1)S(1)}, u32[]{:S(2)}, u32[]{:S(2)}) async-start(bf16[8,64,128]{2,1,0:T(8,128)(2,1)} %merge.2), calls=%async_computation.1 | async-start | bytes 262144 | tf_op jit(solution)/shard_map/all_to_all | solution.py:288
  40.4 3.4 %collective-permute-start.2 = (bf16[32,256]{1,0:T(8,128)(2,1)S(1)}, bf16[32,256]{1,0:T(8,128)(2,1)S(1)}, u32[]{:S(2)}, u32[]{:S(2)}) collective-permute-start(bf16[32,256]{1,0:T(8,128)(2,1)S(1)} %pad_maximum_fusion), channel_id=1, source_target_pairs={{0,4},{2,6},{4,0},{6,2},{1,5},{3,7},{5,1},{7,3},{8,12},{10,14},{12... | collective-permute-start | bytes 49160 | tf_op jit(solution)/shard_map/ppermute | solution.py:249
  44.1 1.7 %kernel.1.kernel_ref = bf16[512,1024]{1,0:T(8,128)(2,1)S(1)} custom-call(f32[7,512]{1,0:T(8,128)S(1)} %copy-done.10, bf16[80,640]{1,0:T(8,128)(2,1)S(1)} %collective-permute-done.packet_ref.other_ref, s32[4,8]{1,0:T(4,128)S(1)} %copy-done.12), custom_call_target="tpu_custom_call" | custom-call | tf_op jit(solution)/shard_map/kernel/pallas_call | solution.py:291
  45.8 1.9 %collective-permute-done.2.eight_ref = bf16[32,256]{1,0:T(8,128)(2,1)S(1)} collective-permute-done((bf16[32,256]{1,0:T(8,128)(2,1)S(1)}, bf16[32,256]{1,0:T(8,128)(2,1)S(1)}, u32[]{:S(2)}, u32[]{:S(2)}) %collective-permute-start.2) | collective-permute-done | bytes 16416 | tf_op jit(solution)/shard_map/ppermute | solution.py:249
  47.7 0.6 nearby.2
  48.3 8.0 %all-to-all-done.1.recv_ref = bf16[8,64,128]{2,1,0:T(8,128)(2,1)S(1)} async-done(((bf16[8,64,128]{2,1,0:T(8,128)(2,1)}), bf16[8,64,128]{2,1,0:T(8,128)(2,1)S(1)}, u32[]{:S(2)}, u32[]{:S(2)}) %all-to-all-start.1) | async-done | bytes 131104 | tf_op jit(solution)/shard_map/all_to_all | solution.py:288
  56.3 2.7 %middle.1 = (bf16[32,512]{1,0:T(8,128)(2,1)}, bf16[8,272,128]{2,1,0:T(8,128)(2,1)}, bf16[32,640]{1,0:T(8,128)(2,1)S(1)}) custom-call(bf16[8,64,128]{2,1,0:T(8,128)(2,1)S(1)} %all-to-all-done.1.recv_ref, f32[64,128]{1,0:T(8,128)S(1)} %get-tuple-element.27.spread_ref, f32[32,512]{1,0:T(8,128)S(1)} %get-tuple-element.28.base_ref, ...), custom_call_target="tpu_custom_call" | custom-call | tf_op jit(solution)/shard_map/middle/pallas_call | solution.py:302
  59.0 4.4 %all-to-all-start.2 = ((bf16[8,272,128]{2,1,0:T(8,128)(2,1)}), bf16[8,272,128]{2,1,0:T(8,128)(2,1)S(1)}, u32[]{:S(2)}, u32[]{:S(2)}) async-start(bf16[8,272,128]{2,1,0:T(8,128)(2,1)} %get-tuple-element.32), calls=%async_computation.2 | async-start | bytes 1114112 | tf_op jit(solution)/shard_map/all_to_all | solution.py:282
  63.4 1.9 %collective-permute-start.3 = (bf16[32,640]{1,0:T(8,128)(2,1)S(1)}, bf16[32,640]{1,0:T(8,128)(2,1)S(1)}, u32[]{:S(2)}, u32[]{:S(2)}) collective-permute-start(bf16[32,640]{1,0:T(8,128)(2,1)S(1)} %get-tuple-element.33), channel_id=1, source_target_pairs={{0,1},{1,0},{2,3},{3,2},{4,5},{5,4},{6,7},{7,6},{8,9},{9,8},{10,11... | collective-permute-start | bytes 122888 | tf_op jit(solution)/shard_map/ppermute | solution.py:249
  65.4 1.2 %collective-permute-done.3.other_ref = bf16[32,640]{1,0:T(8,128)(2,1)S(1)} collective-permute-done((bf16[32,640]{1,0:T(8,128)(2,1)S(1)}, bf16[32,640]{1,0:T(8,128)(2,1)S(1)}, u32[]{:S(2)}, u32[]{:S(2)}) %collective-permute-start.3) | collective-permute-done | bytes 40992 | tf_op jit(solution)/shard_map/ppermute | solution.py:249
  66.6 2.7 %collective-permute-start.4 = (bf16[32,128]{1,0:T(8,128)(2,1)S(1)}, bf16[32,128]{1,0:T(8,128)(2,1)S(1)}, u32[]{:S(2)}, u32[]{:S(2)}) collective-permute-start(bf16[32,128]{1,0:T(8,128)(2,1)S(1)} %pad_maximum_fusion.3.two_ref), channel_id=1, source_target_pairs={{0,2},{2,0},{4,6},{6,4},{1,3},{3,1},{5,7},{7,5},{8,10},{10,8},{12,... | collective-permute-start | bytes 24584 | tf_op jit(solution)/shard_map/ppermute | solution.py:249
  69.4 2.8 %collective-permute-done.4.four_ref = bf16[32,128]{1,0:T(8,128)(2,1)S(1)} collective-permute-done((bf16[32,128]{1,0:T(8,128)(2,1)S(1)}, bf16[32,128]{1,0:T(8,128)(2,1)S(1)}, u32[]{:S(2)}, u32[]{:S(2)}) %collective-permute-start.4) | collective-permute-done | bytes 8224 | tf_op jit(solution)/shard_map/ppermute | solution.py:249
  72.2 1.0 %merge.3 = bf16[8,64,128]{2,1,0:T(8,128)(2,1)} custom-call(bf16[8,272,128]{2,1,0:T(8,128)(2,1)S(1)} %all-to-all-done.2.recv_ref), custom_call_target="tpu_custom_call" | custom-call | tf_op jit(solution)/shard_map/merge/pallas_call | solution.py:287
  73.2 5.4 %all-to-all-start.3 = ((bf16[8,64,128]{2,1,0:T(8,128)(2,1)}), bf16[8,64,128]{2,1,0:T(8,128)(2,1)S(1)}, u32[]{:S(2)}, u32[]{:S(2)}) async-start(bf16[8,64,128]{2,1,0:T(8,128)(2,1)} %merge.3), calls=%async_computation.3 | async-start | bytes 262144 | tf_op jit(solution)/shard_map/all_to_all | solution.py:288
  78.6 3.3 %collective-permute-start.5 = (bf16[32,256]{1,0:T(8,128)(2,1)S(1)}, bf16[32,256]{1,0:T(8,128)(2,1)S(1)}, u32[]{:S(2)}, u32[]{:S(2)}) collective-permute-start(bf16[32,256]{1,0:T(8,128)(2,1)S(1)} %pad_maximum_fusion.1), channel_id=1, source_target_pairs={{0,4},{2,6},{4,0},{6,2},{1,5},{3,7},{5,1},{7,3},{8,12},{10,14},{12... | collective-permute-start | bytes 49160 | tf_op jit(solution)/shard_map/ppermute | solution.py:249
  82.0 3.8 %collective-permute-done.5.eight_ref = bf16[32,256]{1,0:T(8,128)(2,1)S(1)} collective-permute-done((bf16[32,256]{1,0:T(8,128)(2,1)S(1)}, bf16[32,256]{1,0:T(8,128)(2,1)S(1)}, u32[]{:S(2)}, u32[]{:S(2)}) %collective-permute-start.5) | collective-permute-done | bytes 16416 | tf_op jit(solution)/shard_map/ppermute | solution.py:249
  85.8 0.6 nearby.3
  86.4 7.8 %all-to-all-done.3.recv_ref = bf16[8,64,128]{2,1,0:T(8,128)(2,1)S(1)} async-done(((bf16[8,64,128]{2,1,0:T(8,128)(2,1)}), bf16[8,64,128]{2,1,0:T(8,128)(2,1)S(1)}, u32[]{:S(2)}, u32[]{:S(2)}) %all-to-all-start.3) | async-done | bytes 131104 | tf_op jit(solution)/shard_map/all_to_all | solution.py:288
  94.2 0.8 last.1
  (39 shorter events, 0.5 us)
Async XLA Ops:
  0.6 0.7 copy-start.13
  0.6 0.7 copy-start.14
  0.7 0.7 copy-start.15
  1.3 1.2 %copy-start = (bf16[64,64,64]{2,1,0:T(8,128)(2,1)S(1)}, bf16[64,64,64]{2,1,0:T(8,128)(2,1)}, u32[]{:S(2)}) copy-start(bf16[64,64,64]{2,1,0:T(8,128)(2,1)} %coupling_ref.1) | copy-start | bytes 1572868
  2.5 0.8 copy-start.2
  3.4 0.8 copy-start.5
  4.2 0.8 copy-start.7
  5.0 0.7 copy-start.9
  9.9 15.1 %all-to-all-start = ((bf16[8,272,128]{2,1,0:T(8,128)(2,1)}), bf16[8,272,128]{2,1,0:T(8,128)(2,1)S(1)}, u32[]{:S(2)}, u32[]{:S(2)}) async-start(bf16[8,272,128]{2,1,0:T(8,128)(2,1)} %get-tuple-element.21), calls=%async_computation | async-start | bytes 1114112 | tf_op jit(solution)/shard_map/all_to_all | solution.py:282
  16.2 3.2 %collective-permute-start = (bf16[80,640]{1,0:T(8,128)(2,1)S(1)}, bf16[80,640]{1,0:T(8,128)(2,1)S(1)}, u32[]{:S(2)}, u32[]{:S(2)}) collective-permute-start(bf16[80,640]{1,0:T(8,128)(2,1)S(1)} %get-tuple-element.22), channel_id=1, source_target_pairs={{0,1},{1,0},{2,3},{3,2},{4,5},{5,4},{6,7},{7,6},{8,9},{9,8},{10,11... | collective-permute-start | bytes 307208 | tf_op jit(solution)/shard_map/ppermute | solution.py:249
  19.4 5.5 %collective-permute-start.1 = (bf16[32,128]{1,0:T(8,128)(2,1)S(1)}, bf16[32,128]{1,0:T(8,128)(2,1)S(1)}, u32[]{:S(2)}, u32[]{:S(2)}) collective-permute-start(bf16[32,128]{1,0:T(8,128)(2,1)S(1)} %pad_maximum_fusion.2.two_ref), channel_id=1, source_target_pairs={{0,2},{2,0},{4,6},{6,4},{1,3},{3,1},{5,7},{7,5},{8,10},{10,8},{12,... | collective-permute-start | bytes 24584 | tf_op jit(solution)/shard_map/ppermute | solution.py:249
  26.0 17.9 %copy-start.16 = (bf16[1,512,64]{1,2,0:T(8,128)(2,1)S(1)}, bf16[1,512,64]{1,2,0:T(8,128)(2,1)}, u32[]{:S(2)}) copy-start(bf16[1,512,64]{1,2,0:T(8,128)(2,1)} %param.16) | copy-start | bytes 196612
  26.0 30.3 %all-to-all-start.1 = ((bf16[8,64,128]{2,1,0:T(8,128)(2,1)}), bf16[8,64,128]{2,1,0:T(8,128)(2,1)S(1)}, u32[]{:S(2)}, u32[]{:S(2)}) async-start(bf16[8,64,128]{2,1,0:T(8,128)(2,1)} %merge.2), calls=%async_computation.1 | async-start | bytes 262144 | tf_op jit(solution)/shard_map/all_to_all | solution.py:288
  40.4 3.6 %copy-start.10 = (f32[7,512]{1,0:T(8,128)S(1)}, f32[7,512]{1,0:T(8,128)}, u32[]{:S(2)}) copy-start(f32[7,512]{1,0:T(8,128)} %own_ref.1) | copy-start | bytes 43012
  40.4 3.6 %copy-start.12 = (s32[4,8]{1,0:T(4,128)S(1)}, s32[4,8]{1,0:T(4,128)}, u32[]{:S(2)}) copy-start(s32[4,8]{1,0:T(4,128)} %mask_ref.1) | copy-start | bytes 388
  40.4 7.3 %collective-permute-start.2 = (bf16[32,256]{1,0:T(8,128)(2,1)S(1)}, bf16[32,256]{1,0:T(8,128)(2,1)S(1)}, u32[]{:S(2)}, u32[]{:S(2)}) collective-permute-start(bf16[32,256]{1,0:T(8,128)(2,1)S(1)} %pad_maximum_fusion), channel_id=1, source_target_pairs={{0,4},{2,6},{4,0},{6,2},{1,5},{3,7},{5,1},{7,3},{8,12},{10,14},{12... | collective-permute-start | bytes 49160 | tf_op jit(solution)/shard_map/ppermute | solution.py:249
  44.0 3.7 %copy-start.3 = (bf16[4,64,64]{2,1,0:T(8,128)(2,1)S(1)}, bf16[4,64,64]{2,1,0:T(8,128)(2,1)}, u32[]{:S(2)}) copy-start(bf16[4,64,64]{2,1,0:T(8,128)(2,1)} %transfer_ref.5) | copy-start | bytes 98308
  44.0 3.7 %copy-start.8 = (bf16[32,512]{1,0:T(8,128)(2,1)S(1)}, bf16[32,512]{1,0:T(8,128)(2,1)}, u32[]{:S(2)}) copy-start(bf16[32,512]{1,0:T(8,128)(2,1)} %value_ref.1) | copy-start | bytes 98308
  44.0 12.3 %copy-start.1 = (bf16[64,64,64]{2,1,0:T(8,128)(2,1)S(1)}, bf16[64,64,64]{2,1,0:T(8,128)(2,1)}, u32[]{:S(2)}) copy-start(bf16[64,64,64]{2,1,0:T(8,128)(2,1)} %coupling_ref.1) | copy-start | bytes 1572868
  45.8 10.5 %copy-start.4 = (bf16[64,512]{1,0:T(8,128)(2,1)S(1)}, bf16[64,512]{1,0:T(8,128)(2,1)}, u32[]{:S(2)}) copy-start(bf16[64,512]{1,0:T(8,128)(2,1)} %target_ref.5) | copy-start | bytes 196612
  45.8 10.5 %copy-start.6 = (bf16[64,512]{1,0:T(8,128)(2,1)S(1)}, bf16[64,512]{1,0:T(8,128)(2,1)}, u32[]{:S(2)}) copy-start(bf16[64,512]{1,0:T(8,128)(2,1)} %basis_ref.1) | copy-start | bytes 196612
  59.0 13.2 %all-to-all-start.2 = ((bf16[8,272,128]{2,1,0:T(8,128)(2,1)}), bf16[8,272,128]{2,1,0:T(8,128)(2,1)S(1)}, u32[]{:S(2)}, u32[]{:S(2)}) async-start(bf16[8,272,128]{2,1,0:T(8,128)(2,1)} %get-tuple-element.32), calls=%async_computation.2 | async-start | bytes 1114112 | tf_op jit(solution)/shard_map/all_to_all | solution.py:282
  63.4 3.1 %collective-permute-start.3 = (bf16[32,640]{1,0:T(8,128)(2,1)S(1)}, bf16[32,640]{1,0:T(8,128)(2,1)S(1)}, u32[]{:S(2)}, u32[]{:S(2)}) collective-permute-start(bf16[32,640]{1,0:T(8,128)(2,1)S(1)} %get-tuple-element.33), channel_id=1, source_target_pairs={{0,1},{1,0},{2,3},{3,2},{4,5},{5,4},{6,7},{7,6},{8,9},{9,8},{10,11... | collective-permute-start | bytes 122888 | tf_op jit(solution)/shard_map/ppermute | solution.py:249
  66.6 5.5 %collective-permute-start.4 = (bf16[32,128]{1,0:T(8,128)(2,1)S(1)}, bf16[32,128]{1,0:T(8,128)(2,1)S(1)}, u32[]{:S(2)}, u32[]{:S(2)}) collective-permute-start(bf16[32,128]{1,0:T(8,128)(2,1)S(1)} %pad_maximum_fusion.3.two_ref), channel_id=1, source_target_pairs={{0,2},{2,0},{4,6},{6,4},{1,3},{3,1},{5,7},{7,5},{8,10},{10,8},{12,... | collective-permute-start | bytes 24584 | tf_op jit(solution)/shard_map/ppermute | solution.py:249
  73.2 21.0 %all-to-all-start.3 = ((bf16[8,64,128]{2,1,0:T(8,128)(2,1)}), bf16[8,64,128]{2,1,0:T(8,128)(2,1)S(1)}, u32[]{:S(2)}, u32[]{:S(2)}) async-start(bf16[8,64,128]{2,1,0:T(8,128)(2,1)} %merge.3), calls=%async_computation.3 | async-start | bytes 262144 | tf_op jit(solution)/shard_map/all_to_all | solution.py:288
  78.6 7.2 %copy-start.11 = (bf16[32,512]{1,0:T(8,128)(2,1)S(1)}, bf16[32,512]{1,0:T(8,128)(2,1)}, u32[]{:S(2)}) copy-start(bf16[32,512]{1,0:T(8,128)(2,1)} %get-tuple-element.19.value_ref) | copy-start | bytes 98308
  78.6 7.1 %collective-permute-start.5 = (bf16[32,256]{1,0:T(8,128)(2,1)S(1)}, bf16[32,256]{1,0:T(8,128)(2,1)S(1)}, u32[]{:S(2)}, u32[]{:S(2)}) collective-permute-start(bf16[32,256]{1,0:T(8,128)(2,1)S(1)} %pad_maximum_fusion.1), channel_id=1, source_target_pairs={{0,4},{2,6},{4,0},{6,2},{1,5},{3,7},{5,1},{7,3},{8,12},{10,14},{12... | collective-permute-start | bytes 49160 | tf_op jit(solution)/shard_map/ppermute | solution.py:249

commit v4 on v3

--- a/solution.py
+++ b/solution.py
@@ -18,9 +18,9 @@
 PEERS = NB * NY
 SLOTS = 2 * NA
 ROWS = 16
-CHUNK = SLOTS * ROWS + SLOTS
+CHUNK = SLOTS * ROWS
+IDS = 16
 PARTS = 3
-EMPTY = 4
 F32, BF16 = jnp.float32, jnp.bfloat16
 NT = (((1,), (1,)), ((), ()))
 
@@ -73,54 +73,58 @@
 
 def product(block, place_ref, coupling_ref, coeff_ref, send_ref):
     place = place_ref[block]
-    source = place % 4
-    slot = (place // 16) % SLOTS
-    peer = place // (16 * SLOTS)
-    coeff = coeff_ref[pl.ds(pl.multiple_of(source * RIGHT_SIDES, RIGHT_SIDES), RIGHT_SIDES), :]
-    packed = pack(dot(coeff, coupling_ref[block])).astype(BF16)
-    send_ref[peer, pl.ds(pl.multiple_of(slot * ROWS, ROWS), ROWS), :] = packed
+    peer = lax.shift_right_logical(place, 8)
+    row = pl.multiple_of(jnp.bitwise_and(place, CHUNK - 1), ROWS)
+    source = pl.multiple_of(place_ref[OUTS + block], RIGHT_SIDES)
+    packed = pack(dot(coeff_ref[pl.ds(source, RIGHT_SIDES), :], coupling_ref[block])).astype(BF16)
+    send_ref[peer, pl.ds(row, ROWS), :] = packed
 
 
 def clear(send_ref):
     for peer in range(PEERS):
-        send_ref[peer, : SLOTS * ROWS, :] = jnp.zeros((SLOTS * ROWS, 128), BF16)
+        send_ref[peer, :CHUNK, :] = jnp.zeros((CHUNK, 128), BF16)
 
 
 def first_body(
-    leaf_ref, wide_ref, target_ref, panel_hbm, value_hbm, basis_hbm, transfer_hbm, coupling_hbm,
-    send_ref, swap_ref, ids_ref, place_ref,
-    panel_ref, value_ref, basis_ref, transfer_ref, coupling_ref, coeff_ref, row_ref, count_ref, sems,
+    leaf_hbm, wide_hbm, target_hbm, panel_hbm, value_hbm, basis_hbm, transfer_hbm, coupling_hbm,
+    send_ref, swap_ref, place_ref,
+    leaf_ref, wide_ref, target_ref, panel_ref, value_ref, basis_ref, transfer_ref, coupling_ref,
+    coeff_ref, row_ref, count_ref, sems,
 ):
-    copies = [
-        pltpu.make_async_copy(value_hbm, value_ref, sems.at[0]),
-        pltpu.make_async_copy(basis_hbm, basis_ref, sems.at[1]),
-        pltpu.make_async_copy(transfer_hbm, transfer_ref, sems.at[2]),
-        pltpu.make_async_copy(panel_hbm, panel_ref, sems.at[3]),
+    pairs = [
+        (wide_hbm, wide_ref), (target_hbm, target_ref), (leaf_hbm, leaf_ref),
+        (value_hbm, value_ref), (basis_hbm, basis_ref), (transfer_hbm, transfer_ref), (panel_hbm, panel_ref),
     ]
     parts = 4
     each = OUTS // parts
     for part in range(parts):
         span = pl.ds(part * each, each)
-        copies.append(pltpu.make_async_copy(coupling_hbm.at[span], coupling_ref.at[span], sems.at[4 + part]))
+        pairs.append((coupling_hbm.at[span], coupling_ref.at[span]))
+    copies = [pltpu.make_async_copy(source, place, sems.at[i]) for i, (source, place) in enumerate(pairs)]
     for copy in copies:
         copy.start()
     for wide in range(NA * PEERS):
         count_ref[wide] = 0
-    row_ref[...] = jnp.full((PEERS * SLOTS, 128), EMPTY, F32)
     clear(send_ref)
+    for copy in copies[:3]:
+        copy.wait()
+    row_ref[...] = jnp.zeros((2 * PEERS * NA, 128), F32)
     for block in range(OUTS):
         wide = wide_ref[block]
-        target = target_ref[block]
         turn = count_ref[wide]
         count_ref[wide] = turn + 1
-        spot = (wide % PEERS) * SLOTS + (wide // PEERS) * 2 + turn
-        place_ref[block] = spot * 16 + target * 4 + leaf_ref[block]
-        row_ref[pl.ds(spot, 1), :] = jnp.full((1, 128), target, jnp.int32).astype(F32)
+        peer = jnp.bitwise_and(wide, PEERS - 1)
+        pair = lax.shift_right_logical(wide, 3)
+        place_ref[block] = peer * CHUNK + (pair * 2 + turn) * ROWS
+        place_ref[OUTS + block] = leaf_ref[block] * RIGHT_SIDES
+        spot = turn * (PEERS * NA) + peer * NA + pair
+        row_ref[pl.ds(spot, 1), :] = jnp.full((1, 128), target_ref[block] + 1, jnp.int32).astype(F32)
+    early = jnp.bitwise_and(lax.broadcasted_iota(jnp.int32, (NA, 128), 1), 2 * ROWS - 1) < ROWS
     for peer in range(PEERS):
-        ids = row_ref[peer * SLOTS : (peer + 1) * SLOTS, :].astype(BF16)
-        ids_ref[peer] = ids
-        send_ref[peer, SLOTS * ROWS :, :] = ids
-    for copy in copies[:4]:
+        turns = [row_ref[(turn * PEERS + peer) * NA : (turn * PEERS + peer + 1) * NA, :] for turn in range(2)]
+        ids = jnp.where(early, turns[0], turns[1])
+        send_ref[peer, CHUNK:, :] = jnp.concatenate([ids, ids], axis=0).astype(BF16)
+    for copy in copies[3:7]:
         copy.wait()
     leaf_coeffs(value_ref, basis_ref, transfer_ref, swap_ref, coeff_ref)
     swap_ref[RIGHT_SIDES:, :] = jnp.zeros((PARTS * ROWS, LEAVES * LEAF_SIZE + 128), BF16)
@@ -129,24 +133,39 @@
         start = RIGHT_SIDES + part * ROWS
         swap_ref[start : start + ROWS, : LEAVES * LEAF_SIZE] = rows
     for part in range(parts):
-        copies[4 + part].wait()
+        copies[7 + part].wait()
         for block in range(part * each, (part + 1) * each):
             product(block, place_ref, coupling_ref, coeff_ref, send_ref)
 
 
-def merge_body(recv_ref, out_ref):
-    ids = [recv_ref[src, SLOTS * ROWS :, :].astype(F32) for src in range(PEERS)]
+def merge(recv_ref, choice_ref, out_ref):
     for pair in range(NA):
-        total = [jnp.zeros((ROWS, 128), F32) for _ in range(LEAVES)]
-        for src in range(PEERS):
-            for turn in range(2):
-                slot = pair * 2 + turn
-                block = recv_ref[src, slot * ROWS : (slot + 1) * ROWS, :].astype(F32)
-                row = jnp.broadcast_to(ids[src][slot : slot + 1, :], (ROWS, 128))
-                for leaf in range(LEAVES):
-                    total[leaf] += jnp.where(row == leaf, block, 0.0)
-        for leaf in range(LEAVES):
-            out_ref[pair, leaf * ROWS : (leaf + 1) * ROWS, :] = total[leaf].astype(BF16)
+        blocks = [recv_ref[src, pair * 2 * ROWS : (pair + 1) * 2 * ROWS, :] for src in range(PEERS)]
+        out_ref[pair] = dot(choice_ref[pair], jnp.concatenate(blocks, axis=0)).astype(BF16)
+
+
+def first_merge_body(recv_ref, out_ref, choice_ref):
+    group = lax.shift_right_logical(lax.broadcasted_iota(jnp.int32, (NA, 128), 1), 5)
+    halves = []
+    for half in range(2):
+        ids = jnp.zeros((NA, 128), F32)
+        for src in range(4):
+            rows = recv_ref[half * 4 + src, CHUNK : CHUNK + IDS, :].astype(F32)[:NA]
+            ids += jnp.where(group == src, rows, 0.0)
+        halves.append(ids)
+    ids = jnp.concatenate(halves, axis=1)
+    dims = (LEAVES * ROWS, 2 * 128)
+    row, lane = lax.broadcasted_iota(jnp.int32, dims, 0), lax.broadcasted_iota(jnp.int32, dims, 1)
+    same = jnp.bitwise_and(row, ROWS - 1) == jnp.bitwise_and(lane, ROWS - 1)
+    wanted = jnp.where(same, lax.shift_right_logical(row, 4) + 1, -1).astype(F32)
+    for pair in range(NA):
+        here = jnp.broadcast_to(ids[pair : pair + 1, :], dims)
+        choice_ref[pair] = jnp.where(here == wanted, 1.0, 0.0).astype(BF16)
+    merge(recv_ref, choice_ref, out_ref)
+
+
+def merge_body(recv_ref, choice_ref, out_ref):
+    merge(recv_ref, choice_ref, out_ref)
 
 
 def kernel_body(own_ref, packet_ref, mask_ref, kernel_ref, other_ref):
@@ -214,13 +233,11 @@
 
 
 def middle_body(
-    recv_ref, spread_ref, base_ref, target_ref, place_ref, ids_ref, basis_ref, transfer_ref, coupling_ref,
+    recv_ref, spread_ref, base_ref, target_ref, place_ref, basis_ref, transfer_ref, coupling_ref,
     out_ref, send_ref, swap_ref, coeff_ref,
 ):
     finish(recv_ref, spread_ref, base_ref, target_ref, out_ref)
     clear(send_ref)
-    for peer in range(PEERS):
-        send_ref[peer, SLOTS * ROWS :, :] = ids_ref[peer]
     leaf_coeffs(out_ref, basis_ref, transfer_ref, swap_ref, coeff_ref)
     for block in range(OUTS):
         product(block, place_ref, coupling_ref, coeff_ref, send_ref)
@@ -241,7 +258,7 @@
     panels_here = LEAVES * LEAF_SIZE
     values = shape(RIGHT_SIDES, panels_here)
     packet_width = panels_here + 128
-    send_shape = shape(PEERS, CHUNK, 128)
+    merged_shape = shape(NA, LEAVES * ROWS, 128)
     coeff_work = pltpu.VMEM((LEAVES * RIGHT_SIDES, RANK), BF16)
 
     def swap(block, axis, distance):
@@ -251,24 +268,30 @@
     first = call(
         first_body, "first",
         [
-            send_shape, shape(RIGHT_SIDES + PARTS * ROWS, packet_width),
-            shape(PEERS, SLOTS, 128), shape(OUTS, dtype=jnp.int32),
+            shape(PEERS, CHUNK + IDS, 128), shape(RIGHT_SIDES + PARTS * ROWS, packet_width),
+            shape(2 * OUTS, dtype=jnp.int32),
         ],
-        [SM] * 3 + [pltpu.HBM] * 5,
+        [pltpu.HBM] * 8,
         [
+            pltpu.SMEM((OUTS,), jnp.int32),
+            pltpu.SMEM((OUTS,), jnp.int32),
+            pltpu.SMEM((OUTS,), jnp.int32),
             pltpu.VMEM((7, panels_here), F32),
             pltpu.VMEM((RIGHT_SIDES, panels_here), BF16),
             pltpu.VMEM((RANK, panels_here), BF16),
             pltpu.VMEM((LEAVES, RANK, RANK), BF16),
             pltpu.VMEM((OUTS, RANK, RANK), BF16),
             coeff_work,
-            pltpu.VMEM((PEERS * SLOTS, 128), F32),
+            pltpu.VMEM((2 * PEERS * NA, 128), F32),
             pltpu.SMEM((NA * PEERS,), jnp.int32),
-            pltpu.SemaphoreType.DMA((8,)),
+            pltpu.SemaphoreType.DMA((11,)),
         ],
-        [VM, VM, VM, SM],
-    )
-    merge = call(merge_body, "merge", [shape(NA, LEAVES * ROWS, 128)], [VM])
+        [VM, VM, SM],
+    )
+    first_merge = call(
+        first_merge_body, "first_merge", [merged_shape, shape(NA, LEAVES * ROWS, 2 * 128)], [VM]
+    )
+    next_merge = call(merge_body, "merge", [merged_shape], [VM] * 2)
     nearby = call(
         near_body, "nearby",
         [shape(RIGHT_SIDES, panels_here, dtype=F32), shape(LEAVES * ROWS, 128, dtype=F32)], [VM] * 8,
@@ -277,14 +300,18 @@
     def together(*arrays):
         return lax.optimization_barrier(arrays)
 
-    def couple(value, send, packet, kernel):
+    def couple(value, send, packet, choice, kernel):
         columns = slice(panels_here, panels_here + RANK)
         arrived = lax.all_to_all(send, ("b", "y"), 0, 0, tiled=True)
         other = swap(packet, "c", 1)
         two = jnp.concatenate([packet[:RIGHT_SIDES, columns], other[:RIGHT_SIDES, columns]], axis=1)
         four = swap(two, "x", 1)
         arrived, four = together(arrived, four)
-        merged, four = together(merge(arrived)[0], four)
+        if choice is None:
+            merged, choice = first_merge(arrived)
+        else:
+            merged = next_merge(arrived, choice)[0]
+        merged, four = together(merged, four)
         received = lax.all_to_all(merged, "a", 0, 0, tiled=True)
         eight = swap(jnp.concatenate([two, four], axis=1), "x", 2)
         if kernel is None:
@@ -293,18 +320,19 @@
                 [pltpu.VMEM((8, panels_here), F32)],
             )(panels, other, near_mask)[0]
         base, spread = nearby(value, other, kernel, two, four, eight, cluster_coupling, leaf_transfer)
-        return received, base, spread, kernel
-
-    send, packet, ids, place = first(
+        return received, base, spread, choice, kernel
+
+    operands = (
         out_leaf, out_wide.reshape(OUTS), out_target, panels, density, source_basis, leaf_transfer, coupling
     )
-    received, base, spread, kernel = couple(density, send, packet, None)
+    send, packet, place = first(*[pltpu.with_memory_space_constraint(array, pltpu.HBM) for array in operands])
+    received, base, spread, choice, kernel = couple(density, send, packet, None, None)
     first_pass, send, packet = call(
-        middle_body, "middle", [values, send_shape, shape(RIGHT_SIDES, packet_width)],
-        [VM, VM, VM, VM, SM, VM, VM, VM, VM], [coeff_work],
-    )(received, spread, base, target_basis, place, ids, source_basis, leaf_transfer, coupling)
-
-    received, base, spread, kernel = couple(first_pass, send, packet, kernel)
+        middle_body, "middle", [values, shape(PEERS, CHUNK, 128), shape(RIGHT_SIDES, packet_width)],
+        [VM, VM, VM, VM, SM, VM, VM, VM], [coeff_work],
+    )(received, spread, base, target_basis, place, source_basis, leaf_transfer, coupling)
+
+    received, base, spread, choice, kernel = couple(first_pass, send, packet, choice, kernel)
     second_pass = call(last_body, "last", [values], [VM] * 4)(received, spread, base, target_basis)[0]
     return (first_pass, second_pass)
 

time: 96 us -> 89.1 us (0.928)
  the two profiles are of different devices: /device:TPU:14 before, /device:TPU:10 now
where the time goes in v4:
time: 89.1 us; the launch traced here: 88.3 us
  starting transfers between devices  48.7 us (55%)
  waiting for transfers between devices  27.2 us (31%)
  Pallas kernels  11.1 us (12%)
    ppermute x6, starting transfers between devices, swap(): return lax.ppermute(block, axis, [(i, i ^ distance) for i in range(count)])  19.9 us
    all_to_all x2, starting transfers between devices, couple(): received = lax.all_to_all(merged, 'a', 0, 0, tiled=True)  18.2 us
    all_to_all x2, waiting for transfers between devices, couple(): received = lax.all_to_all(merged, 'a', 0, 0, tiled=True)  15.8 us
    ppermute x6, waiting for transfers between devices, swap(): return lax.ppermute(block, axis, [(i, i ^ distance) for i in range(count)])  11.4 us
    all_to_all x2, starting transfers between devices, couple(): arrived = lax.all_to_all(send, ('b', 'y'), 0, 0, tiled=True)  10.7 us
    pallas_call x1, Pallas kernels, shards(): first(*[pltpu.with_memory_space_constraint(array, pltpu.HBM) for array in...  3.37 us
    pallas_call x1, Pallas kernels, shards(): call(middle_body, 'middle', [values, shape(PEERS, CHUNK, 128), shape(RIGH...  2.18 us
  transfers between devices with their start and end apart: 10, of which 8 were waited for; matrix products, arithmetic and copies ran while one was open for 1% of the time, Pallas kernels for 3%

profile of v4, /device:TPU:10, one launch (start us, length us, event | category | flops | bytes accessed | tf_op | source)
XLA Modules:
  0.0 88.3 jit_solution(16304380855531833948)
XLA Ops:
  0.6 3.4 %first.1 = (bf16[8,272,128]{2,1,0:T(8,128)(2,1)}, bf16[80,640]{1,0:T(8,128)(2,1)S(1)}, s32[128]{0:T(128)S(1)}) custom-call(s32[64]{0:T(128)} %leaf_hbm.1, s32[64]{0:T(128)} %bitcast.1, s32[64]{0:T(128)} %target_hbm.1, f32[7,512]{1,0:T(8,128)} %own_ref.1, bf16[32,512]{1,0:T(8,128)(2,1)} %value_ref.1, bf16[64,512]{1,0:T(8,128)(2,1)} %basis_ref.1, ...), custom_call_target="tpu_custom_call" | custom-call | tf_op jit(solution)/shard_map/first/pallas_call | solution.py:328
  4.0 6.3 %all-to-all-start = ((bf16[8,272,128]{2,1,0:T(8,128)(2,1)}), bf16[8,272,128]{2,1,0:T(8,128)(2,1)S(1)}, u32[]{:S(2)}, u32[]{:S(2)}) async-start(bf16[8,272,128]{2,1,0:T(8,128)(2,1)} %get-tuple-element.22), calls=%async_computation | async-start | bytes 1114112 | tf_op jit(solution)/shard_map/all_to_all | solution.py:305
  10.3 1.9 %collective-permute-start = (bf16[80,640]{1,0:T(8,128)(2,1)S(1)}, bf16[80,640]{1,0:T(8,128)(2,1)S(1)}, u32[]{:S(2)}, u32[]{:S(2)}) collective-permute-start(bf16[80,640]{1,0:T(8,128)(2,1)S(1)} %get-tuple-element.23), channel_id=1, source_target_pairs={{0,1},{1,0},{2,3},{3,2},{4,5},{5,4},{6,7},{7,6},{8,9},{9,8},{10,11... | collective-permute-start | bytes 307208 | tf_op jit(solution)/shard_map/ppermute | solution.py:266
  12.2 1.3 %collective-permute-done.packet_ref.other_ref = bf16[80,640]{1,0:T(8,128)(2,1)S(1)} collective-permute-done((bf16[80,640]{1,0:T(8,128)(2,1)S(1)}, bf16[80,640]{1,0:T(8,128)(2,1)S(1)}, u32[]{:S(2)}, u32[]{:S(2)}) %collective-permute-start) | collective-permute-done | bytes 102432 | tf_op jit(solution)/shard_map/ppermute | solution.py:266
  13.5 0.1 pad_maximum_fusion.2.two_ref
  13.6 5.4 %collective-permute-start.1 = (bf16[32,128]{1,0:T(8,128)(2,1)S(1)}, bf16[32,128]{1,0:T(8,128)(2,1)S(1)}, u32[]{:S(2)}, u32[]{:S(2)}) collective-permute-start(bf16[32,128]{1,0:T(8,128)(2,1)S(1)} %pad_maximum_fusion.2.two_ref), channel_id=1, source_target_pairs={{0,2},{2,0},{4,6},{6,4},{1,3},{3,1},{5,7},{7,5},{8,10},{10,8},{12,... | collective-permute-start | bytes 24584 | tf_op jit(solution)/shard_map/ppermute | solution.py:266
  19.0 1.6 %collective-permute-done.1.four_ref = bf16[32,128]{1,0:T(8,128)(2,1)S(1)} collective-permute-done((bf16[32,128]{1,0:T(8,128)(2,1)S(1)}, bf16[32,128]{1,0:T(8,128)(2,1)S(1)}, u32[]{:S(2)}, u32[]{:S(2)}) %collective-permute-start.1) | collective-permute-done | bytes 8224 | tf_op jit(solution)/shard_map/ppermute | solution.py:266
  20.6 0.9 first_merge.1
  21.5 12.8 %all-to-all-start.1 = ((bf16[8,64,128]{2,1,0:T(8,128)(2,1)}), bf16[8,64,128]{2,1,0:T(8,128)(2,1)S(1)}, u32[]{:S(2)}, u32[]{:S(2)}) async-start(bf16[8,64,128]{2,1,0:T(8,128)(2,1)} %get-tuple-element.27), calls=%async_computation.1 | async-start | bytes 262144 | tf_op jit(solution)/shard_map/all_to_all | solution.py:315
  34.3 0.1 pad_maximum_fusion
  34.4 4.2 %collective-permute-start.2 = (bf16[32,256]{1,0:T(8,128)(2,1)S(1)}, bf16[32,256]{1,0:T(8,128)(2,1)S(1)}, u32[]{:S(2)}, u32[]{:S(2)}) collective-permute-start(bf16[32,256]{1,0:T(8,128)(2,1)S(1)} %pad_maximum_fusion), channel_id=1, source_target_pairs={{0,4},{2,6},{4,0},{6,2},{1,5},{3,7},{5,1},{7,3},{8,12},{10,14},{12... | collective-permute-start | bytes 49160 | tf_op jit(solution)/shard_map/ppermute | solution.py:266
  38.6 0.1 copy.13.rows_ref
  38.7 0.0 copy-start.1
  38.7 1.7 %kernel.1.kernel_ref = bf16[512,1024]{1,0:T(8,128)(2,1)S(1)} custom-call(f32[7,512]{1,0:T(8,128)S(1)} %copy-done.5, bf16[80,640]{1,0:T(8,128)(2,1)S(1)} %collective-permute-done.packet_ref.other_ref, s32[4,8]{1,0:T(4,128)S(1)} %copy-done.7), custom_call_target="tpu_custom_call" | custom-call | tf_op jit(solution)/shard_map/kernel/pallas_call | solution.py:318
  40.5 1.1 %collective-permute-done.2.eight_ref = bf16[32,256]{1,0:T(8,128)(2,1)S(1)} collective-permute-done((bf16[32,256]{1,0:T(8,128)(2,1)S(1)}, bf16[32,256]{1,0:T(8,128)(2,1)S(1)}, u32[]{:S(2)}, u32[]{:S(2)}) %collective-permute-start.2) | collective-permute-done | bytes 16416 | tf_op jit(solution)/shard_map/ppermute | solution.py:266
  41.7 0.6 nearby.2
  42.3 8.0 %all-to-all-done.1.recv_ref = bf16[8,64,128]{2,1,0:T(8,128)(2,1)S(1)} async-done(((bf16[8,64,128]{2,1,0:T(8,128)(2,1)}), bf16[8,64,128]{2,1,0:T(8,128)(2,1)S(1)}, u32[]{:S(2)}, u32[]{:S(2)}) %all-to-all-start.1) | async-done | bytes 131104 | tf_op jit(solution)/shard_map/all_to_all | solution.py:315
  50.3 2.2 %middle.1 = (bf16[32,512]{1,0:T(8,128)(2,1)}, bf16[8,256,128]{2,1,0:T(8,128)(2,1)}, bf16[32,640]{1,0:T(8,128)(2,1)S(1)}) custom-call(bf16[8,64,128]{2,1,0:T(8,128)(2,1)S(1)} %all-to-all-done.1.recv_ref, f32[64,128]{1,0:T(8,128)S(1)} %get-tuple-element.29.spread_ref, f32[32,512]{1,0:T(8,128)S(1)} %get-tuple-element.30.base_ref, ...), custom_call_target="tpu_custom_call" | custom-call | tf_op jit(solution)/shard_map/middle/pallas_call | solution.py:330
  52.5 4.4 %all-to-all-start.2 = ((bf16[8,256,128]{2,1,0:T(8,128)(2,1)}), bf16[8,256,128]{2,1,0:T(8,128)(2,1)S(1)}, u32[]{:S(2)}, u32[]{:S(2)}) async-start(bf16[8,256,128]{2,1,0:T(8,128)(2,1)} %get-tuple-element.33), calls=%async_computation.2 | async-start | bytes 1048576 | tf_op jit(solution)/shard_map/all_to_all | solution.py:305
  56.9 1.9 %collective-permute-start.3 = (bf16[32,640]{1,0:T(8,128)(2,1)S(1)}, bf16[32,640]{1,0:T(8,128)(2,1)S(1)}, u32[]{:S(2)}, u32[]{:S(2)}) collective-permute-start(bf16[32,640]{1,0:T(8,128)(2,1)S(1)} %get-tuple-element.34), channel_id=1, source_target_pairs={{0,1},{1,0},{2,3},{3,2},{4,5},{5,4},{6,7},{7,6},{8,9},{9,8},{10,11... | collective-permute-start | bytes 122888 | tf_op jit(solution)/shard_map/ppermute | solution.py:266
  58.8 1.2 %collective-permute-done.3.other_ref = bf16[32,640]{1,0:T(8,128)(2,1)S(1)} collective-permute-done((bf16[32,640]{1,0:T(8,128)(2,1)S(1)}, bf16[32,640]{1,0:T(8,128)(2,1)S(1)}, u32[]{:S(2)}, u32[]{:S(2)}) %collective-permute-start.3) | collective-permute-done | bytes 40992 | tf_op jit(solution)/shard_map/ppermute | solution.py:266
  60.0 0.1 pad_maximum_fusion.3.two_ref
  60.1 2.4 %collective-permute-start.4 = (bf16[32,128]{1,0:T(8,128)(2,1)S(1)}, bf16[32,128]{1,0:T(8,128)(2,1)S(1)}, u32[]{:S(2)}, u32[]{:S(2)}) collective-permute-start(bf16[32,128]{1,0:T(8,128)(2,1)S(1)} %pad_maximum_fusion.3.two_ref), channel_id=1, source_target_pairs={{0,2},{2,0},{4,6},{6,4},{1,3},{3,1},{5,7},{7,5},{8,10},{10,8},{12,... | collective-permute-start | bytes 24584 | tf_op jit(solution)/shard_map/ppermute | solution.py:266
  62.5 3.1 %collective-permute-done.4.four_ref = bf16[32,128]{1,0:T(8,128)(2,1)S(1)} collective-permute-done((bf16[32,128]{1,0:T(8,128)(2,1)S(1)}, bf16[32,128]{1,0:T(8,128)(2,1)S(1)}, u32[]{:S(2)}, u32[]{:S(2)}) %collective-permute-start.4) | collective-permute-done | bytes 8224 | tf_op jit(solution)/shard_map/ppermute | solution.py:266
  65.6 0.9 merge.1
  66.5 5.4 %all-to-all-start.3 = ((bf16[8,64,128]{2,1,0:T(8,128)(2,1)}), bf16[8,64,128]{2,1,0:T(8,128)(2,1)S(1)}, u32[]{:S(2)}, u32[]{:S(2)}) async-start(bf16[8,64,128]{2,1,0:T(8,128)(2,1)} %merge.1), calls=%async_computation.3 | async-start | bytes 262144 | tf_op jit(solution)/shard_map/all_to_all | solution.py:315
  71.9 0.1 pad_maximum_fusion.1
  71.9 4.0 %collective-permute-start.5 = (bf16[32,256]{1,0:T(8,128)(2,1)S(1)}, bf16[32,256]{1,0:T(8,128)(2,1)S(1)}, u32[]{:S(2)}, u32[]{:S(2)}) collective-permute-start(bf16[32,256]{1,0:T(8,128)(2,1)S(1)} %pad_maximum_fusion.1), channel_id=1, source_target_pairs={{0,4},{2,6},{4,0},{6,2},{1,5},{3,7},{5,1},{7,3},{8,12},{10,14},{12... | collective-permute-start | bytes 49160 | tf_op jit(solution)/shard_map/ppermute | solution.py:266
  76.0 3.1 %collective-permute-done.5.eight_ref = bf16[32,256]{1,0:T(8,128)(2,1)S(1)} collective-permute-done((bf16[32,256]{1,0:T(8,128)(2,1)S(1)}, bf16[32,256]{1,0:T(8,128)(2,1)S(1)}, u32[]{:S(2)}, u32[]{:S(2)}) %collective-permute-start.5) | collective-permute-done | bytes 16416 | tf_op jit(solution)/shard_map/ppermute | solution.py:266
  79.1 0.6 nearby.3
  79.7 7.8 %all-to-all-done.3.recv_ref = bf16[8,64,128]{2,1,0:T(8,128)(2,1)S(1)} async-done(((bf16[8,64,128]{2,1,0:T(8,128)(2,1)}), bf16[8,64,128]{2,1,0:T(8,128)(2,1)S(1)}, u32[]{:S(2)}, u32[]{:S(2)}) %all-to-all-start.3) | async-done | bytes 131104 | tf_op jit(solution)/shard_map/all_to_all | solution.py:315
  87.5 0.8 last.1
  (23 shorter events, 0.1 us)
Async XLA Ops:
  4.0 16.6 %all-to-all-start = ((bf16[8,272,128]{2,1,0:T(8,128)(2,1)}), bf16[8,272,128]{2,1,0:T(8,128)(2,1)S(1)}, u32[]{:S(2)}, u32[]{:S(2)}) async-start(bf16[8,272,128]{2,1,0:T(8,128)(2,1)} %get-tuple-element.22), calls=%async_computation | async-start | bytes 1114112 | tf_op jit(solution)/shard_map/all_to_all | solution.py:305
  10.3 3.2 %collective-permute-start = (bf16[80,640]{1,0:T(8,128)(2,1)S(1)}, bf16[80,640]{1,0:T(8,128)(2,1)S(1)}, u32[]{:S(2)}, u32[]{:S(2)}) collective-permute-start(bf16[80,640]{1,0:T(8,128)(2,1)S(1)} %get-tuple-element.23), channel_id=1, source_target_pairs={{0,1},{1,0},{2,3},{3,2},{4,5},{5,4},{6,7},{7,6},{8,9},{9,8},{10,11... | collective-permute-start | bytes 307208 | tf_op jit(solution)/shard_map/ppermute | solution.py:266
  13.6 7.0 %collective-permute-start.1 = (bf16[32,128]{1,0:T(8,128)(2,1)S(1)}, bf16[32,128]{1,0:T(8,128)(2,1)S(1)}, u32[]{:S(2)}, u32[]{:S(2)}) collective-permute-start(bf16[32,128]{1,0:T(8,128)(2,1)S(1)} %pad_maximum_fusion.2.two_ref), channel_id=1, source_target_pairs={{0,2},{2,0},{4,6},{6,4},{1,3},{3,1},{5,7},{7,5},{8,10},{10,8},{12,... | collective-permute-start | bytes 24584 | tf_op jit(solution)/shard_map/ppermute | solution.py:266
  21.5 17.1 %copy-start.8 = (bf16[1,512,64]{1,2,0:T(8,128)(2,1)S(1)}, bf16[1,512,64]{1,2,0:T(8,128)(2,1)}, u32[]{:S(2)}) copy-start(bf16[1,512,64]{1,2,0:T(8,128)(2,1)} %param.16) | copy-start | bytes 196612
  21.5 28.8 %all-to-all-start.1 = ((bf16[8,64,128]{2,1,0:T(8,128)(2,1)}), bf16[8,64,128]{2,1,0:T(8,128)(2,1)S(1)}, u32[]{:S(2)}, u32[]{:S(2)}) async-start(bf16[8,64,128]{2,1,0:T(8,128)(2,1)} %get-tuple-element.27), calls=%async_computation.1 | async-start | bytes 262144 | tf_op jit(solution)/shard_map/all_to_all | solution.py:315
  34.4 4.3 %copy-start.5 = (f32[7,512]{1,0:T(8,128)S(1)}, f32[7,512]{1,0:T(8,128)}, u32[]{:S(2)}) copy-start(f32[7,512]{1,0:T(8,128)} %own_ref.1) | copy-start | bytes 43012
  34.4 4.3 %copy-start.7 = (s32[4,8]{1,0:T(4,128)S(1)}, s32[4,8]{1,0:T(4,128)}, u32[]{:S(2)}) copy-start(s32[4,8]{1,0:T(4,128)} %mask_ref.1) | copy-start | bytes 388
  34.4 7.3 %collective-permute-start.2 = (bf16[32,256]{1,0:T(8,128)(2,1)S(1)}, bf16[32,256]{1,0:T(8,128)(2,1)S(1)}, u32[]{:S(2)}, u32[]{:S(2)}) collective-permute-start(bf16[32,256]{1,0:T(8,128)(2,1)S(1)} %pad_maximum_fusion), channel_id=1, source_target_pairs={{0,4},{2,6},{4,0},{6,2},{1,5},{3,7},{5,1},{7,3},{8,12},{10,14},{12... | collective-permute-start | bytes 49160 | tf_op jit(solution)/shard_map/ppermute | solution.py:266
  38.7 2.9 %copy-start.1 = (bf16[4,64,64]{2,1,0:T(8,128)(2,1)S(1)}, bf16[4,64,64]{2,1,0:T(8,128)(2,1)}, u32[]{:S(2)}) copy-start(bf16[4,64,64]{2,1,0:T(8,128)(2,1)} %transfer_ref.5) | copy-start | bytes 98308
  38.7 2.9 %copy-start.4 = (bf16[32,512]{1,0:T(8,128)(2,1)S(1)}, bf16[32,512]{1,0:T(8,128)(2,1)}, u32[]{:S(2)}) copy-start(bf16[32,512]{1,0:T(8,128)(2,1)} %value_ref.1) | copy-start | bytes 98308
  38.7 11.5 %copy-start = (bf16[64,64,64]{2,1,0:T(8,128)(2,1)S(1)}, bf16[64,64,64]{2,1,0:T(8,128)(2,1)}, u32[]{:S(2)}) copy-start(bf16[64,64,64]{2,1,0:T(8,128)(2,1)} %coupling_ref.1) | copy-start | bytes 1572868
  40.5 9.8 %copy-start.2 = (bf16[64,512]{1,0:T(8,128)(2,1)S(1)}, bf16[64,512]{1,0:T(8,128)(2,1)}, u32[]{:S(2)}) copy-start(bf16[64,512]{1,0:T(8,128)(2,1)} %target_ref.3) | copy-start | bytes 196612
  40.5 9.8 %copy-start.3 = (bf16[64,512]{1,0:T(8,128)(2,1)S(1)}, bf16[64,512]{1,0:T(8,128)(2,1)}, u32[]{:S(2)}) copy-start(bf16[64,512]{1,0:T(8,128)(2,1)} %basis_ref.1) | copy-start | bytes 196612
  52.5 13.2 %all-to-all-start.2 = ((bf16[8,256,128]{2,1,0:T(8,128)(2,1)}), bf16[8,256,128]{2,1,0:T(8,128)(2,1)S(1)}, u32[]{:S(2)}, u32[]{:S(2)}) async-start(bf16[8,256,128]{2,1,0:T(8,128)(2,1)} %get-tuple-element.33), calls=%async_computation.2 | async-start | bytes 1048576 | tf_op jit(solution)/shard_map/all_to_all | solution.py:305
  56.9 3.1 %collective-permute-start.3 = (bf16[32,640]{1,0:T(8,128)(2,1)S(1)}, bf16[32,640]{1,0:T(8,128)(2,1)S(1)}, u32[]{:S(2)}, u32[]{:S(2)}) collective-permute-start(bf16[32,640]{1,0:T(8,128)(2,1)S(1)} %get-tuple-element.34), channel_id=1, source_target_pairs={{0,1},{1,0},{2,3},{3,2},{4,5},{5,4},{6,7},{7,6},{8,9},{9,8},{10,11... | collective-permute-start | bytes 122888 | tf_op jit(solution)/shard_map/ppermute | solution.py:266
  60.1 5.5 %collective-permute-start.4 = (bf16[32,128]{1,0:T(8,128)(2,1)S(1)}, bf16[32,128]{1,0:T(8,128)(2,1)S(1)}, u32[]{:S(2)}, u32[]{:S(2)}) collective-permute-start(bf16[32,128]{1,0:T(8,128)(2,1)S(1)} %pad_maximum_fusion.3.two_ref), channel_id=1, source_target_pairs={{0,2},{2,0},{4,6},{6,4},{1,3},{3,1},{5,7},{7,5},{8,10},{10,8},{12,... | collective-permute-start | bytes 24584 | tf_op jit(solution)/shard_map/ppermute | solution.py:266
  66.5 21.0 %all-to-all-start.3 = ((bf16[8,64,128]{2,1,0:T(8,128)(2,1)}), bf16[8,64,128]{2,1,0:T(8,128)(2,1)S(1)}, u32[]{:S(2)}, u32[]{:S(2)}) async-start(bf16[8,64,128]{2,1,0:T(8,128)(2,1)} %merge.1), calls=%async_computation.3 | async-start | bytes 262144 | tf_op jit(solution)/shard_map/all_to_all | solution.py:315
  71.9 7.2 %copy-start.6 = (bf16[32,512]{1,0:T(8,128)(2,1)S(1)}, bf16[32,512]{1,0:T(8,128)(2,1)}, u32[]{:S(2)}) copy-start(bf16[32,512]{1,0:T(8,128)(2,1)} %get-tuple-element.20.value_ref) | copy-start | bytes 98308
  71.9 7.1 %collective-permute-start.5 = (bf16[32,256]{1,0:T(8,128)(2,1)S(1)}, bf16[32,256]{1,0:T(8,128)(2,1)S(1)}, u32[]{:S(2)}, u32[]{:S(2)}) collective-permute-start(bf16[32,256]{1,0:T(8,128)(2,1)S(1)} %pad_maximum_fusion.1), channel_id=1, source_target_pairs={{0,4},{2,6},{4,0},{6,2},{1,5},{3,7},{5,1},{7,3},{8,12},{10,14},{12... | collective-permute-start | bytes 49160 | tf_op jit(solution)/shard_map/ppermute | solution.py:266

commit v5 on v4

--- a/solution.py
+++ b/solution.py
@@ -20,6 +20,8 @@
 ROWS = 16
 CHUNK = SLOTS * ROWS
 IDS = 16
+FIRST_PAIR = 5
+ORDER = [(FIRST_PAIR + i) % NA for i in range(NA)]
 PARTS = 3
 F32, BF16 = jnp.float32, jnp.bfloat16
 NT = (((1,), (1,)), ((), ()))
@@ -139,9 +141,9 @@
 
 
 def merge(recv_ref, choice_ref, out_ref):
-    for pair in range(NA):
+    for place, pair in enumerate(ORDER):
         blocks = [recv_ref[src, pair * 2 * ROWS : (pair + 1) * 2 * ROWS, :] for src in range(PEERS)]
-        out_ref[pair] = dot(choice_ref[pair], jnp.concatenate(blocks, axis=0)).astype(BF16)
+        out_ref[place] = dot(choice_ref[pair], jnp.concatenate(blocks, axis=0)).astype(BF16)
 
 
 def first_merge_body(recv_ref, out_ref, choice_ref):
@@ -312,7 +314,7 @@
         else:
             merged = next_merge(arrived, choice)[0]
         merged, four = together(merged, four)
-        received = lax.all_to_all(merged, "a", 0, 0, tiled=True)
+        received = lax.all_to_all(merged, "a", 0, 0, axis_index_groups=[ORDER], tiled=True)
         eight = swap(jnp.concatenate([two, four], axis=1), "x", 2)
         if kernel is None:
             kernel = call(

time: 89.1 us -> 82.8 us (0.929)
  the two profiles are of different devices: /device:TPU:10 before, /device:TPU:14 now
where the time goes in v5:
time: 82.8 us; the launch traced here: 82 us
  starting transfers between devices  55.8 us (67%)
  waiting for transfers between devices  13.7 us (17%)
  Pallas kernels  11.1 us (13%)
    all_to_all x2, starting transfers between devices, couple(): lax.all_to_all(merged, 'a', 0, 0, axis_index_groups=[ORDER], tiled=True)  27.8 us
    ppermute x6, starting transfers between devices, swap(): return lax.ppermute(block, axis, [(i, i ^ distance) for i in range(count)])  16 us
    ppermute x6, waiting for transfers between devices, swap(): return lax.ppermute(block, axis, [(i, i ^ distance) for i in range(count)])  13.7 us
    all_to_all x2, starting transfers between devices, couple(): arrived = lax.all_to_all(send, ('b', 'y'), 0, 0, tiled=True)  12 us
    pallas_call x1, Pallas kernels, shards(): first(*[pltpu.with_memory_space_constraint(array, pltpu.HBM) for array in...  3.37 us
    pallas_call x1, Pallas kernels, shards(): call(middle_body, 'middle', [values, shape(PEERS, CHUNK, 128), shape(RIGH...  2.18 us
    pallas_call x1, Pallas kernels, couple(): call(kernel_body, 'kernel', [shape(panels_here, 2 * panels_here)], [VM, V...  1.73 us
  transfers between devices with their start and end apart: 10, of which 6 were waited for; matrix products, arithmetic and copies ran while one was open for 1% of the time, Pallas kernels for 4%

profile of v5, /device:TPU:14, one launch (start us, length us, event | category | flops | bytes accessed | tf_op | source)
XLA Modules:
  0.0 82.0 jit_solution(13522406480752184648)
XLA Ops:
  0.6 3.4 %first.1 = (bf16[8,272,128]{2,1,0:T(8,128)(2,1)}, bf16[80,640]{1,0:T(8,128)(2,1)S(1)}, s32[128]{0:T(128)S(1)}) custom-call(s32[64]{0:T(128)} %leaf_hbm.1, s32[64]{0:T(128)} %bitcast.1, s32[64]{0:T(128)} %target_hbm.1, f32[7,512]{1,0:T(8,128)} %own_ref.1, bf16[32,512]{1,0:T(8,128)(2,1)} %value_ref.1, bf16[64,512]{1,0:T(8,128)(2,1)} %basis_ref.1, ...), custom_call_target="tpu_custom_call" | custom-call | tf_op jit(solution)/shard_map/first/pallas_call | solution.py:330
  4.0 6.3 %all-to-all-start = ((bf16[8,272,128]{2,1,0:T(8,128)(2,1)}), bf16[8,272,128]{2,1,0:T(8,128)(2,1)S(1)}, u32[]{:S(2)}, u32[]{:S(2)}) async-start(bf16[8,272,128]{2,1,0:T(8,128)(2,1)} %get-tuple-element.22), calls=%async_computation | async-start | bytes 1114112 | tf_op jit(solution)/shard_map/all_to_all | solution.py:307
  10.3 1.9 %collective-permute-start = (bf16[80,640]{1,0:T(8,128)(2,1)S(1)}, bf16[80,640]{1,0:T(8,128)(2,1)S(1)}, u32[]{:S(2)}, u32[]{:S(2)}) collective-permute-start(bf16[80,640]{1,0:T(8,128)(2,1)S(1)} %get-tuple-element.23), channel_id=1, source_target_pairs={{0,1},{1,0},{2,3},{3,2},{4,5},{5,4},{6,7},{7,6},{8,9},{9,8},{10,11... | collective-permute-start | bytes 307208 | tf_op jit(solution)/shard_map/ppermute | solution.py:268
  12.2 1.3 %collective-permute-done.packet_ref.other_ref = bf16[80,640]{1,0:T(8,128)(2,1)S(1)} collective-permute-done((bf16[80,640]{1,0:T(8,128)(2,1)S(1)}, bf16[80,640]{1,0:T(8,128)(2,1)S(1)}, u32[]{:S(2)}, u32[]{:S(2)}) %collective-permute-start) | collective-permute-done | bytes 102432 | tf_op jit(solution)/shard_map/ppermute | solution.py:268
  13.5 0.1 pad_maximum_fusion.2.two_ref
  13.6 2.7 %collective-permute-start.1 = (bf16[32,128]{1,0:T(8,128)(2,1)S(1)}, bf16[32,128]{1,0:T(8,128)(2,1)S(1)}, u32[]{:S(2)}, u32[]{:S(2)}) collective-permute-start(bf16[32,128]{1,0:T(8,128)(2,1)S(1)} %pad_maximum_fusion.2.two_ref), channel_id=1, source_target_pairs={{0,2},{2,0},{4,6},{6,4},{1,3},{3,1},{5,7},{7,5},{8,10},{10,8},{12,... | collective-permute-start | bytes 24584 | tf_op jit(solution)/shard_map/ppermute | solution.py:268
  16.3 2.8 %collective-permute-done.1.four_ref = bf16[32,128]{1,0:T(8,128)(2,1)S(1)} collective-permute-done((bf16[32,128]{1,0:T(8,128)(2,1)S(1)}, bf16[32,128]{1,0:T(8,128)(2,1)S(1)}, u32[]{:S(2)}, u32[]{:S(2)}) %collective-permute-start.1) | collective-permute-done | bytes 8224 | tf_op jit(solution)/shard_map/ppermute | solution.py:268
  19.1 0.9 %first_merge.1 = (bf16[8,64,128]{2,1,0:T(8,128)(2,1)}, bf16[8,64,256]{2,1,0:T(8,128)(2,1)S(1)}) custom-call(bf16[8,272,128]{2,1,0:T(8,128)(2,1)S(1)} %all-to-all-done.recv_ref), custom_call_target="tpu_custom_call" | custom-call | tf_op jit(solution)/shard_map/first_merge/pallas_call | solution.py:313
  20.0 15.8 %all-to-all-start.1 = ((bf16[8,64,128]{2,1,0:T(8,128)(2,1)}), bf16[8,64,128]{2,1,0:T(8,128)(2,1)S(1)}, u32[]{:S(2)}, u32[]{:S(2)}) async-start(bf16[8,64,128]{2,1,0:T(8,128)(2,1)} %get-tuple-element.27), calls=%async_computation.1 | async-start | bytes 262144 | tf_op jit(solution)/shard_map/all_to_all | solution.py:317
  35.8 0.1 pad_maximum_fusion
  35.9 3.4 %collective-permute-start.2 = (bf16[32,256]{1,0:T(8,128)(2,1)S(1)}, bf16[32,256]{1,0:T(8,128)(2,1)S(1)}, u32[]{:S(2)}, u32[]{:S(2)}) collective-permute-start(bf16[32,256]{1,0:T(8,128)(2,1)S(1)} %pad_maximum_fusion), channel_id=1, source_target_pairs={{0,4},{2,6},{4,0},{6,2},{1,5},{3,7},{5,1},{7,3},{8,12},{10,14},{12... | collective-permute-start | bytes 49160 | tf_op jit(solution)/shard_map/ppermute | solution.py:268
  39.3 0.1 copy.13.rows_ref
  39.5 0.0 copy-start.1
  39.5 0.0 copy-start.4
  39.5 1.7 %kernel.1.kernel_ref = bf16[512,1024]{1,0:T(8,128)(2,1)S(1)} custom-call(f32[7,512]{1,0:T(8,128)S(1)} %copy-done.5, bf16[80,640]{1,0:T(8,128)(2,1)S(1)} %collective-permute-done.packet_ref.other_ref, s32[4,8]{1,0:T(4,128)S(1)} %copy-done.7), custom_call_target="tpu_custom_call" | custom-call | tf_op jit(solution)/shard_map/kernel/pallas_call | solution.py:320
  41.3 1.9 %collective-permute-done.2.eight_ref = bf16[32,256]{1,0:T(8,128)(2,1)S(1)} collective-permute-done((bf16[32,256]{1,0:T(8,128)(2,1)S(1)}, bf16[32,256]{1,0:T(8,128)(2,1)S(1)}, u32[]{:S(2)}, u32[]{:S(2)}) %collective-permute-start.2) | collective-permute-done | bytes 16416 | tf_op jit(solution)/shard_map/ppermute | solution.py:268
  43.1 0.6 nearby.2
  43.8 0.0 copy-done.2
  43.8 2.2 %middle.1 = (bf16[32,512]{1,0:T(8,128)(2,1)}, bf16[8,256,128]{2,1,0:T(8,128)(2,1)}, bf16[32,640]{1,0:T(8,128)(2,1)S(1)}) custom-call(bf16[8,64,128]{2,1,0:T(8,128)(2,1)S(1)} %all-to-all-done.1.recv_ref, f32[64,128]{1,0:T(8,128)S(1)} %get-tuple-element.29.spread_ref, f32[32,512]{1,0:T(8,128)S(1)} %get-tuple-element.30.base_ref, ...), custom_call_target="tpu_custom_call" | custom-call | tf_op jit(solution)/shard_map/middle/pallas_call | solution.py:332
  46.0 5.7 %all-to-all-start.2 = ((bf16[8,256,128]{2,1,0:T(8,128)(2,1)}), bf16[8,256,128]{2,1,0:T(8,128)(2,1)S(1)}, u32[]{:S(2)}, u32[]{:S(2)}) async-start(bf16[8,256,128]{2,1,0:T(8,128)(2,1)} %get-tuple-element.33), calls=%async_computation.2 | async-start | bytes 1048576 | tf_op jit(solution)/shard_map/all_to_all | solution.py:307
  51.7 1.9 %collective-permute-start.3 = (bf16[32,640]{1,0:T(8,128)(2,1)S(1)}, bf16[32,640]{1,0:T(8,128)(2,1)S(1)}, u32[]{:S(2)}, u32[]{:S(2)}) collective-permute-start(bf16[32,640]{1,0:T(8,128)(2,1)S(1)} %get-tuple-element.34), channel_id=1, source_target_pairs={{0,1},{1,0},{2,3},{3,2},{4,5},{5,4},{6,7},{7,6},{8,9},{9,8},{10,11... | collective-permute-start | bytes 122888 | tf_op jit(solution)/shard_map/ppermute | solution.py:268
  53.7 1.2 %collective-permute-done.3.other_ref = bf16[32,640]{1,0:T(8,128)(2,1)S(1)} collective-permute-done((bf16[32,640]{1,0:T(8,128)(2,1)S(1)}, bf16[32,640]{1,0:T(8,128)(2,1)S(1)}, u32[]{:S(2)}, u32[]{:S(2)}) %collective-permute-start.3) | collective-permute-done | bytes 40992 | tf_op jit(solution)/shard_map/ppermute | solution.py:268
  54.8 0.1 pad_maximum_fusion.3.two_ref
  54.9 2.7 %collective-permute-start.4 = (bf16[32,128]{1,0:T(8,128)(2,1)S(1)}, bf16[32,128]{1,0:T(8,128)(2,1)S(1)}, u32[]{:S(2)}, u32[]{:S(2)}) collective-permute-start(bf16[32,128]{1,0:T(8,128)(2,1)S(1)} %pad_maximum_fusion.3.two_ref), channel_id=1, source_target_pairs={{0,2},{2,0},{4,6},{6,4},{1,3},{3,1},{5,7},{7,5},{8,10},{10,8},{12,... | collective-permute-start | bytes 24584 | tf_op jit(solution)/shard_map/ppermute | solution.py:268
  57.6 2.8 %collective-permute-done.4.four_ref = bf16[32,128]{1,0:T(8,128)(2,1)S(1)} collective-permute-done((bf16[32,128]{1,0:T(8,128)(2,1)S(1)}, bf16[32,128]{1,0:T(8,128)(2,1)S(1)}, u32[]{:S(2)}, u32[]{:S(2)}) %collective-permute-start.4) | collective-permute-done | bytes 8224 | tf_op jit(solution)/shard_map/ppermute | solution.py:268
  60.5 0.9 %merge.1 = bf16[8,64,128]{2,1,0:T(8,128)(2,1)} custom-call(bf16[8,256,128]{2,1,0:T(8,128)(2,1)S(1)} %all-to-all-done.2.recv_ref, bf16[8,64,256]{2,1,0:T(8,128)(2,1)S(1)} %get-tuple-element.36.choice_ref), custom_call_target="tpu_custom_call" | custom-call | tf_op jit(solution)/shard_map/merge/pallas_call | solution.py:315
  61.3 12.0 %all-to-all-start.3 = ((bf16[8,64,128]{2,1,0:T(8,128)(2,1)}), bf16[8,64,128]{2,1,0:T(8,128)(2,1)S(1)}, u32[]{:S(2)}, u32[]{:S(2)}) async-start(bf16[8,64,128]{2,1,0:T(8,128)(2,1)} %merge.1), calls=%async_computation.3 | async-start | bytes 262144 | tf_op jit(solution)/shard_map/all_to_all | solution.py:317
  73.3 0.1 pad_maximum_fusion.1
  73.4 3.3 %collective-permute-start.5 = (bf16[32,256]{1,0:T(8,128)(2,1)S(1)}, bf16[32,256]{1,0:T(8,128)(2,1)S(1)}, u32[]{:S(2)}, u32[]{:S(2)}) collective-permute-start(bf16[32,256]{1,0:T(8,128)(2,1)S(1)} %pad_maximum_fusion.1), channel_id=1, source_target_pairs={{0,4},{2,6},{4,0},{6,2},{1,5},{3,7},{5,1},{7,3},{8,12},{10,14},{12... | collective-permute-start | bytes 49160 | tf_op jit(solution)/shard_map/ppermute | solution.py:268
  76.7 3.8 %collective-permute-done.5.eight_ref = bf16[32,256]{1,0:T(8,128)(2,1)S(1)} collective-permute-done((bf16[32,256]{1,0:T(8,128)(2,1)S(1)}, bf16[32,256]{1,0:T(8,128)(2,1)S(1)}, u32[]{:S(2)}, u32[]{:S(2)}) %collective-permute-start.5) | collective-permute-done | bytes 16416 | tf_op jit(solution)/shard_map/ppermute | solution.py:268
  80.6 0.6 nearby.3
  81.2 0.8 last.1
  (23 shorter events, 0.1 us)
Async XLA Ops:
  4.0 15.1 %all-to-all-start = ((bf16[8,272,128]{2,1,0:T(8,128)(2,1)}), bf16[8,272,128]{2,1,0:T(8,128)(2,1)S(1)}, u32[]{:S(2)}, u32[]{:S(2)}) async-start(bf16[8,272,128]{2,1,0:T(8,128)(2,1)} %get-tuple-element.22), calls=%async_computation | async-start | bytes 1114112 | tf_op jit(solution)/shard_map/all_to_all | solution.py:307
  10.3 3.2 %collective-permute-start = (bf16[80,640]{1,0:T(8,128)(2,1)S(1)}, bf16[80,640]{1,0:T(8,128)(2,1)S(1)}, u32[]{:S(2)}, u32[]{:S(2)}) collective-permute-start(bf16[80,640]{1,0:T(8,128)(2,1)S(1)} %get-tuple-element.23), channel_id=1, source_target_pairs={{0,1},{1,0},{2,3},{3,2},{4,5},{5,4},{6,7},{7,6},{8,9},{9,8},{10,11... | collective-permute-start | bytes 307208 | tf_op jit(solution)/shard_map/ppermute | solution.py:268
  13.6 5.5 %collective-permute-start.1 = (bf16[32,128]{1,0:T(8,128)(2,1)S(1)}, bf16[32,128]{1,0:T(8,128)(2,1)S(1)}, u32[]{:S(2)}, u32[]{:S(2)}) collective-permute-start(bf16[32,128]{1,0:T(8,128)(2,1)S(1)} %pad_maximum_fusion.2.two_ref), channel_id=1, source_target_pairs={{0,2},{2,0},{4,6},{6,4},{1,3},{3,1},{5,7},{7,5},{8,10},{10,8},{12,... | collective-permute-start | bytes 24584 | tf_op jit(solution)/shard_map/ppermute | solution.py:268
  20.0 19.3 %copy-start.8 = (bf16[1,512,64]{1,2,0:T(8,128)(2,1)S(1)}, bf16[1,512,64]{1,2,0:T(8,128)(2,1)}, u32[]{:S(2)}) copy-start(bf16[1,512,64]{1,2,0:T(8,128)(2,1)} %param.16) | copy-start | bytes 196612
  20.0 23.8 %all-to-all-start.1 = ((bf16[8,64,128]{2,1,0:T(8,128)(2,1)}), bf16[8,64,128]{2,1,0:T(8,128)(2,1)S(1)}, u32[]{:S(2)}, u32[]{:S(2)}) async-start(bf16[8,64,128]{2,1,0:T(8,128)(2,1)} %get-tuple-element.27), calls=%async_computation.1 | async-start | bytes 262144 | tf_op jit(solution)/shard_map/all_to_all | solution.py:317
  35.9 3.6 %copy-start.5 = (f32[7,512]{1,0:T(8,128)S(1)}, f32[7,512]{1,0:T(8,128)}, u32[]{:S(2)}) copy-start(f32[7,512]{1,0:T(8,128)} %own_ref.1) | copy-start | bytes 43012
  35.9 3.6 %copy-start.7 = (s32[4,8]{1,0:T(4,128)S(1)}, s32[4,8]{1,0:T(4,128)}, u32[]{:S(2)}) copy-start(s32[4,8]{1,0:T(4,128)} %mask_ref.1) | copy-start | bytes 388
  35.9 7.3 %collective-permute-start.2 = (bf16[32,256]{1,0:T(8,128)(2,1)S(1)}, bf16[32,256]{1,0:T(8,128)(2,1)S(1)}, u32[]{:S(2)}, u32[]{:S(2)}) collective-permute-start(bf16[32,256]{1,0:T(8,128)(2,1)S(1)} %pad_maximum_fusion), channel_id=1, source_target_pairs={{0,4},{2,6},{4,0},{6,2},{1,5},{3,7},{5,1},{7,3},{8,12},{10,14},{12... | collective-permute-start | bytes 49160 | tf_op jit(solution)/shard_map/ppermute | solution.py:268
  39.5 3.7 %copy-start.1 = (bf16[4,64,64]{2,1,0:T(8,128)(2,1)S(1)}, bf16[4,64,64]{2,1,0:T(8,128)(2,1)}, u32[]{:S(2)}) copy-start(bf16[4,64,64]{2,1,0:T(8,128)(2,1)} %transfer_ref.5) | copy-start | bytes 98308
  39.5 3.7 %copy-start.4 = (bf16[32,512]{1,0:T(8,128)(2,1)S(1)}, bf16[32,512]{1,0:T(8,128)(2,1)}, u32[]{:S(2)}) copy-start(bf16[32,512]{1,0:T(8,128)(2,1)} %value_ref.1) | copy-start | bytes 98308
  39.5 4.3 %copy-start = (bf16[64,64,64]{2,1,0:T(8,128)(2,1)S(1)}, bf16[64,64,64]{2,1,0:T(8,128)(2,1)}, u32[]{:S(2)}) copy-start(bf16[64,64,64]{2,1,0:T(8,128)(2,1)} %coupling_ref.1) | copy-start | bytes 1572868
  41.2 2.6 %copy-start.2 = (bf16[64,512]{1,0:T(8,128)(2,1)S(1)}, bf16[64,512]{1,0:T(8,128)(2,1)}, u32[]{:S(2)}) copy-start(bf16[64,512]{1,0:T(8,128)(2,1)} %target_ref.3) | copy-start | bytes 196612
  41.3 2.6 %copy-start.3 = (bf16[64,512]{1,0:T(8,128)(2,1)S(1)}, bf16[64,512]{1,0:T(8,128)(2,1)}, u32[]{:S(2)}) copy-start(bf16[64,512]{1,0:T(8,128)(2,1)} %basis_ref.1) | copy-start | bytes 196612
  46.0 14.4 %all-to-all-start.2 = ((bf16[8,256,128]{2,1,0:T(8,128)(2,1)}), bf16[8,256,128]{2,1,0:T(8,128)(2,1)S(1)}, u32[]{:S(2)}, u32[]{:S(2)}) async-start(bf16[8,256,128]{2,1,0:T(8,128)(2,1)} %get-tuple-element.33), calls=%async_computation.2 | async-start | bytes 1048576 | tf_op jit(solution)/shard_map/all_to_all | solution.py:307
  51.7 3.1 %collective-permute-start.3 = (bf16[32,640]{1,0:T(8,128)(2,1)S(1)}, bf16[32,640]{1,0:T(8,128)(2,1)S(1)}, u32[]{:S(2)}, u32[]{:S(2)}) collective-permute-start(bf16[32,640]{1,0:T(8,128)(2,1)S(1)} %get-tuple-element.34), channel_id=1, source_target_pairs={{0,1},{1,0},{2,3},{3,2},{4,5},{5,4},{6,7},{7,6},{8,9},{9,8},{10,11... | collective-permute-start | bytes 122888 | tf_op jit(solution)/shard_map/ppermute | solution.py:268
  54.9 5.5 %collective-permute-start.4 = (bf16[32,128]{1,0:T(8,128)(2,1)S(1)}, bf16[32,128]{1,0:T(8,128)(2,1)S(1)}, u32[]{:S(2)}, u32[]{:S(2)}) collective-permute-start(bf16[32,128]{1,0:T(8,128)(2,1)S(1)} %pad_maximum_fusion.3.two_ref), channel_id=1, source_target_pairs={{0,2},{2,0},{4,6},{6,4},{1,3},{3,1},{5,7},{7,5},{8,10},{10,8},{12,... | collective-permute-start | bytes 24584 | tf_op jit(solution)/shard_map/ppermute | solution.py:268
  61.3 19.9 %all-to-all-start.3 = ((bf16[8,64,128]{2,1,0:T(8,128)(2,1)}), bf16[8,64,128]{2,1,0:T(8,128)(2,1)S(1)}, u32[]{:S(2)}, u32[]{:S(2)}) async-start(bf16[8,64,128]{2,1,0:T(8,128)(2,1)} %merge.1), calls=%async_computation.3 | async-start | bytes 262144 | tf_op jit(solution)/shard_map/all_to_all | solution.py:317
  73.3 7.2 %copy-start.6 = (bf16[32,512]{1,0:T(8,128)(2,1)S(1)}, bf16[32,512]{1,0:T(8,128)(2,1)}, u32[]{:S(2)}) copy-start(bf16[32,512]{1,0:T(8,128)(2,1)} %get-tuple-element.20.value_ref) | copy-start | bytes 98308
  73.4 7.1 %collective-permute-start.5 = (bf16[32,256]{1,0:T(8,128)(2,1)S(1)}, bf16[32,256]{1,0:T(8,128)(2,1)S(1)}, u32[]{:S(2)}, u32[]{:S(2)}) collective-permute-start(bf16[32,256]{1,0:T(8,128)(2,1)S(1)} %pad_maximum_fusion.1), channel_id=1, source_target_pairs={{0,4},{2,6},{4,0},{6,2},{1,5},{3,7},{5,1},{7,3},{8,12},{10,14},{12... | collective-permute-start | bytes 49160 | tf_op jit(solution)/shard_map/ppermute | solution.py:268

commit v6 on v5

--- a/solution.py
+++ b/solution.py
@@ -197,13 +197,16 @@
                 ).astype(BF16)
 
 
-def near_body(value_ref, other_ref, kernel_ref, two_ref, four_ref, eight_ref, rows_ref, transfer_ref, base_ref, spread_ref):
+def near_body(value_ref, other_ref, kernel_ref, base_ref):
     width = LEAVES * LEAF_SIZE
     for leaf in range(LEAVES):
         low, high = max(leaf - 1, 0) * LEAF_SIZE, min(leaf + 2, LEAVES) * LEAF_SIZE
         near = dot(value_ref[:, low:high], kernel_ref[leaf_cols(leaf), low:high], NT)
         near += dot(other_ref[:RIGHT_SIDES, low:high], kernel_ref[leaf_cols(leaf), width + low : width + high], NT)
         base_ref[:, leaf_cols(leaf)] = near + 0.5 * value_ref[:, leaf_cols(leaf)].astype(F32)
+
+
+def spread_body(two_ref, four_ref, eight_ref, rows_ref, transfer_ref, spread_ref):
     me = lax.axis_index("x") * NC + lax.axis_index("c")
     down = jnp.zeros((RIGHT_SIDES, RANK), F32)
     pairs = [two_ref[...], four_ref[...], eight_ref[:, :128], eight_ref[:, 128:]]
@@ -294,10 +297,8 @@
         first_merge_body, "first_merge", [merged_shape, shape(NA, LEAVES * ROWS, 2 * 128)], [VM]
     )
     next_merge = call(merge_body, "merge", [merged_shape], [VM] * 2)
-    nearby = call(
-        near_body, "nearby",
-        [shape(RIGHT_SIDES, panels_here, dtype=F32), shape(LEAVES * ROWS, 128, dtype=F32)], [VM] * 8,
-    )
+    nearby = call(near_body, "nearby", [shape(RIGHT_SIDES, panels_here, dtype=F32)], [VM] * 3)
+    spreading = call(spread_body, "spread", [shape(LEAVES * ROWS, 128, dtype=F32)], [VM] * 5)
 
     def together(*arrays):
         return lax.optimization_barrier(arrays)
@@ -308,7 +309,13 @@
         other = swap(packet, "c", 1)
         two = jnp.concatenate([packet[:RIGHT_SIDES, columns], other[:RIGHT_SIDES, columns]], axis=1)
         four = swap(two, "x", 1)
-        arrived, four = together(arrived, four)
+        if kernel is None:
+            kernel = call(
+                kernel_body, "kernel", [shape(panels_here, 2 * panels_here)], [VM, VM, SM],
+                [pltpu.VMEM((8, panels_here), F32)],
+            )(panels, other, near_mask)[0]
+        base = nearby(value, other, kernel)[0]
+        arrived, four, base = together(arrived, four, base)
         if choice is None:
             merged, choice = first_merge(arrived)
         else:
@@ -316,12 +323,7 @@
         merged, four = together(merged, four)
         received = lax.all_to_all(merged, "a", 0, 0, axis_index_groups=[ORDER], tiled=True)
         eight = swap(jnp.concatenate([two, four], axis=1), "x", 2)
-        if kernel is None:
-            kernel = call(
-                kernel_body, "kernel", [shape(panels_here, 2 * panels_here)], [VM, VM, SM],
-                [pltpu.VMEM((8, panels_here), F32)],
-            )(panels, other, near_mask)[0]
-        base, spread = nearby(value, other, kernel, two, four, eight, cluster_coupling, leaf_transfer)
+        spread = spreading(two, four, eight, cluster_coupling, leaf_transfer)[0]
         return received, base, spread, choice, kernel
 
     operands = (

time: 82.8 us -> 82.6 us (level)
  the two profiles are of different devices: /device:TPU:14 before, /device:TPU:12 now
where the time goes in v6:
time: 82.6 us; the launch traced here: 81.8 us
  starting transfers between devices  55 us (67%)
  waiting for transfers between devices  14.3 us (17%)
  Pallas kernels  11.3 us (14%)
    all_to_all x2, starting transfers between devices, couple(): lax.all_to_all(merged, 'a', 0, 0, axis_index_groups=[ORDER], tiled=True)  27.8 us
    ppermute x6, starting transfers between devices, swap(): return lax.ppermute(block, axis, [(i, i ^ distance) for i in range(count)])  15.2 us
    ppermute x6, waiting for transfers between devices, swap(): return lax.ppermute(block, axis, [(i, i ^ distance) for i in range(count)])  14.2 us
    all_to_all x2, starting transfers between devices, couple(): arrived = lax.all_to_all(send, ('b', 'y'), 0, 0, tiled=True)  12 us
    pallas_call x1, Pallas kernels, shards(): first(*[pltpu.with_memory_space_constraint(array, pltpu.HBM) for array in...  3.36 us
    pallas_call x1, Pallas kernels, shards(): call(middle_body, 'middle', [values, shape(PEERS, CHUNK, 128), shape(RIGH...  2.17 us
    pallas_call x1, Pallas kernels, couple(): call(kernel_body, 'kernel', [shape(panels_here, 2 * panels_here)], [VM, V...  1.72 us
  transfers between devices with their start and end apart: 10, of which 7 were waited for; matrix products, arithmetic and copies ran while one was open for 1% of the time, Pallas kernels for 4%

profile of v6, /device:TPU:12, one launch (start us, length us, event | category | flops | bytes accessed | tf_op | source)
XLA Modules:
  0.0 81.8 jit_solution(7258523305648588312)
XLA Ops:
  0.6 3.4 %first.1 = (bf16[8,272,128]{2,1,0:T(8,128)(2,1)}, bf16[80,640]{1,0:T(8,128)(2,1)S(1)}, s32[128]{0:T(128)S(1)}) custom-call(s32[64]{0:T(128)} %leaf_hbm.1, s32[64]{0:T(128)} %bitcast.1, s32[64]{0:T(128)} %target_hbm.1, f32[7,512]{1,0:T(8,128)} %own_ref.1, bf16[32,512]{1,0:T(8,128)(2,1)} %value_ref.1, bf16[64,512]{1,0:T(8,128)(2,1)} %basis_ref.1, ...), custom_call_target="tpu_custom_call" | custom-call | tf_op jit(solution)/shard_map/first/pallas_call | solution.py:332
  4.0 6.3 %all-to-all-start = ((bf16[8,272,128]{2,1,0:T(8,128)(2,1)}), bf16[8,272,128]{2,1,0:T(8,128)(2,1)S(1)}, u32[]{:S(2)}, u32[]{:S(2)}) async-start(bf16[8,272,128]{2,1,0:T(8,128)(2,1)} %get-tuple-element.20), calls=%async_computation | async-start | bytes 1114112 | tf_op jit(solution)/shard_map/all_to_all | solution.py:308
  10.3 1.9 %collective-permute-start = (bf16[80,640]{1,0:T(8,128)(2,1)S(1)}, bf16[80,640]{1,0:T(8,128)(2,1)S(1)}, u32[]{:S(2)}, u32[]{:S(2)}) collective-permute-start(bf16[80,640]{1,0:T(8,128)(2,1)S(1)} %get-tuple-element.21), channel_id=1, source_target_pairs={{0,1},{1,0},{2,3},{3,2},{4,5},{5,4},{6,7},{7,6},{8,9},{9,8},{10,11... | collective-permute-start | bytes 307208 | tf_op jit(solution)/shard_map/ppermute | solution.py:271
  12.2 1.3 %collective-permute-done.packet_ref.other_ref = bf16[80,640]{1,0:T(8,128)(2,1)S(1)} collective-permute-done((bf16[80,640]{1,0:T(8,128)(2,1)S(1)}, bf16[80,640]{1,0:T(8,128)(2,1)S(1)}, u32[]{:S(2)}, u32[]{:S(2)}) %collective-permute-start) | collective-permute-done | bytes 102432 | tf_op jit(solution)/shard_map/ppermute | solution.py:271
  13.5 0.1 pad_maximum_fusion.2.two_ref
  13.6 3.2 %collective-permute-start.1 = (bf16[32,128]{1,0:T(8,128)(2,1)S(1)}, bf16[32,128]{1,0:T(8,128)(2,1)S(1)}, u32[]{:S(2)}, u32[]{:S(2)}) collective-permute-start(bf16[32,128]{1,0:T(8,128)(2,1)S(1)} %pad_maximum_fusion.2.two_ref), channel_id=1, source_target_pairs={{0,2},{2,0},{4,6},{6,4},{1,3},{3,1},{5,7},{7,5},{8,10},{10,8},{12,... | collective-permute-start | bytes 24584 | tf_op jit(solution)/shard_map/ppermute | solution.py:271
  16.8 1.7 %kernel.1.kernel_ref = bf16[512,1024]{1,0:T(8,128)(2,1)S(1)} custom-call(f32[7,512]{1,0:T(8,128)S(1)} %copy-done.5, bf16[80,640]{1,0:T(8,128)(2,1)S(1)} %collective-permute-done.packet_ref.other_ref, s32[4,8]{1,0:T(4,128)S(1)} %copy-done.7), custom_call_target="tpu_custom_call" | custom-call | tf_op jit(solution)/shard_map/kernel/pallas_call | solution.py:313
  18.6 0.3 nearby.2.base_ref
  18.9 0.3 collective-permute-done.1.four_ref
  19.2 0.9 %first_merge.1 = (bf16[8,64,128]{2,1,0:T(8,128)(2,1)}, bf16[8,64,256]{2,1,0:T(8,128)(2,1)S(1)}) custom-call(bf16[8,272,128]{2,1,0:T(8,128)(2,1)S(1)} %all-to-all-done.recv_ref), custom_call_target="tpu_custom_call" | custom-call | tf_op jit(solution)/shard_map/first_merge/pallas_call | solution.py:320
  20.1 15.8 %all-to-all-start.1 = ((bf16[8,64,128]{2,1,0:T(8,128)(2,1)}), bf16[8,64,128]{2,1,0:T(8,128)(2,1)S(1)}, u32[]{:S(2)}, u32[]{:S(2)}) async-start(bf16[8,64,128]{2,1,0:T(8,128)(2,1)} %get-tuple-element.25), calls=%async_computation.1 | async-start | bytes 262144 | tf_op jit(solution)/shard_map/all_to_all | solution.py:324
  35.9 0.1 pad_maximum_fusion
  36.0 2.5 %collective-permute-start.2 = (bf16[32,256]{1,0:T(8,128)(2,1)S(1)}, bf16[32,256]{1,0:T(8,128)(2,1)S(1)}, u32[]{:S(2)}, u32[]{:S(2)}) collective-permute-start(bf16[32,256]{1,0:T(8,128)(2,1)S(1)} %pad_maximum_fusion), channel_id=1, source_target_pairs={{0,4},{2,6},{4,0},{6,2},{1,5},{3,7},{5,1},{7,3},{8,12},{10,14},{12... | collective-permute-start | bytes 49160 | tf_op jit(solution)/shard_map/ppermute | solution.py:271
  38.5 0.1 copy.13.rows_ref
  38.7 4.6 %collective-permute-done.2.eight_ref = bf16[32,256]{1,0:T(8,128)(2,1)S(1)} collective-permute-done((bf16[32,256]{1,0:T(8,128)(2,1)S(1)}, bf16[32,256]{1,0:T(8,128)(2,1)S(1)}, u32[]{:S(2)}, u32[]{:S(2)}) %collective-permute-start.2) | collective-permute-done | bytes 16416 | tf_op jit(solution)/shard_map/ppermute | solution.py:271
  43.3 0.4 spread.2.spread_ref
  43.7 0.1 all-to-all-done.1.recv_ref
  43.8 2.2 %middle.1 = (bf16[32,512]{1,0:T(8,128)(2,1)}, bf16[8,256,128]{2,1,0:T(8,128)(2,1)}, bf16[32,640]{1,0:T(8,128)(2,1)S(1)}) custom-call(bf16[8,64,128]{2,1,0:T(8,128)(2,1)S(1)} %all-to-all-done.1.recv_ref, f32[64,128]{1,0:T(8,128)S(1)} %spread.2.spread_ref, f32[32,512]{1,0:T(8,128)S(1)} %nearby.2.base_ref, bf16[64,512]{1,0:T(8,128)(2,1)S(1)} %copy-done.2, ...), custom_call_target="tpu_custom_call" | custom-call | tf_op jit(solution)/shard_map/middle/pallas_call | solution.py:334
  45.9 5.7 %all-to-all-start.2 = ((bf16[8,256,128]{2,1,0:T(8,128)(2,1)}), bf16[8,256,128]{2,1,0:T(8,128)(2,1)S(1)}, u32[]{:S(2)}, u32[]{:S(2)}) async-start(bf16[8,256,128]{2,1,0:T(8,128)(2,1)} %get-tuple-element.30), calls=%async_computation.2 | async-start | bytes 1048576 | tf_op jit(solution)/shard_map/all_to_all | solution.py:308
  51.6 2.0 %collective-permute-start.3 = (bf16[32,640]{1,0:T(8,128)(2,1)S(1)}, bf16[32,640]{1,0:T(8,128)(2,1)S(1)}, u32[]{:S(2)}, u32[]{:S(2)}) collective-permute-start(bf16[32,640]{1,0:T(8,128)(2,1)S(1)} %get-tuple-element.31), channel_id=1, source_target_pairs={{0,1},{1,0},{2,3},{3,2},{4,5},{5,4},{6,7},{7,6},{8,9},{9,8},{10,11... | collective-permute-start | bytes 122888 | tf_op jit(solution)/shard_map/ppermute | solution.py:271
  53.7 1.2 %collective-permute-done.3.other_ref = bf16[32,640]{1,0:T(8,128)(2,1)S(1)} collective-permute-done((bf16[32,640]{1,0:T(8,128)(2,1)S(1)}, bf16[32,640]{1,0:T(8,128)(2,1)S(1)}, u32[]{:S(2)}, u32[]{:S(2)}) %collective-permute-start.3) | collective-permute-done | bytes 40992 | tf_op jit(solution)/shard_map/ppermute | solution.py:271
  54.9 0.1 pad_maximum_fusion.3.two_ref
  54.9 3.1 %collective-permute-start.4 = (bf16[32,128]{1,0:T(8,128)(2,1)S(1)}, bf16[32,128]{1,0:T(8,128)(2,1)S(1)}, u32[]{:S(2)}, u32[]{:S(2)}) collective-permute-start(bf16[32,128]{1,0:T(8,128)(2,1)S(1)} %pad_maximum_fusion.3.two_ref), channel_id=1, source_target_pairs={{0,2},{2,0},{4,6},{6,4},{1,3},{3,1},{5,7},{7,5},{8,10},{10,8},{12,... | collective-permute-start | bytes 24584 | tf_op jit(solution)/shard_map/ppermute | solution.py:271
  58.0 0.3 nearby.3.base_ref
  58.4 2.1 %collective-permute-done.4.four_ref = bf16[32,128]{1,0:T(8,128)(2,1)S(1)} collective-permute-done((bf16[32,128]{1,0:T(8,128)(2,1)S(1)}, bf16[32,128]{1,0:T(8,128)(2,1)S(1)}, u32[]{:S(2)}, u32[]{:S(2)}) %collective-permute-start.4) | collective-permute-done | bytes 8224 | tf_op jit(solution)/shard_map/ppermute | solution.py:271
  60.5 0.9 %merge.1 = bf16[8,64,128]{2,1,0:T(8,128)(2,1)} custom-call(bf16[8,256,128]{2,1,0:T(8,128)(2,1)S(1)} %all-to-all-done.2.recv_ref, bf16[8,64,256]{2,1,0:T(8,128)(2,1)S(1)} %get-tuple-element.33.choice_ref), custom_call_target="tpu_custom_call" | custom-call | tf_op jit(solution)/shard_map/merge/pallas_call | solution.py:322
  61.3 12.0 %all-to-all-start.3 = ((bf16[8,64,128]{2,1,0:T(8,128)(2,1)}), bf16[8,64,128]{2,1,0:T(8,128)(2,1)S(1)}, u32[]{:S(2)}, u32[]{:S(2)}) async-start(bf16[8,64,128]{2,1,0:T(8,128)(2,1)} %merge.1), calls=%async_computation.3 | async-start | bytes 262144 | tf_op jit(solution)/shard_map/all_to_all | solution.py:324
  73.3 0.1 pad_maximum_fusion.1
  73.4 2.4 %collective-permute-start.5 = (bf16[32,256]{1,0:T(8,128)(2,1)S(1)}, bf16[32,256]{1,0:T(8,128)(2,1)S(1)}, u32[]{:S(2)}, u32[]{:S(2)}) collective-permute-start(bf16[32,256]{1,0:T(8,128)(2,1)S(1)} %pad_maximum_fusion.1), channel_id=1, source_target_pairs={{0,4},{2,6},{4,0},{6,2},{1,5},{3,7},{5,1},{7,3},{8,12},{10,14},{12... | collective-permute-start | bytes 49160 | tf_op jit(solution)/shard_map/ppermute | solution.py:271
  75.8 4.7 %collective-permute-done.5.eight_ref = bf16[32,256]{1,0:T(8,128)(2,1)S(1)} collective-permute-done((bf16[32,256]{1,0:T(8,128)(2,1)S(1)}, bf16[32,256]{1,0:T(8,128)(2,1)S(1)}, u32[]{:S(2)}, u32[]{:S(2)}) %collective-permute-start.5) | collective-permute-done | bytes 16416 | tf_op jit(solution)/shard_map/ppermute | solution.py:271
  80.5 0.4 spread.3.spread_ref
  81.0 0.8 last.1
  (25 shorter events, 0.1 us)
Async XLA Ops:
  4.0 15.2 %all-to-all-start = ((bf16[8,272,128]{2,1,0:T(8,128)(2,1)}), bf16[8,272,128]{2,1,0:T(8,128)(2,1)S(1)}, u32[]{:S(2)}, u32[]{:S(2)}) async-start(bf16[8,272,128]{2,1,0:T(8,128)(2,1)} %get-tuple-element.20), calls=%async_computation | async-start | bytes 1114112 | tf_op jit(solution)/shard_map/all_to_all | solution.py:308
  10.3 3.2 %collective-permute-start = (bf16[80,640]{1,0:T(8,128)(2,1)S(1)}, bf16[80,640]{1,0:T(8,128)(2,1)S(1)}, u32[]{:S(2)}, u32[]{:S(2)}) collective-permute-start(bf16[80,640]{1,0:T(8,128)(2,1)S(1)} %get-tuple-element.21), channel_id=1, source_target_pairs={{0,1},{1,0},{2,3},{3,2},{4,5},{5,4},{6,7},{7,6},{8,9},{9,8},{10,11... | collective-permute-start | bytes 307208 | tf_op jit(solution)/shard_map/ppermute | solution.py:271
  13.5 3.3 %copy-start.5 = (f32[7,512]{1,0:T(8,128)S(1)}, f32[7,512]{1,0:T(8,128)}, u32[]{:S(2)}) copy-start(f32[7,512]{1,0:T(8,128)} %own_ref.1) | copy-start | bytes 43012
  13.5 3.3 %copy-start.7 = (s32[4,8]{1,0:T(4,128)S(1)}, s32[4,8]{1,0:T(4,128)}, u32[]{:S(2)}) copy-start(s32[4,8]{1,0:T(4,128)} %mask_ref.1) | copy-start | bytes 388
  13.6 5.0 %copy-start.4 = (bf16[32,512]{1,0:T(8,128)(2,1)S(1)}, bf16[32,512]{1,0:T(8,128)(2,1)}, u32[]{:S(2)}) copy-start(bf16[32,512]{1,0:T(8,128)(2,1)} %value_ref.1) | copy-start | bytes 98308
  13.6 5.7 %collective-permute-start.1 = (bf16[32,128]{1,0:T(8,128)(2,1)S(1)}, bf16[32,128]{1,0:T(8,128)(2,1)S(1)}, u32[]{:S(2)}, u32[]{:S(2)}) collective-permute-start(bf16[32,128]{1,0:T(8,128)(2,1)S(1)} %pad_maximum_fusion.2.two_ref), channel_id=1, source_target_pairs={{0,2},{2,0},{4,6},{6,4},{1,3},{3,1},{5,7},{7,5},{8,10},{10,8},{12,... | collective-permute-start | bytes 24584 | tf_op jit(solution)/shard_map/ppermute | solution.py:271
  18.5 25.2 %copy-start = (bf16[64,64,64]{2,1,0:T(8,128)(2,1)S(1)}, bf16[64,64,64]{2,1,0:T(8,128)(2,1)}, u32[]{:S(2)}) copy-start(bf16[64,64,64]{2,1,0:T(8,128)(2,1)} %coupling_ref.1) | copy-start | bytes 1572868
  20.1 18.4 %copy-start.8 = (bf16[1,512,64]{1,2,0:T(8,128)(2,1)S(1)}, bf16[1,512,64]{1,2,0:T(8,128)(2,1)}, u32[]{:S(2)}) copy-start(bf16[1,512,64]{1,2,0:T(8,128)(2,1)} %param.16) | copy-start | bytes 196612
  20.1 23.7 %all-to-all-start.1 = ((bf16[8,64,128]{2,1,0:T(8,128)(2,1)}), bf16[8,64,128]{2,1,0:T(8,128)(2,1)S(1)}, u32[]{:S(2)}, u32[]{:S(2)}) async-start(bf16[8,64,128]{2,1,0:T(8,128)(2,1)} %get-tuple-element.25), calls=%async_computation.1 | async-start | bytes 262144 | tf_op jit(solution)/shard_map/all_to_all | solution.py:324
  36.0 7.3 %copy-start.1 = (bf16[4,64,64]{2,1,0:T(8,128)(2,1)S(1)}, bf16[4,64,64]{2,1,0:T(8,128)(2,1)}, u32[]{:S(2)}) copy-start(bf16[4,64,64]{2,1,0:T(8,128)(2,1)} %transfer_ref.5) | copy-start | bytes 98308
  36.0 7.3 %collective-permute-start.2 = (bf16[32,256]{1,0:T(8,128)(2,1)S(1)}, bf16[32,256]{1,0:T(8,128)(2,1)S(1)}, u32[]{:S(2)}, u32[]{:S(2)}) collective-permute-start(bf16[32,256]{1,0:T(8,128)(2,1)S(1)} %pad_maximum_fusion), channel_id=1, source_target_pairs={{0,4},{2,6},{4,0},{6,2},{1,5},{3,7},{5,1},{7,3},{8,12},{10,14},{12... | collective-permute-start | bytes 49160 | tf_op jit(solution)/shard_map/ppermute | solution.py:271
  38.7 5.1 %copy-start.2 = (bf16[64,512]{1,0:T(8,128)(2,1)S(1)}, bf16[64,512]{1,0:T(8,128)(2,1)}, u32[]{:S(2)}) copy-start(bf16[64,512]{1,0:T(8,128)(2,1)} %target_ref.3) | copy-start | bytes 196612
  38.7 5.1 %copy-start.3 = (bf16[64,512]{1,0:T(8,128)(2,1)S(1)}, bf16[64,512]{1,0:T(8,128)(2,1)}, u32[]{:S(2)}) copy-start(bf16[64,512]{1,0:T(8,128)(2,1)} %basis_ref.1) | copy-start | bytes 196612
  45.9 14.5 %all-to-all-start.2 = ((bf16[8,256,128]{2,1,0:T(8,128)(2,1)}), bf16[8,256,128]{2,1,0:T(8,128)(2,1)S(1)}, u32[]{:S(2)}, u32[]{:S(2)}) async-start(bf16[8,256,128]{2,1,0:T(8,128)(2,1)} %get-tuple-element.30), calls=%async_computation.2 | async-start | bytes 1048576 | tf_op jit(solution)/shard_map/all_to_all | solution.py:308
  51.6 6.4 %copy-start.6 = (bf16[32,512]{1,0:T(8,128)(2,1)S(1)}, bf16[32,512]{1,0:T(8,128)(2,1)}, u32[]{:S(2)}) copy-start(bf16[32,512]{1,0:T(8,128)(2,1)} %get-tuple-element.18.value_ref) | copy-start | bytes 98308
  51.6 3.2 %collective-permute-start.3 = (bf16[32,640]{1,0:T(8,128)(2,1)S(1)}, bf16[32,640]{1,0:T(8,128)(2,1)S(1)}, u32[]{:S(2)}, u32[]{:S(2)}) collective-permute-start(bf16[32,640]{1,0:T(8,128)(2,1)S(1)} %get-tuple-element.31), channel_id=1, source_target_pairs={{0,1},{1,0},{2,3},{3,2},{4,5},{5,4},{6,7},{7,6},{8,9},{9,8},{10,11... | collective-permute-start | bytes 122888 | tf_op jit(solution)/shard_map/ppermute | solution.py:271
  54.9 5.5 %collective-permute-start.4 = (bf16[32,128]{1,0:T(8,128)(2,1)S(1)}, bf16[32,128]{1,0:T(8,128)(2,1)S(1)}, u32[]{:S(2)}, u32[]{:S(2)}) collective-permute-start(bf16[32,128]{1,0:T(8,128)(2,1)S(1)} %pad_maximum_fusion.3.two_ref), channel_id=1, source_target_pairs={{0,2},{2,0},{4,6},{6,4},{1,3},{3,1},{5,7},{7,5},{8,10},{10,8},{12,... | collective-permute-start | bytes 24584 | tf_op jit(solution)/shard_map/ppermute | solution.py:271
  61.3 19.7 %all-to-all-start.3 = ((bf16[8,64,128]{2,1,0:T(8,128)(2,1)}), bf16[8,64,128]{2,1,0:T(8,128)(2,1)S(1)}, u32[]{:S(2)}, u32[]{:S(2)}) async-start(bf16[8,64,128]{2,1,0:T(8,128)(2,1)} %merge.1), calls=%async_computation.3 | async-start | bytes 262144 | tf_op jit(solution)/shard_map/all_to_all | solution.py:324
  73.4 7.1 %collective-permute-start.5 = (bf16[32,256]{1,0:T(8,128)(2,1)S(1)}, bf16[32,256]{1,0:T(8,128)(2,1)S(1)}, u32[]{:S(2)}, u32[]{:S(2)}) collective-permute-start(bf16[32,256]{1,0:T(8,128)(2,1)S(1)} %pad_maximum_fusion.1), channel_id=1, source_target_pairs={{0,4},{2,6},{4,0},{6,2},{1,5},{3,7},{5,1},{7,3},{8,12},{10,14},{12... | collective-permute-start | bytes 49160 | tf_op jit(solution)/shard_map/ppermute | solution.py:271

commit v7 on v6

--- a/solution.py
+++ b/solution.py
@@ -96,12 +96,8 @@
     pairs = [
         (wide_hbm, wide_ref), (target_hbm, target_ref), (leaf_hbm, leaf_ref),
         (value_hbm, value_ref), (basis_hbm, basis_ref), (transfer_hbm, transfer_ref), (panel_hbm, panel_ref),
+        (coupling_hbm, coupling_ref),
     ]
-    parts = 4
-    each = OUTS // parts
-    for part in range(parts):
-        span = pl.ds(part * each, each)
-        pairs.append((coupling_hbm.at[span], coupling_ref.at[span]))
     copies = [pltpu.make_async_copy(source, place, sems.at[i]) for i, (source, place) in enumerate(pairs)]
     for copy in copies:
         copy.start()
@@ -134,10 +130,9 @@
     for part, rows in enumerate(split_parts(panel)):
         start = RIGHT_SIDES + part * ROWS
         swap_ref[start : start + ROWS, : LEAVES * LEAF_SIZE] = rows
-    for part in range(parts):
-        copies[7 + part].wait()
-        for block in range(part * each, (part + 1) * each):
-            product(block, place_ref, coupling_ref, coeff_ref, send_ref)
+    copies[7].wait()
+    for block in range(OUTS):
+        product(block, place_ref, coupling_ref, coeff_ref, send_ref)
 
 
 def merge(recv_ref, choice_ref, out_ref):
@@ -289,7 +284,7 @@
             coeff_work,
             pltpu.VMEM((2 * PEERS * NA, 128), F32),
             pltpu.SMEM((NA * PEERS,), jnp.int32),
-            pltpu.SemaphoreType.DMA((11,)),
+            pltpu.SemaphoreType.DMA((8,)),
         ],
         [VM, VM, SM],
     )

time: 82.6 us -> 82 us (level)
  the two profiles are of different devices: /device:TPU:12 before, /device:TPU:14 now
where the time goes in v7:
time: 82 us; the launch traced here: 81.2 us
  starting transfers between devices  56.1 us (68%)
  waiting for transfers between devices  13.1 us (16%)
  Pallas kernels  10.7 us (13%)
    all_to_all x2, starting transfers between devices, couple(): lax.all_to_all(merged, 'a', 0, 0, axis_index_groups=[ORDER], tiled=True)  27.8 us
    ppermute x6, starting transfers between devices, swap(): return lax.ppermute(block, axis, [(i, i ^ distance) for i in range(count)])  16.3 us
    ppermute x6, waiting for transfers between devices, swap(): return lax.ppermute(block, axis, [(i, i ^ distance) for i in range(count)])  13.1 us
    all_to_all x2, starting transfers between devices, couple(): arrived = lax.all_to_all(send, ('b', 'y'), 0, 0, tiled=True)  12 us
    pallas_call x1, Pallas kernels, shards(): first(*[pltpu.with_memory_space_constraint(array, pltpu.HBM) for array in...  2.74 us
    pallas_call x1, Pallas kernels, shards(): call(middle_body, 'middle', [values, shape(PEERS, CHUNK, 128), shape(RIGH...  2.17 us
    pallas_call x1, Pallas kernels, couple(): call(kernel_body, 'kernel', [shape(panels_here, 2 * panels_here)], [VM, V...  1.72 us
  transfers between devices with their start and end apart: 10, of which 6 were waited for; matrix products, arithmetic and copies ran while one was open for 1% of the time, Pallas kernels for 4%

profile of v7, /device:TPU:14, one launch (start us, length us, event | category | flops | bytes accessed | tf_op | source)
XLA Modules:
  0.0 81.2 jit_solution(3654878823995287889)
XLA Ops:
  0.6 2.7 %first.1 = (bf16[8,272,128]{2,1,0:T(8,128)(2,1)}, bf16[80,640]{1,0:T(8,128)(2,1)S(1)}, s32[128]{0:T(128)S(1)}) custom-call(s32[64]{0:T(128)} %leaf_hbm.1, s32[64]{0:T(128)} %bitcast.1, s32[64]{0:T(128)} %target_hbm.1, f32[7,512]{1,0:T(8,128)} %own_ref.1, bf16[32,512]{1,0:T(8,128)(2,1)} %value_ref.1, bf16[64,512]{1,0:T(8,128)(2,1)} %basis_ref.1, ...), custom_call_target="tpu_custom_call" | custom-call | tf_op jit(solution)/shard_map/first/pallas_call | solution.py:327
  3.4 6.3 %all-to-all-start = ((bf16[8,272,128]{2,1,0:T(8,128)(2,1)}), bf16[8,272,128]{2,1,0:T(8,128)(2,1)S(1)}, u32[]{:S(2)}, u32[]{:S(2)}) async-start(bf16[8,272,128]{2,1,0:T(8,128)(2,1)} %get-tuple-element.20), calls=%async_computation | async-start | bytes 1114112 | tf_op jit(solution)/shard_map/all_to_all | solution.py:303
  9.7 1.9 %collective-permute-start = (bf16[80,640]{1,0:T(8,128)(2,1)S(1)}, bf16[80,640]{1,0:T(8,128)(2,1)S(1)}, u32[]{:S(2)}, u32[]{:S(2)}) collective-permute-start(bf16[80,640]{1,0:T(8,128)(2,1)S(1)} %get-tuple-element.21), channel_id=1, source_target_pairs={{0,1},{1,0},{2,3},{3,2},{4,5},{5,4},{6,7},{7,6},{8,9},{9,8},{10,11... | collective-permute-start | bytes 307208 | tf_op jit(solution)/shard_map/ppermute | solution.py:266
  11.6 1.3 %collective-permute-done.packet_ref.other_ref = bf16[80,640]{1,0:T(8,128)(2,1)S(1)} collective-permute-done((bf16[80,640]{1,0:T(8,128)(2,1)S(1)}, bf16[80,640]{1,0:T(8,128)(2,1)S(1)}, u32[]{:S(2)}, u32[]{:S(2)}) %collective-permute-start) | collective-permute-done | bytes 102432 | tf_op jit(solution)/shard_map/ppermute | solution.py:266
  12.9 0.1 pad_maximum_fusion.2.two_ref
  12.9 2.9 %collective-permute-start.1 = (bf16[32,128]{1,0:T(8,128)(2,1)S(1)}, bf16[32,128]{1,0:T(8,128)(2,1)S(1)}, u32[]{:S(2)}, u32[]{:S(2)}) collective-permute-start(bf16[32,128]{1,0:T(8,128)(2,1)S(1)} %pad_maximum_fusion.2.two_ref), channel_id=1, source_target_pairs={{0,2},{2,0},{4,6},{6,4},{1,3},{3,1},{5,7},{7,5},{8,10},{10,8},{12,... | collective-permute-start | bytes 24584 | tf_op jit(solution)/shard_map/ppermute | solution.py:266
  15.8 1.7 %kernel.1.kernel_ref = bf16[512,1024]{1,0:T(8,128)(2,1)S(1)} custom-call(f32[7,512]{1,0:T(8,128)S(1)} %copy-done.5, bf16[80,640]{1,0:T(8,128)(2,1)S(1)} %collective-permute-done.packet_ref.other_ref, s32[4,8]{1,0:T(4,128)S(1)} %copy-done.7), custom_call_target="tpu_custom_call" | custom-call | tf_op jit(solution)/shard_map/kernel/pallas_call | solution.py:308
  17.6 0.3 nearby.2.base_ref
  17.9 0.7 collective-permute-done.1.four_ref
  18.6 0.9 %first_merge.1 = (bf16[8,64,128]{2,1,0:T(8,128)(2,1)}, bf16[8,64,256]{2,1,0:T(8,128)(2,1)S(1)}) custom-call(bf16[8,272,128]{2,1,0:T(8,128)(2,1)S(1)} %all-to-all-done.recv_ref), custom_call_target="tpu_custom_call" | custom-call | tf_op jit(solution)/shard_map/first_merge/pallas_call | solution.py:315
  19.5 15.8 %all-to-all-start.1 = ((bf16[8,64,128]{2,1,0:T(8,128)(2,1)}), bf16[8,64,128]{2,1,0:T(8,128)(2,1)S(1)}, u32[]{:S(2)}, u32[]{:S(2)}) async-start(bf16[8,64,128]{2,1,0:T(8,128)(2,1)} %get-tuple-element.25), calls=%async_computation.1 | async-start | bytes 262144 | tf_op jit(solution)/shard_map/all_to_all | solution.py:319
  35.3 0.1 pad_maximum_fusion
  35.4 3.4 %collective-permute-start.2 = (bf16[32,256]{1,0:T(8,128)(2,1)S(1)}, bf16[32,256]{1,0:T(8,128)(2,1)S(1)}, u32[]{:S(2)}, u32[]{:S(2)}) collective-permute-start(bf16[32,256]{1,0:T(8,128)(2,1)S(1)} %pad_maximum_fusion), channel_id=1, source_target_pairs={{0,4},{2,6},{4,0},{6,2},{1,5},{3,7},{5,1},{7,3},{8,12},{10,14},{12... | collective-permute-start | bytes 49160 | tf_op jit(solution)/shard_map/ppermute | solution.py:266
  38.8 0.1 copy.13.rows_ref
  39.0 3.7 %collective-permute-done.2.eight_ref = bf16[32,256]{1,0:T(8,128)(2,1)S(1)} collective-permute-done((bf16[32,256]{1,0:T(8,128)(2,1)S(1)}, bf16[32,256]{1,0:T(8,128)(2,1)S(1)}, u32[]{:S(2)}, u32[]{:S(2)}) %collective-permute-start.2) | collective-permute-done | bytes 16416 | tf_op jit(solution)/shard_map/ppermute | solution.py:266
  42.6 0.4 spread.2.spread_ref
  43.1 0.0 copy-done.2
  43.1 2.2 %middle.1 = (bf16[32,512]{1,0:T(8,128)(2,1)}, bf16[8,256,128]{2,1,0:T(8,128)(2,1)}, bf16[32,640]{1,0:T(8,128)(2,1)S(1)}) custom-call(bf16[8,64,128]{2,1,0:T(8,128)(2,1)S(1)} %all-to-all-done.1.recv_ref, f32[64,128]{1,0:T(8,128)S(1)} %spread.2.spread_ref, f32[32,512]{1,0:T(8,128)S(1)} %nearby.2.base_ref, bf16[64,512]{1,0:T(8,128)(2,1)S(1)} %copy-done.2, ...), custom_call_target="tpu_custom_call" | custom-call | tf_op jit(solution)/shard_map/middle/pallas_call | solution.py:329
  45.3 5.7 %all-to-all-start.2 = ((bf16[8,256,128]{2,1,0:T(8,128)(2,1)}), bf16[8,256,128]{2,1,0:T(8,128)(2,1)S(1)}, u32[]{:S(2)}, u32[]{:S(2)}) async-start(bf16[8,256,128]{2,1,0:T(8,128)(2,1)} %get-tuple-element.30), calls=%async_computation.2 | async-start | bytes 1048576 | tf_op jit(solution)/shard_map/all_to_all | solution.py:303
  51.0 2.0 %collective-permute-start.3 = (bf16[32,640]{1,0:T(8,128)(2,1)S(1)}, bf16[32,640]{1,0:T(8,128)(2,1)S(1)}, u32[]{:S(2)}, u32[]{:S(2)}) collective-permute-start(bf16[32,640]{1,0:T(8,128)(2,1)S(1)} %get-tuple-element.31), channel_id=1, source_target_pairs={{0,1},{1,0},{2,3},{3,2},{4,5},{5,4},{6,7},{7,6},{8,9},{9,8},{10,11... | collective-permute-start | bytes 122888 | tf_op jit(solution)/shard_map/ppermute | solution.py:266
  53.1 1.2 %collective-permute-done.3.other_ref = bf16[32,640]{1,0:T(8,128)(2,1)S(1)} collective-permute-done((bf16[32,640]{1,0:T(8,128)(2,1)S(1)}, bf16[32,640]{1,0:T(8,128)(2,1)S(1)}, u32[]{:S(2)}, u32[]{:S(2)}) %collective-permute-start.3) | collective-permute-done | bytes 40992 | tf_op jit(solution)/shard_map/ppermute | solution.py:266
  54.2 0.1 pad_maximum_fusion.3.two_ref
  54.3 2.7 %collective-permute-start.4 = (bf16[32,128]{1,0:T(8,128)(2,1)S(1)}, bf16[32,128]{1,0:T(8,128)(2,1)S(1)}, u32[]{:S(2)}, u32[]{:S(2)}) collective-permute-start(bf16[32,128]{1,0:T(8,128)(2,1)S(1)} %pad_maximum_fusion.3.two_ref), channel_id=1, source_target_pairs={{0,2},{2,0},{4,6},{6,4},{1,3},{3,1},{5,7},{7,5},{8,10},{10,8},{12,... | collective-permute-start | bytes 24584 | tf_op jit(solution)/shard_map/ppermute | solution.py:266
  57.1 0.3 nearby.3.base_ref
  57.4 2.5 %collective-permute-done.4.four_ref = bf16[32,128]{1,0:T(8,128)(2,1)S(1)} collective-permute-done((bf16[32,128]{1,0:T(8,128)(2,1)S(1)}, bf16[32,128]{1,0:T(8,128)(2,1)S(1)}, u32[]{:S(2)}, u32[]{:S(2)}) %collective-permute-start.4) | collective-permute-done | bytes 8224 | tf_op jit(solution)/shard_map/ppermute | solution.py:266
  59.9 0.9 %merge.1 = bf16[8,64,128]{2,1,0:T(8,128)(2,1)} custom-call(bf16[8,256,128]{2,1,0:T(8,128)(2,1)S(1)} %all-to-all-done.2.recv_ref, bf16[8,64,256]{2,1,0:T(8,128)(2,1)S(1)} %get-tuple-element.33.choice_ref), custom_call_target="tpu_custom_call" | custom-call | tf_op jit(solution)/shard_map/merge/pallas_call | solution.py:317
  60.7 12.0 %all-to-all-start.3 = ((bf16[8,64,128]{2,1,0:T(8,128)(2,1)}), bf16[8,64,128]{2,1,0:T(8,128)(2,1)S(1)}, u32[]{:S(2)}, u32[]{:S(2)}) async-start(bf16[8,64,128]{2,1,0:T(8,128)(2,1)} %merge.1), calls=%async_computation.3 | async-start | bytes 262144 | tf_op jit(solution)/shard_map/all_to_all | solution.py:319
  72.7 0.1 pad_maximum_fusion.1
  72.8 3.3 %collective-permute-start.5 = (bf16[32,256]{1,0:T(8,128)(2,1)S(1)}, bf16[32,256]{1,0:T(8,128)(2,1)S(1)}, u32[]{:S(2)}, u32[]{:S(2)}) collective-permute-start(bf16[32,256]{1,0:T(8,128)(2,1)S(1)} %pad_maximum_fusion.1), channel_id=1, source_target_pairs={{0,4},{2,6},{4,0},{6,2},{1,5},{3,7},{5,1},{7,3},{8,12},{10,14},{12... | collective-permute-start | bytes 49160 | tf_op jit(solution)/shard_map/ppermute | solution.py:266
  76.1 3.8 %collective-permute-done.5.eight_ref = bf16[32,256]{1,0:T(8,128)(2,1)S(1)} collective-permute-done((bf16[32,256]{1,0:T(8,128)(2,1)S(1)}, bf16[32,256]{1,0:T(8,128)(2,1)S(1)}, u32[]{:S(2)}, u32[]{:S(2)}) %collective-permute-start.5) | collective-permute-done | bytes 16416 | tf_op jit(solution)/shard_map/ppermute | solution.py:266
  79.9 0.4 spread.3.spread_ref
  80.4 0.8 last.1
  (25 shorter events, 0.1 us)
Async XLA Ops:
  3.4 15.2 %all-to-all-start = ((bf16[8,272,128]{2,1,0:T(8,128)(2,1)}), bf16[8,272,128]{2,1,0:T(8,128)(2,1)S(1)}, u32[]{:S(2)}, u32[]{:S(2)}) async-start(bf16[8,272,128]{2,1,0:T(8,128)(2,1)} %get-tuple-element.20), calls=%async_computation | async-start | bytes 1114112 | tf_op jit(solution)/shard_map/all_to_all | solution.py:303
  9.7 3.2 %collective-permute-start = (bf16[80,640]{1,0:T(8,128)(2,1)S(1)}, bf16[80,640]{1,0:T(8,128)(2,1)S(1)}, u32[]{:S(2)}, u32[]{:S(2)}) collective-permute-start(bf16[80,640]{1,0:T(8,128)(2,1)S(1)} %get-tuple-element.21), channel_id=1, source_target_pairs={{0,1},{1,0},{2,3},{3,2},{4,5},{5,4},{6,7},{7,6},{8,9},{9,8},{10,11... | collective-permute-start | bytes 307208 | tf_op jit(solution)/shard_map/ppermute | solution.py:266
  12.9 3.0 %copy-start.5 = (f32[7,512]{1,0:T(8,128)S(1)}, f32[7,512]{1,0:T(8,128)}, u32[]{:S(2)}) copy-start(f32[7,512]{1,0:T(8,128)} %own_ref.1) | copy-start | bytes 43012
  12.9 3.0 %copy-start.7 = (s32[4,8]{1,0:T(4,128)S(1)}, s32[4,8]{1,0:T(4,128)}, u32[]{:S(2)}) copy-start(s32[4,8]{1,0:T(4,128)} %mask_ref.1) | copy-start | bytes 388
  12.9 4.6 %copy-start.4 = (bf16[32,512]{1,0:T(8,128)(2,1)S(1)}, bf16[32,512]{1,0:T(8,128)(2,1)}, u32[]{:S(2)}) copy-start(bf16[32,512]{1,0:T(8,128)(2,1)} %value_ref.1) | copy-start | bytes 98308
  12.9 5.7 %collective-permute-start.1 = (bf16[32,128]{1,0:T(8,128)(2,1)S(1)}, bf16[32,128]{1,0:T(8,128)(2,1)S(1)}, u32[]{:S(2)}, u32[]{:S(2)}) collective-permute-start(bf16[32,128]{1,0:T(8,128)(2,1)S(1)} %pad_maximum_fusion.2.two_ref), channel_id=1, source_target_pairs={{0,2},{2,0},{4,6},{6,4},{1,3},{3,1},{5,7},{7,5},{8,10},{10,8},{12,... | collective-permute-start | bytes 24584 | tf_op jit(solution)/shard_map/ppermute | solution.py:266
  17.6 25.5 %copy-start = (bf16[64,64,64]{2,1,0:T(8,128)(2,1)S(1)}, bf16[64,64,64]{2,1,0:T(8,128)(2,1)}, u32[]{:S(2)}) copy-start(bf16[64,64,64]{2,1,0:T(8,128)(2,1)} %coupling_ref.1) | copy-start | bytes 1572868
  19.5 19.3 %copy-start.8 = (bf16[1,512,64]{1,2,0:T(8,128)(2,1)S(1)}, bf16[1,512,64]{1,2,0:T(8,128)(2,1)}, u32[]{:S(2)}) copy-start(bf16[1,512,64]{1,2,0:T(8,128)(2,1)} %param.16) | copy-start | bytes 196612
  19.5 23.6 %all-to-all-start.1 = ((bf16[8,64,128]{2,1,0:T(8,128)(2,1)}), bf16[8,64,128]{2,1,0:T(8,128)(2,1)S(1)}, u32[]{:S(2)}, u32[]{:S(2)}) async-start(bf16[8,64,128]{2,1,0:T(8,128)(2,1)} %get-tuple-element.25), calls=%async_computation.1 | async-start | bytes 262144 | tf_op jit(solution)/shard_map/all_to_all | solution.py:319
  35.4 7.3 %copy-start.1 = (bf16[4,64,64]{2,1,0:T(8,128)(2,1)S(1)}, bf16[4,64,64]{2,1,0:T(8,128)(2,1)}, u32[]{:S(2)}) copy-start(bf16[4,64,64]{2,1,0:T(8,128)(2,1)} %transfer_ref.5) | copy-start | bytes 98308
  35.4 7.3 %collective-permute-start.2 = (bf16[32,256]{1,0:T(8,128)(2,1)S(1)}, bf16[32,256]{1,0:T(8,128)(2,1)S(1)}, u32[]{:S(2)}, u32[]{:S(2)}) collective-permute-start(bf16[32,256]{1,0:T(8,128)(2,1)S(1)} %pad_maximum_fusion), channel_id=1, source_target_pairs={{0,4},{2,6},{4,0},{6,2},{1,5},{3,7},{5,1},{7,3},{8,12},{10,14},{12... | collective-permute-start | bytes 49160 | tf_op jit(solution)/shard_map/ppermute | solution.py:266
  39.0 4.2 %copy-start.2 = (bf16[64,512]{1,0:T(8,128)(2,1)S(1)}, bf16[64,512]{1,0:T(8,128)(2,1)}, u32[]{:S(2)}) copy-start(bf16[64,512]{1,0:T(8,128)(2,1)} %target_ref.3) | copy-start | bytes 196612
  39.0 4.2 %copy-start.3 = (bf16[64,512]{1,0:T(8,128)(2,1)S(1)}, bf16[64,512]{1,0:T(8,128)(2,1)}, u32[]{:S(2)}) copy-start(bf16[64,512]{1,0:T(8,128)(2,1)} %basis_ref.1) | copy-start | bytes 196612
  45.3 14.6 %all-to-all-start.2 = ((bf16[8,256,128]{2,1,0:T(8,128)(2,1)}), bf16[8,256,128]{2,1,0:T(8,128)(2,1)S(1)}, u32[]{:S(2)}, u32[]{:S(2)}) async-start(bf16[8,256,128]{2,1,0:T(8,128)(2,1)} %get-tuple-element.30), calls=%async_computation.2 | async-start | bytes 1048576 | tf_op jit(solution)/shard_map/all_to_all | solution.py:303
  51.0 6.1 %copy-start.6 = (bf16[32,512]{1,0:T(8,128)(2,1)S(1)}, bf16[32,512]{1,0:T(8,128)(2,1)}, u32[]{:S(2)}) copy-start(bf16[32,512]{1,0:T(8,128)(2,1)} %get-tuple-element.18.value_ref) | copy-start | bytes 98308
  51.0 3.2 %collective-permute-start.3 = (bf16[32,640]{1,0:T(8,128)(2,1)S(1)}, bf16[32,640]{1,0:T(8,128)(2,1)S(1)}, u32[]{:S(2)}, u32[]{:S(2)}) collective-permute-start(bf16[32,640]{1,0:T(8,128)(2,1)S(1)} %get-tuple-element.31), channel_id=1, source_target_pairs={{0,1},{1,0},{2,3},{3,2},{4,5},{5,4},{6,7},{7,6},{8,9},{9,8},{10,11... | collective-permute-start | bytes 122888 | tf_op jit(solution)/shard_map/ppermute | solution.py:266
  54.3 5.5 %collective-permute-start.4 = (bf16[32,128]{1,0:T(8,128)(2,1)S(1)}, bf16[32,128]{1,0:T(8,128)(2,1)S(1)}, u32[]{:S(2)}, u32[]{:S(2)}) collective-permute-start(bf16[32,128]{1,0:T(8,128)(2,1)S(1)} %pad_maximum_fusion.3.two_ref), channel_id=1, source_target_pairs={{0,2},{2,0},{4,6},{6,4},{1,3},{3,1},{5,7},{7,5},{8,10},{10,8},{12,... | collective-permute-start | bytes 24584 | tf_op jit(solution)/shard_map/ppermute | solution.py:266
  60.7 19.7 %all-to-all-start.3 = ((bf16[8,64,128]{2,1,0:T(8,128)(2,1)}), bf16[8,64,128]{2,1,0:T(8,128)(2,1)S(1)}, u32[]{:S(2)}, u32[]{:S(2)}) async-start(bf16[8,64,128]{2,1,0:T(8,128)(2,1)} %merge.1), calls=%async_computation.3 | async-start | bytes 262144 | tf_op jit(solution)/shard_map/all_to_all | solution.py:319
  72.8 7.1 %collective-permute-start.5 = (bf16[32,256]{1,0:T(8,128)(2,1)S(1)}, bf16[32,256]{1,0:T(8,128)(2,1)S(1)}, u32[]{:S(2)}, u32[]{:S(2)}) collective-permute-start(bf16[32,256]{1,0:T(8,128)(2,1)S(1)} %pad_maximum_fusion.1), channel_id=1, source_target_pairs={{0,4},{2,6},{4,0},{6,2},{1,5},{3,7},{5,1},{7,3},{8,12},{10,14},{12... | collective-permute-start | bytes 49160 | tf_op jit(solution)/shard_map/ppermute | solution.py:266

commit v8 on v7

--- a/solution.py
+++ b/solution.py
@@ -22,6 +22,7 @@
 IDS = 16
 FIRST_PAIR = 5
 ORDER = [(FIRST_PAIR + i) % NA for i in range(NA)]
+LATER_ORDER = [(4 + i) % NA for i in range(NA)]
 PARTS = 3
 F32, BF16 = jnp.float32, jnp.bfloat16
 NT = (((1,), (1,)), ((), ()))
@@ -135,8 +136,8 @@
         product(block, place_ref, coupling_ref, coeff_ref, send_ref)
 
 
-def merge(recv_ref, choice_ref, out_ref):
-    for place, pair in enumerate(ORDER):
+def merge(recv_ref, choice_ref, out_ref, order):
+    for place, pair in enumerate(order):
         blocks = [recv_ref[src, pair * 2 * ROWS : (pair + 1) * 2 * ROWS, :] for src in range(PEERS)]
         out_ref[place] = dot(choice_ref[pair], jnp.concatenate(blocks, axis=0)).astype(BF16)
 
@@ -158,11 +159,11 @@
     for pair in range(NA):
         here = jnp.broadcast_to(ids[pair : pair + 1, :], dims)
         choice_ref[pair] = jnp.where(here == wanted, 1.0, 0.0).astype(BF16)
-    merge(recv_ref, choice_ref, out_ref)
+    merge(recv_ref, choice_ref, out_ref, ORDER)
 
 
 def merge_body(recv_ref, choice_ref, out_ref):
-    merge(recv_ref, choice_ref, out_ref)
+    merge(recv_ref, choice_ref, out_ref, LATER_ORDER)
 
 
 def kernel_body(own_ref, packet_ref, mask_ref, kernel_ref, other_ref):
@@ -205,7 +206,7 @@
     me = lax.axis_index("x") * NC + lax.axis_index("c")
     down = jnp.zeros((RIGHT_SIDES, RANK), F32)
     pairs = [two_ref[...], four_ref[...], eight_ref[:, :128], eight_ref[:, 128:]]
-    for step, pair in enumerate(pairs):
+    for step, pair in zip((0, 1, 3, 2), pairs):
         rows = [
             rows_ref[0, pl.ds(pl.multiple_of(jnp.bitwise_xor(me, 2 * step + turn) * RANK, RANK), RANK), :]
             for turn in range(2)
@@ -312,12 +313,14 @@
         base = nearby(value, other, kernel)[0]
         arrived, four, base = together(arrived, four, base)
         if choice is None:
+            order = ORDER
             merged, choice = first_merge(arrived)
         else:
+            order = LATER_ORDER
             merged = next_merge(arrived, choice)[0]
         merged, four = together(merged, four)
-        received = lax.all_to_all(merged, "a", 0, 0, axis_index_groups=[ORDER], tiled=True)
-        eight = swap(jnp.concatenate([two, four], axis=1), "x", 2)
+        received = lax.all_to_all(merged, "a", 0, 0, axis_index_groups=[order], tiled=True)
+        eight = swap(jnp.concatenate([two, four], axis=1), "x", 3)
         spread = spreading(two, four, eight, cluster_coupling, leaf_transfer)[0]
         return received, base, spread, choice, kernel
 

time: 82 us -> 81.4 us (level)
  starting transfers between devices: 56.1 us -> 53.4 us
  waiting for transfers between devices: 13.1 us -> 15.2 us
    ppermute x6, starting transfers between devices: 16.3 us -> 13.8 us  [swap(): return lax.ppermute(block, axis, [(i, i ^ distance) for i in range(count)])]
    ppermute x6, waiting for transfers between devices: 13.1 us -> 15 us  [swap(): return lax.ppermute(block, axis, [(i, i ^ distance) for i in range(count)])]
  transfers between devices with their start and end apart: 10 -> 10, of which waited for: 6 -> 7; matrix products, arithmetic and copies ran while one was open for 1% -> 1% of each run, Pallas kernels for 4% -> 4%
where the time goes in v8:
time: 81.4 us; the launch traced here: 80.6 us
  starting transfers between devices  53.4 us (66%)
  waiting for transfers between devices  15.2 us (19%)
  Pallas kernels  10.7 us (13%)
    all_to_all x2, starting transfers between devices, couple(): lax.all_to_all(merged, 'a', 0, 0, axis_index_groups=[order], tiled=True)  27.8 us
    ppermute x6, waiting for transfers between devices, swap(): return lax.ppermute(block, axis, [(i, i ^ distance) for i in range(count)])  15 us
    ppermute x6, starting transfers between devices, swap(): return lax.ppermute(block, axis, [(i, i ^ distance) for i in range(count)])  13.8 us
    all_to_all x2, starting transfers between devices, couple(): arrived = lax.all_to_all(send, ('b', 'y'), 0, 0, tiled=True)  11.8 us
    pallas_call x1, Pallas kernels, shards(): first(*[pltpu.with_memory_space_constraint(array, pltpu.HBM) for array in...  2.74 us
    pallas_call x1, Pallas kernels, shards(): call(middle_body, 'middle', [values, shape(PEERS, CHUNK, 128), shape(RIGH...  2.17 us
    pallas_call x1, Pallas kernels, couple(): call(kernel_body, 'kernel', [shape(panels_here, 2 * panels_here)], [VM, V...  1.72 us
  transfers between devices with their start and end apart: 10, of which 7 were waited for; matrix products, arithmetic and copies ran while one was open for 1% of the time, Pallas kernels for 4%

profile of v8, /device:TPU:14, one launch (start us, length us, event | category | flops | bytes accessed | tf_op | source)
XLA Modules:
  0.0 80.6 jit_solution(7711019409467349539)
XLA Ops:
  0.6 2.7 %first.1 = (bf16[8,272,128]{2,1,0:T(8,128)(2,1)}, bf16[80,640]{1,0:T(8,128)(2,1)S(1)}, s32[128]{0:T(128)S(1)}) custom-call(s32[64]{0:T(128)} %leaf_hbm.1, s32[64]{0:T(128)} %bitcast.1, s32[64]{0:T(128)} %target_hbm.1, f32[7,512]{1,0:T(8,128)} %own_ref.1, bf16[32,512]{1,0:T(8,128)(2,1)} %value_ref.1, bf16[64,512]{1,0:T(8,128)(2,1)} %basis_ref.1, ...), custom_call_target="tpu_custom_call" | custom-call | tf_op jit(solution)/shard_map/first/pallas_call | solution.py:330
  3.4 6.3 %all-to-all-start = ((bf16[8,272,128]{2,1,0:T(8,128)(2,1)}), bf16[8,272,128]{2,1,0:T(8,128)(2,1)S(1)}, u32[]{:S(2)}, u32[]{:S(2)}) async-start(bf16[8,272,128]{2,1,0:T(8,128)(2,1)} %get-tuple-element.20), calls=%async_computation | async-start | bytes 1114112 | tf_op jit(solution)/shard_map/all_to_all | solution.py:304
  9.7 1.9 %collective-permute-start = (bf16[80,640]{1,0:T(8,128)(2,1)S(1)}, bf16[80,640]{1,0:T(8,128)(2,1)S(1)}, u32[]{:S(2)}, u32[]{:S(2)}) collective-permute-start(bf16[80,640]{1,0:T(8,128)(2,1)S(1)} %get-tuple-element.21), channel_id=1, source_target_pairs={{0,1},{1,0},{2,3},{3,2},{4,5},{5,4},{6,7},{7,6},{8,9},{9,8},{10,11... | collective-permute-start | bytes 307208 | tf_op jit(solution)/shard_map/ppermute | solution.py:267
  11.6 1.3 %collective-permute-done.packet_ref.other_ref = bf16[80,640]{1,0:T(8,128)(2,1)S(1)} collective-permute-done((bf16[80,640]{1,0:T(8,128)(2,1)S(1)}, bf16[80,640]{1,0:T(8,128)(2,1)S(1)}, u32[]{:S(2)}, u32[]{:S(2)}) %collective-permute-start) | collective-permute-done | bytes 102432 | tf_op jit(solution)/shard_map/ppermute | solution.py:267
  12.9 0.1 pad_maximum_fusion.2.two_ref
  12.9 2.9 %collective-permute-start.1 = (bf16[32,128]{1,0:T(8,128)(2,1)S(1)}, bf16[32,128]{1,0:T(8,128)(2,1)S(1)}, u32[]{:S(2)}, u32[]{:S(2)}) collective-permute-start(bf16[32,128]{1,0:T(8,128)(2,1)S(1)} %pad_maximum_fusion.2.two_ref), channel_id=1, source_target_pairs={{0,2},{2,0},{4,6},{6,4},{1,3},{3,1},{5,7},{7,5},{8,10},{10,8},{12,... | collective-permute-start | bytes 24584 | tf_op jit(solution)/shard_map/ppermute | solution.py:267
  15.8 1.7 %kernel.1.kernel_ref = bf16[512,1024]{1,0:T(8,128)(2,1)S(1)} custom-call(f32[7,512]{1,0:T(8,128)S(1)} %copy-done.5, bf16[80,640]{1,0:T(8,128)(2,1)S(1)} %collective-permute-done.packet_ref.other_ref, s32[4,8]{1,0:T(4,128)S(1)} %copy-done.7), custom_call_target="tpu_custom_call" | custom-call | tf_op jit(solution)/shard_map/kernel/pallas_call | solution.py:309
  17.6 0.3 nearby.2.base_ref
  17.9 0.7 collective-permute-done.1.four_ref
  18.6 0.9 %first_merge.1 = (bf16[8,64,128]{2,1,0:T(8,128)(2,1)}, bf16[8,64,256]{2,1,0:T(8,128)(2,1)S(1)}) custom-call(bf16[8,272,128]{2,1,0:T(8,128)(2,1)S(1)} %all-to-all-done.recv_ref), custom_call_target="tpu_custom_call" | custom-call | tf_op jit(solution)/shard_map/first_merge/pallas_call | solution.py:317
  19.5 15.8 %all-to-all-start.1 = ((bf16[8,64,128]{2,1,0:T(8,128)(2,1)}), bf16[8,64,128]{2,1,0:T(8,128)(2,1)S(1)}, u32[]{:S(2)}, u32[]{:S(2)}) async-start(bf16[8,64,128]{2,1,0:T(8,128)(2,1)} %get-tuple-element.25), calls=%async_computation.1 | async-start | bytes 262144 | tf_op jit(solution)/shard_map/all_to_all | solution.py:322
  35.3 0.1 pad_maximum_fusion
  35.4 2.5 %collective-permute-start.2 = (bf16[32,256]{1,0:T(8,128)(2,1)S(1)}, bf16[32,256]{1,0:T(8,128)(2,1)S(1)}, u32[]{:S(2)}, u32[]{:S(2)}) collective-permute-start(bf16[32,256]{1,0:T(8,128)(2,1)S(1)} %pad_maximum_fusion), channel_id=1, source_target_pairs={{0,6},{2,4},{4,2},{6,0},{1,7},{3,5},{5,3},{7,1},{8,14},{10,12},{12... | collective-permute-start | bytes 49160 | tf_op jit(solution)/shard_map/ppermute | solution.py:267
  37.9 0.1 copy.13.rows_ref
  38.0 4.3 %collective-permute-done.2.eight_ref = bf16[32,256]{1,0:T(8,128)(2,1)S(1)} collective-permute-done((bf16[32,256]{1,0:T(8,128)(2,1)S(1)}, bf16[32,256]{1,0:T(8,128)(2,1)S(1)}, u32[]{:S(2)}, u32[]{:S(2)}) %collective-permute-start.2) | collective-permute-done | bytes 16416 | tf_op jit(solution)/shard_map/ppermute | solution.py:267
  42.3 0.4 spread.2.spread_ref
  42.8 0.3 all-to-all-done.1.recv_ref
  43.1 2.2 %middle.1 = (bf16[32,512]{1,0:T(8,128)(2,1)}, bf16[8,256,128]{2,1,0:T(8,128)(2,1)}, bf16[32,640]{1,0:T(8,128)(2,1)S(1)}) custom-call(bf16[8,64,128]{2,1,0:T(8,128)(2,1)S(1)} %all-to-all-done.1.recv_ref, f32[64,128]{1,0:T(8,128)S(1)} %spread.2.spread_ref, f32[32,512]{1,0:T(8,128)S(1)} %nearby.2.base_ref, bf16[64,512]{1,0:T(8,128)(2,1)S(1)} %copy-done.2, ...), custom_call_target="tpu_custom_call" | custom-call | tf_op jit(solution)/shard_map/middle/pallas_call | solution.py:332
  45.2 5.5 %all-to-all-start.2 = ((bf16[8,256,128]{2,1,0:T(8,128)(2,1)}), bf16[8,256,128]{2,1,0:T(8,128)(2,1)S(1)}, u32[]{:S(2)}, u32[]{:S(2)}) async-start(bf16[8,256,128]{2,1,0:T(8,128)(2,1)} %get-tuple-element.30), calls=%async_computation.2 | async-start | bytes 1048576 | tf_op jit(solution)/shard_map/all_to_all | solution.py:304
  50.7 2.0 %collective-permute-start.3 = (bf16[32,640]{1,0:T(8,128)(2,1)S(1)}, bf16[32,640]{1,0:T(8,128)(2,1)S(1)}, u32[]{:S(2)}, u32[]{:S(2)}) collective-permute-start(bf16[32,640]{1,0:T(8,128)(2,1)S(1)} %get-tuple-element.31), channel_id=1, source_target_pairs={{0,1},{1,0},{2,3},{3,2},{4,5},{5,4},{6,7},{7,6},{8,9},{9,8},{10,11... | collective-permute-start | bytes 122888 | tf_op jit(solution)/shard_map/ppermute | solution.py:267
  52.8 1.2 %collective-permute-done.3.other_ref = bf16[32,640]{1,0:T(8,128)(2,1)S(1)} collective-permute-done((bf16[32,640]{1,0:T(8,128)(2,1)S(1)}, bf16[32,640]{1,0:T(8,128)(2,1)S(1)}, u32[]{:S(2)}, u32[]{:S(2)}) %collective-permute-start.3) | collective-permute-done | bytes 40992 | tf_op jit(solution)/shard_map/ppermute | solution.py:267
  53.9 0.1 pad_maximum_fusion.3.two_ref
  54.0 2.2 %collective-permute-start.4 = (bf16[32,128]{1,0:T(8,128)(2,1)S(1)}, bf16[32,128]{1,0:T(8,128)(2,1)S(1)}, u32[]{:S(2)}, u32[]{:S(2)}) collective-permute-start(bf16[32,128]{1,0:T(8,128)(2,1)S(1)} %pad_maximum_fusion.3.two_ref), channel_id=1, source_target_pairs={{0,2},{2,0},{4,6},{6,4},{1,3},{3,1},{5,7},{7,5},{8,10},{10,8},{12,... | collective-permute-start | bytes 24584 | tf_op jit(solution)/shard_map/ppermute | solution.py:267
  56.2 0.3 nearby.3.base_ref
  56.5 3.1 %collective-permute-done.4.four_ref = bf16[32,128]{1,0:T(8,128)(2,1)S(1)} collective-permute-done((bf16[32,128]{1,0:T(8,128)(2,1)S(1)}, bf16[32,128]{1,0:T(8,128)(2,1)S(1)}, u32[]{:S(2)}, u32[]{:S(2)}) %collective-permute-start.4) | collective-permute-done | bytes 8224 | tf_op jit(solution)/shard_map/ppermute | solution.py:267
  59.6 0.9 %merge.1 = bf16[8,64,128]{2,1,0:T(8,128)(2,1)} custom-call(bf16[8,256,128]{2,1,0:T(8,128)(2,1)S(1)} %all-to-all-done.2.recv_ref, bf16[8,64,256]{2,1,0:T(8,128)(2,1)S(1)} %get-tuple-element.33.choice_ref), custom_call_target="tpu_custom_call" | custom-call | tf_op jit(solution)/shard_map/merge/pallas_call | solution.py:320
  60.4 12.0 %all-to-all-start.3 = ((bf16[8,64,128]{2,1,0:T(8,128)(2,1)}), bf16[8,64,128]{2,1,0:T(8,128)(2,1)S(1)}, u32[]{:S(2)}, u32[]{:S(2)}) async-start(bf16[8,64,128]{2,1,0:T(8,128)(2,1)} %merge.1), calls=%async_computation.3 | async-start | bytes 262144 | tf_op jit(solution)/shard_map/all_to_all | solution.py:322
  72.4 0.1 pad_maximum_fusion.1
  72.5 2.4 %collective-permute-start.5 = (bf16[32,256]{1,0:T(8,128)(2,1)S(1)}, bf16[32,256]{1,0:T(8,128)(2,1)S(1)}, u32[]{:S(2)}, u32[]{:S(2)}) collective-permute-start(bf16[32,256]{1,0:T(8,128)(2,1)S(1)} %pad_maximum_fusion.1), channel_id=1, source_target_pairs={{0,6},{2,4},{4,2},{6,0},{1,7},{3,5},{5,3},{7,1},{8,14},{10,12},{12... | collective-permute-start | bytes 49160 | tf_op jit(solution)/shard_map/ppermute | solution.py:267
  74.9 4.5 %collective-permute-done.5.eight_ref = bf16[32,256]{1,0:T(8,128)(2,1)S(1)} collective-permute-done((bf16[32,256]{1,0:T(8,128)(2,1)S(1)}, bf16[32,256]{1,0:T(8,128)(2,1)S(1)}, u32[]{:S(2)}, u32[]{:S(2)}) %collective-permute-start.5) | collective-permute-done | bytes 16416 | tf_op jit(solution)/shard_map/ppermute | solution.py:267
  79.4 0.4 spread.3.spread_ref
  79.8 0.8 last.1
  (25 shorter events, 0.1 us)
Async XLA Ops:
  3.4 15.2 %all-to-all-start = ((bf16[8,272,128]{2,1,0:T(8,128)(2,1)}), bf16[8,272,128]{2,1,0:T(8,128)(2,1)S(1)}, u32[]{:S(2)}, u32[]{:S(2)}) async-start(bf16[8,272,128]{2,1,0:T(8,128)(2,1)} %get-tuple-element.20), calls=%async_computation | async-start | bytes 1114112 | tf_op jit(solution)/shard_map/all_to_all | solution.py:304
  9.7 3.2 %collective-permute-start = (bf16[80,640]{1,0:T(8,128)(2,1)S(1)}, bf16[80,640]{1,0:T(8,128)(2,1)S(1)}, u32[]{:S(2)}, u32[]{:S(2)}) collective-permute-start(bf16[80,640]{1,0:T(8,128)(2,1)S(1)} %get-tuple-element.21), channel_id=1, source_target_pairs={{0,1},{1,0},{2,3},{3,2},{4,5},{5,4},{6,7},{7,6},{8,9},{9,8},{10,11... | collective-permute-start | bytes 307208 | tf_op jit(solution)/shard_map/ppermute | solution.py:267
  12.9 3.0 %copy-start.5 = (f32[7,512]{1,0:T(8,128)S(1)}, f32[7,512]{1,0:T(8,128)}, u32[]{:S(2)}) copy-start(f32[7,512]{1,0:T(8,128)} %own_ref.1) | copy-start | bytes 43012
  12.9 3.0 %copy-start.7 = (s32[4,8]{1,0:T(4,128)S(1)}, s32[4,8]{1,0:T(4,128)}, u32[]{:S(2)}) copy-start(s32[4,8]{1,0:T(4,128)} %mask_ref.1) | copy-start | bytes 388
  12.9 4.6 %copy-start.4 = (bf16[32,512]{1,0:T(8,128)(2,1)S(1)}, bf16[32,512]{1,0:T(8,128)(2,1)}, u32[]{:S(2)}) copy-start(bf16[32,512]{1,0:T(8,128)(2,1)} %value_ref.1) | copy-start | bytes 98308
  12.9 5.7 %collective-permute-start.1 = (bf16[32,128]{1,0:T(8,128)(2,1)S(1)}, bf16[32,128]{1,0:T(8,128)(2,1)S(1)}, u32[]{:S(2)}, u32[]{:S(2)}) collective-permute-start(bf16[32,128]{1,0:T(8,128)(2,1)S(1)} %pad_maximum_fusion.2.two_ref), channel_id=1, source_target_pairs={{0,2},{2,0},{4,6},{6,4},{1,3},{3,1},{5,7},{7,5},{8,10},{10,8},{12,... | collective-permute-start | bytes 24584 | tf_op jit(solution)/shard_map/ppermute | solution.py:267
  17.6 25.5 %copy-start = (bf16[64,64,64]{2,1,0:T(8,128)(2,1)S(1)}, bf16[64,64,64]{2,1,0:T(8,128)(2,1)}, u32[]{:S(2)}) copy-start(bf16[64,64,64]{2,1,0:T(8,128)(2,1)} %coupling_ref.1) | copy-start | bytes 1572868
  19.5 18.4 %copy-start.8 = (bf16[1,512,64]{1,2,0:T(8,128)(2,1)S(1)}, bf16[1,512,64]{1,2,0:T(8,128)(2,1)}, u32[]{:S(2)}) copy-start(bf16[1,512,64]{1,2,0:T(8,128)(2,1)} %param.16) | copy-start | bytes 196612
  19.5 23.6 %all-to-all-start.1 = ((bf16[8,64,128]{2,1,0:T(8,128)(2,1)}), bf16[8,64,128]{2,1,0:T(8,128)(2,1)S(1)}, u32[]{:S(2)}, u32[]{:S(2)}) async-start(bf16[8,64,128]{2,1,0:T(8,128)(2,1)} %get-tuple-element.25), calls=%async_computation.1 | async-start | bytes 262144 | tf_op jit(solution)/shard_map/all_to_all | solution.py:322
  35.4 7.0 %copy-start.1 = (bf16[4,64,64]{2,1,0:T(8,128)(2,1)S(1)}, bf16[4,64,64]{2,1,0:T(8,128)(2,1)}, u32[]{:S(2)}) copy-start(bf16[4,64,64]{2,1,0:T(8,128)(2,1)} %transfer_ref.5) | copy-start | bytes 98308
  35.4 7.0 %collective-permute-start.2 = (bf16[32,256]{1,0:T(8,128)(2,1)S(1)}, bf16[32,256]{1,0:T(8,128)(2,1)S(1)}, u32[]{:S(2)}, u32[]{:S(2)}) collective-permute-start(bf16[32,256]{1,0:T(8,128)(2,1)S(1)} %pad_maximum_fusion), channel_id=1, source_target_pairs={{0,6},{2,4},{4,2},{6,0},{1,7},{3,5},{5,3},{7,1},{8,14},{10,12},{12... | collective-permute-start | bytes 49160 | tf_op jit(solution)/shard_map/ppermute | solution.py:267
  38.0 5.0 %copy-start.2 = (bf16[64,512]{1,0:T(8,128)(2,1)S(1)}, bf16[64,512]{1,0:T(8,128)(2,1)}, u32[]{:S(2)}) copy-start(bf16[64,512]{1,0:T(8,128)(2,1)} %target_ref.3) | copy-start | bytes 196612
  38.0 5.0 %copy-start.3 = (bf16[64,512]{1,0:T(8,128)(2,1)S(1)}, bf16[64,512]{1,0:T(8,128)(2,1)}, u32[]{:S(2)}) copy-start(bf16[64,512]{1,0:T(8,128)(2,1)} %basis_ref.1) | copy-start | bytes 196612
  45.2 14.3 %all-to-all-start.2 = ((bf16[8,256,128]{2,1,0:T(8,128)(2,1)}), bf16[8,256,128]{2,1,0:T(8,128)(2,1)S(1)}, u32[]{:S(2)}, u32[]{:S(2)}) async-start(bf16[8,256,128]{2,1,0:T(8,128)(2,1)} %get-tuple-element.30), calls=%async_computation.2 | async-start | bytes 1048576 | tf_op jit(solution)/shard_map/all_to_all | solution.py:304
  50.7 5.5 %copy-start.6 = (bf16[32,512]{1,0:T(8,128)(2,1)S(1)}, bf16[32,512]{1,0:T(8,128)(2,1)}, u32[]{:S(2)}) copy-start(bf16[32,512]{1,0:T(8,128)(2,1)} %get-tuple-element.18.value_ref) | copy-start | bytes 98308
  50.7 3.2 %collective-permute-start.3 = (bf16[32,640]{1,0:T(8,128)(2,1)S(1)}, bf16[32,640]{1,0:T(8,128)(2,1)S(1)}, u32[]{:S(2)}, u32[]{:S(2)}) collective-permute-start(bf16[32,640]{1,0:T(8,128)(2,1)S(1)} %get-tuple-element.31), channel_id=1, source_target_pairs={{0,1},{1,0},{2,3},{3,2},{4,5},{5,4},{6,7},{7,6},{8,9},{9,8},{10,11... | collective-permute-start | bytes 122888 | tf_op jit(solution)/shard_map/ppermute | solution.py:267
  54.0 5.5 %collective-permute-start.4 = (bf16[32,128]{1,0:T(8,128)(2,1)S(1)}, bf16[32,128]{1,0:T(8,128)(2,1)S(1)}, u32[]{:S(2)}, u32[]{:S(2)}) collective-permute-start(bf16[32,128]{1,0:T(8,128)(2,1)S(1)} %pad_maximum_fusion.3.two_ref), channel_id=1, source_target_pairs={{0,2},{2,0},{4,6},{6,4},{1,3},{3,1},{5,7},{7,5},{8,10},{10,8},{12,... | collective-permute-start | bytes 24584 | tf_op jit(solution)/shard_map/ppermute | solution.py:267
  60.4 19.4 %all-to-all-start.3 = ((bf16[8,64,128]{2,1,0:T(8,128)(2,1)}), bf16[8,64,128]{2,1,0:T(8,128)(2,1)S(1)}, u32[]{:S(2)}, u32[]{:S(2)}) async-start(bf16[8,64,128]{2,1,0:T(8,128)(2,1)} %merge.1), calls=%async_computation.3 | async-start | bytes 262144 | tf_op jit(solution)/shard_map/all_to_all | solution.py:322
  72.5 6.8 %collective-permute-start.5 = (bf16[32,256]{1,0:T(8,128)(2,1)S(1)}, bf16[32,256]{1,0:T(8,128)(2,1)S(1)}, u32[]{:S(2)}, u32[]{:S(2)}) collective-permute-start(bf16[32,256]{1,0:T(8,128)(2,1)S(1)} %pad_maximum_fusion.1), channel_id=1, source_target_pairs={{0,6},{2,4},{4,2},{6,0},{1,7},{3,5},{5,3},{7,1},{8,14},{10,12},{12... | collective-permute-start | bytes 49160 | tf_op jit(solution)/shard_map/ppermute | solution.py:267

commit v9 on v8

--- a/solution.py
+++ b/solution.py
@@ -202,7 +202,7 @@
         base_ref[:, leaf_cols(leaf)] = near + 0.5 * value_ref[:, leaf_cols(leaf)].astype(F32)
 
 
-def spread_body(two_ref, four_ref, eight_ref, rows_ref, transfer_ref, spread_ref):
+def spread_blocks(two_ref, four_ref, eight_ref, rows_ref, transfer_ref):
     me = lax.axis_index("x") * NC + lax.axis_index("c")
     down = jnp.zeros((RIGHT_SIDES, RANK), F32)
     pairs = [two_ref[...], four_ref[...], eight_ref[:, :128], eight_ref[:, 128:]]
@@ -214,13 +214,17 @@
         down += dot(pair, jnp.concatenate(rows, axis=0))
     high = down.astype(BF16)
     low = (down - high.astype(F32)).astype(BF16)
-    for leaf in range(LEAVES):
-        spread = dot(high, transfer_ref[leaf], NT) + dot(low, transfer_ref[leaf], NT)
-        spread_ref[leaf * ROWS : (leaf + 1) * ROWS, :] = pack(spread)
-
-
-def finish(recv_ref, spread_ref, base_ref, target_ref, out_ref):
-    field = spread_ref[...]
+    blocks = []
+    for leaf in range(LEAVES):
+        blocks.append(pack(dot(high, transfer_ref[leaf], NT) + dot(low, transfer_ref[leaf], NT)))
+    return jnp.concatenate(blocks, axis=0)
+
+
+def spread_body(two_ref, four_ref, eight_ref, rows_ref, transfer_ref, spread_ref):
+    spread_ref[...] = spread_blocks(two_ref, four_ref, eight_ref, rows_ref, transfer_ref)
+
+
+def finish(recv_ref, field, base_ref, target_ref, out_ref):
     for src in range(NA):
         field += recv_ref[src].astype(F32)
     field = field.astype(BF16)
@@ -237,15 +241,16 @@
     recv_ref, spread_ref, base_ref, target_ref, place_ref, basis_ref, transfer_ref, coupling_ref,
     out_ref, send_ref, swap_ref, coeff_ref,
 ):
-    finish(recv_ref, spread_ref, base_ref, target_ref, out_ref)
+    finish(recv_ref, spread_ref[...], base_ref, target_ref, out_ref)
     clear(send_ref)
     leaf_coeffs(out_ref, basis_ref, transfer_ref, swap_ref, coeff_ref)
     for block in range(OUTS):
         product(block, place_ref, coupling_ref, coeff_ref, send_ref)
 
 
-def last_body(recv_ref, spread_ref, base_ref, target_ref, out_ref):
-    finish(recv_ref, spread_ref, base_ref, target_ref, out_ref)
+def last_body(recv_ref, two_ref, four_ref, eight_ref, rows_ref, transfer_ref, base_ref, target_ref, out_ref):
+    spread = spread_blocks(two_ref, four_ref, eight_ref, rows_ref, transfer_ref)
+    finish(recv_ref, spread, base_ref, target_ref, out_ref)
 
 
 def shape(*dims, dtype=BF16):
@@ -311,7 +316,10 @@
                 [pltpu.VMEM((8, panels_here), F32)],
             )(panels, other, near_mask)[0]
         base = nearby(value, other, kernel)[0]
-        arrived, four, base = together(arrived, four, base)
+        if choice is None:
+            arrived, four, kernel = together(arrived, four, kernel)
+        else:
+            arrived, four, base = together(arrived, four, base)
         if choice is None:
             order = ORDER
             merged, choice = first_merge(arrived)
@@ -321,21 +329,20 @@
         merged, four = together(merged, four)
         received = lax.all_to_all(merged, "a", 0, 0, axis_index_groups=[order], tiled=True)
         eight = swap(jnp.concatenate([two, four], axis=1), "x", 3)
-        spread = spreading(two, four, eight, cluster_coupling, leaf_transfer)[0]
-        return received, base, spread, choice, kernel
+        return received, base, (two, four, eight, cluster_coupling, leaf_transfer), choice, kernel
 
     operands = (
         out_leaf, out_wide.reshape(OUTS), out_target, panels, density, source_basis, leaf_transfer, coupling
     )
     send, packet, place = first(*[pltpu.with_memory_space_constraint(array, pltpu.HBM) for array in operands])
-    received, base, spread, choice, kernel = couple(density, send, packet, None, None)
+    received, base, clusters, choice, kernel = couple(density, send, packet, None, None)
     first_pass, send, packet = call(
         middle_body, "middle", [values, shape(PEERS, CHUNK, 128), shape(RIGHT_SIDES, packet_width)],
         [VM, VM, VM, VM, SM, VM, VM, VM], [coeff_work],
-    )(received, spread, base, target_basis, place, source_basis, leaf_transfer, coupling)
-
-    received, base, spread, choice, kernel = couple(first_pass, send, packet, choice, kernel)
-    second_pass = call(last_body, "last", [values], [VM] * 4)(received, spread, base, target_basis)[0]
+    )(received, spreading(*clusters)[0], base, target_basis, place, source_basis, leaf_transfer, coupling)
+
+    received, base, clusters, choice, kernel = couple(first_pass, send, packet, choice, kernel)
+    second_pass = call(last_body, "last", [values], [VM] * 8)(received, *clusters, base, target_basis)[0]
     return (first_pass, second_pass)
 
 

time: 81.4 us -> 81 us (level)
    pallas_call x3 -> x2, Pallas kernels: 1.67 us -> 1.63 us  [the longest x1 1.2 us: shards(): call(last_body, 'last', [values], [VM] * 8)]
  transfers between devices with their start and end apart: 10 -> 10, of which waited for: 7 -> 7; matrix products, arithmetic and copies ran while one was open for 1% -> 1% of each run, Pallas kernels for 4% -> 3%
where the time goes in v9:
time: 81 us; the launch traced here: 80.3 us
  starting transfers between devices  52.8 us (65%)
  waiting for transfers between devices  15.6 us (19%)
  Pallas kernels  10.6 us (13%)
    all_to_all x2, starting transfers between devices, couple(): lax.all_to_all(merged, 'a', 0, 0, axis_index_groups=[order], tiled=True)  27.8 us
    ppermute x6, waiting for transfers between devices, swap(): return lax.ppermute(block, axis, [(i, i ^ distance) for i in range(count)])  15.1 us
    ppermute x6, starting transfers between devices, swap(): return lax.ppermute(block, axis, [(i, i ^ distance) for i in range(count)])  13.4 us
    all_to_all x2, starting transfers between devices, couple(): arrived = lax.all_to_all(send, ('b', 'y'), 0, 0, tiled=True)  11.6 us
    pallas_call x1, Pallas kernels, shards(): first(*[pltpu.with_memory_space_constraint(array, pltpu.HBM) for array in...  2.74 us
    pallas_call x1, Pallas kernels, shards(): call(middle_body, 'middle', [values, shape(PEERS, CHUNK, 128), shape(RIGH...  2.17 us
    pallas_call x1, Pallas kernels, couple(): call(kernel_body, 'kernel', [shape(panels_here, 2 * panels_here)], [VM, V...  1.72 us
  transfers between devices with their start and end apart: 10, of which 7 were waited for; matrix products, arithmetic and copies ran while one was open for 1% of the time, Pallas kernels for 3%

profile of v9, /device:TPU:14, one launch (start us, length us, event | category | flops | bytes accessed | tf_op | source)
XLA Modules:
  0.0 80.3 jit_solution(16044311933437924661)
XLA Ops:
  0.6 2.7 %first.1 = (bf16[8,272,128]{2,1,0:T(8,128)(2,1)}, bf16[80,640]{1,0:T(8,128)(2,1)S(1)}, s32[128]{0:T(128)S(1)}) custom-call(s32[64]{0:T(128)} %leaf_hbm.1, s32[64]{0:T(128)} %bitcast.1, s32[64]{0:T(128)} %target_hbm.1, f32[7,512]{1,0:T(8,128)} %own_ref.1, bf16[32,512]{1,0:T(8,128)(2,1)} %value_ref.1, bf16[64,512]{1,0:T(8,128)(2,1)} %basis_ref.1, ...), custom_call_target="tpu_custom_call" | custom-call | tf_op jit(solution)/shard_map/first/pallas_call | solution.py:337
  3.4 6.3 %all-to-all-start = ((bf16[8,272,128]{2,1,0:T(8,128)(2,1)}), bf16[8,272,128]{2,1,0:T(8,128)(2,1)S(1)}, u32[]{:S(2)}, u32[]{:S(2)}) async-start(bf16[8,272,128]{2,1,0:T(8,128)(2,1)} %get-tuple-element.20), calls=%async_computation | async-start | bytes 1114112 | tf_op jit(solution)/shard_map/all_to_all | solution.py:309
  9.7 1.9 %collective-permute-start = (bf16[80,640]{1,0:T(8,128)(2,1)S(1)}, bf16[80,640]{1,0:T(8,128)(2,1)S(1)}, u32[]{:S(2)}, u32[]{:S(2)}) collective-permute-start(bf16[80,640]{1,0:T(8,128)(2,1)S(1)} %get-tuple-element.21), channel_id=1, source_target_pairs={{0,1},{1,0},{2,3},{3,2},{4,5},{5,4},{6,7},{7,6},{8,9},{9,8},{10,11... | collective-permute-start | bytes 307208 | tf_op jit(solution)/shard_map/ppermute | solution.py:272
  11.6 1.3 %collective-permute-done.packet_ref.other_ref = bf16[80,640]{1,0:T(8,128)(2,1)S(1)} collective-permute-done((bf16[80,640]{1,0:T(8,128)(2,1)S(1)}, bf16[80,640]{1,0:T(8,128)(2,1)S(1)}, u32[]{:S(2)}, u32[]{:S(2)}) %collective-permute-start) | collective-permute-done | bytes 102432 | tf_op jit(solution)/shard_map/ppermute | solution.py:272
  12.9 0.1 pad_maximum_fusion.2.two_ref
  12.9 2.7 %collective-permute-start.1 = (bf16[32,128]{1,0:T(8,128)(2,1)S(1)}, bf16[32,128]{1,0:T(8,128)(2,1)S(1)}, u32[]{:S(2)}, u32[]{:S(2)}) collective-permute-start(bf16[32,128]{1,0:T(8,128)(2,1)S(1)} %pad_maximum_fusion.2.two_ref), channel_id=1, source_target_pairs={{0,2},{2,0},{4,6},{6,4},{1,3},{3,1},{5,7},{7,5},{8,10},{10,8},{12,... | collective-permute-start | bytes 24584 | tf_op jit(solution)/shard_map/ppermute | solution.py:272
  15.7 1.7 %kernel.1.kernel_ref = bf16[512,1024]{1,0:T(8,128)(2,1)S(1)} custom-call(f32[7,512]{1,0:T(8,128)S(1)} %copy-done.5, bf16[80,640]{1,0:T(8,128)(2,1)S(1)} %collective-permute-done.packet_ref.other_ref, s32[4,8]{1,0:T(4,128)S(1)} %copy-done.7), custom_call_target="tpu_custom_call" | custom-call | tf_op jit(solution)/shard_map/kernel/pallas_call | solution.py:314
  17.4 1.1 %collective-permute-done.1.four_ref = bf16[32,128]{1,0:T(8,128)(2,1)S(1)} collective-permute-done((bf16[32,128]{1,0:T(8,128)(2,1)S(1)}, bf16[32,128]{1,0:T(8,128)(2,1)S(1)}, u32[]{:S(2)}, u32[]{:S(2)}) %collective-permute-start.1) | collective-permute-done | bytes 8224 | tf_op jit(solution)/shard_map/ppermute | solution.py:272
  18.5 0.9 %first_merge.1 = (bf16[8,64,128]{2,1,0:T(8,128)(2,1)}, bf16[8,64,256]{2,1,0:T(8,128)(2,1)S(1)}) custom-call(bf16[8,272,128]{2,1,0:T(8,128)(2,1)S(1)} %all-to-all-done.recv_ref), custom_call_target="tpu_custom_call" | custom-call | tf_op jit(solution)/shard_map/first_merge/pallas_call | solution.py:325
  19.4 15.8 %all-to-all-start.1 = ((bf16[8,64,128]{2,1,0:T(8,128)(2,1)}), bf16[8,64,128]{2,1,0:T(8,128)(2,1)S(1)}, u32[]{:S(2)}, u32[]{:S(2)}) async-start(bf16[8,64,128]{2,1,0:T(8,128)(2,1)} %get-tuple-element.25), calls=%async_computation.1 | async-start | bytes 262144 | tf_op jit(solution)/shard_map/all_to_all | solution.py:330
  35.2 0.1 pad_maximum_fusion
  35.2 2.4 %collective-permute-start.2 = (bf16[32,256]{1,0:T(8,128)(2,1)S(1)}, bf16[32,256]{1,0:T(8,128)(2,1)S(1)}, u32[]{:S(2)}, u32[]{:S(2)}) collective-permute-start(bf16[32,256]{1,0:T(8,128)(2,1)S(1)} %pad_maximum_fusion), channel_id=1, source_target_pairs={{0,6},{2,4},{4,2},{6,0},{1,7},{3,5},{5,3},{7,1},{8,14},{10,12},{12... | collective-permute-start | bytes 49160 | tf_op jit(solution)/shard_map/ppermute | solution.py:272
  37.6 0.1 copy.13.rows_ref
  37.8 0.3 nearby.2.base_ref
  38.1 0.0 copy-start.3
  38.1 4.0 %collective-permute-done.2.eight_ref = bf16[32,256]{1,0:T(8,128)(2,1)S(1)} collective-permute-done((bf16[32,256]{1,0:T(8,128)(2,1)S(1)}, bf16[32,256]{1,0:T(8,128)(2,1)S(1)}, u32[]{:S(2)}, u32[]{:S(2)}) %collective-permute-start.2) | collective-permute-done | bytes 16416 | tf_op jit(solution)/shard_map/ppermute | solution.py:272
  42.1 0.4 spread.1.spread_ref
  42.5 0.5 all-to-all-done.1.recv_ref
  43.0 2.2 %middle.1 = (bf16[32,512]{1,0:T(8,128)(2,1)}, bf16[8,256,128]{2,1,0:T(8,128)(2,1)}, bf16[32,640]{1,0:T(8,128)(2,1)S(1)}) custom-call(bf16[8,64,128]{2,1,0:T(8,128)(2,1)S(1)} %all-to-all-done.1.recv_ref, f32[64,128]{1,0:T(8,128)S(1)} %spread.1.spread_ref, f32[32,512]{1,0:T(8,128)S(1)} %nearby.2.base_ref, bf16[64,512]{1,0:T(8,128)(2,1)S(1)} %copy-done.2, ...), custom_call_target="tpu_custom_call" | custom-call | tf_op jit(solution)/shard_map/middle/pallas_call | solution.py:339
  45.2 5.3 %all-to-all-start.2 = ((bf16[8,256,128]{2,1,0:T(8,128)(2,1)}), bf16[8,256,128]{2,1,0:T(8,128)(2,1)S(1)}, u32[]{:S(2)}, u32[]{:S(2)}) async-start(bf16[8,256,128]{2,1,0:T(8,128)(2,1)} %get-tuple-element.29), calls=%async_computation.2 | async-start | bytes 1048576 | tf_op jit(solution)/shard_map/all_to_all | solution.py:309
  50.4 2.0 %collective-permute-start.3 = (bf16[32,640]{1,0:T(8,128)(2,1)S(1)}, bf16[32,640]{1,0:T(8,128)(2,1)S(1)}, u32[]{:S(2)}, u32[]{:S(2)}) collective-permute-start(bf16[32,640]{1,0:T(8,128)(2,1)S(1)} %get-tuple-element.30), channel_id=1, source_target_pairs={{0,1},{1,0},{2,3},{3,2},{4,5},{5,4},{6,7},{7,6},{8,9},{9,8},{10,11... | collective-permute-start | bytes 122888 | tf_op jit(solution)/shard_map/ppermute | solution.py:272
  52.5 1.2 %collective-permute-done.3.other_ref = bf16[32,640]{1,0:T(8,128)(2,1)S(1)} collective-permute-done((bf16[32,640]{1,0:T(8,128)(2,1)S(1)}, bf16[32,640]{1,0:T(8,128)(2,1)S(1)}, u32[]{:S(2)}, u32[]{:S(2)}) %collective-permute-start.3) | collective-permute-done | bytes 40992 | tf_op jit(solution)/shard_map/ppermute | solution.py:272
  53.7 0.1 pad_maximum_fusion.3.two_ref
  53.8 2.0 %collective-permute-start.4 = (bf16[32,128]{1,0:T(8,128)(2,1)S(1)}, bf16[32,128]{1,0:T(8,128)(2,1)S(1)}, u32[]{:S(2)}, u32[]{:S(2)}) collective-permute-start(bf16[32,128]{1,0:T(8,128)(2,1)S(1)} %pad_maximum_fusion.3.two_ref), channel_id=1, source_target_pairs={{0,2},{2,0},{4,6},{6,4},{1,3},{3,1},{5,7},{7,5},{8,10},{10,8},{12,... | collective-permute-start | bytes 24584 | tf_op jit(solution)/shard_map/ppermute | solution.py:272
  55.8 0.3 nearby.3.base_ref
  56.1 3.2 %collective-permute-done.4.four_ref = bf16[32,128]{1,0:T(8,128)(2,1)S(1)} collective-permute-done((bf16[32,128]{1,0:T(8,128)(2,1)S(1)}, bf16[32,128]{1,0:T(8,128)(2,1)S(1)}, u32[]{:S(2)}, u32[]{:S(2)}) %collective-permute-start.4) | collective-permute-done | bytes 8224 | tf_op jit(solution)/shard_map/ppermute | solution.py:272
  59.3 0.9 %merge.1 = bf16[8,64,128]{2,1,0:T(8,128)(2,1)} custom-call(bf16[8,256,128]{2,1,0:T(8,128)(2,1)S(1)} %all-to-all-done.2.recv_ref, bf16[8,64,256]{2,1,0:T(8,128)(2,1)S(1)} %get-tuple-element.33.choice_ref), custom_call_target="tpu_custom_call" | custom-call | tf_op jit(solution)/shard_map/merge/pallas_call | solution.py:328
  60.2 12.0 %all-to-all-start.3 = ((bf16[8,64,128]{2,1,0:T(8,128)(2,1)}), bf16[8,64,128]{2,1,0:T(8,128)(2,1)S(1)}, u32[]{:S(2)}, u32[]{:S(2)}) async-start(bf16[8,64,128]{2,1,0:T(8,128)(2,1)} %merge.1), calls=%async_computation.3 | async-start | bytes 262144 | tf_op jit(solution)/shard_map/all_to_all | solution.py:330
  72.2 0.1 pad_maximum_fusion.1
  72.3 2.4 %collective-permute-start.5 = (bf16[32,256]{1,0:T(8,128)(2,1)S(1)}, bf16[32,256]{1,0:T(8,128)(2,1)S(1)}, u32[]{:S(2)}, u32[]{:S(2)}) collective-permute-start(bf16[32,256]{1,0:T(8,128)(2,1)S(1)} %pad_maximum_fusion.1), channel_id=1, source_target_pairs={{0,6},{2,4},{4,2},{6,0},{1,7},{3,5},{5,3},{7,1},{8,14},{10,12},{12... | collective-permute-start | bytes 49160 | tf_op jit(solution)/shard_map/ppermute | solution.py:272
  74.6 4.5 %collective-permute-done.5.eight_ref = bf16[32,256]{1,0:T(8,128)(2,1)S(1)} collective-permute-done((bf16[32,256]{1,0:T(8,128)(2,1)S(1)}, bf16[32,256]{1,0:T(8,128)(2,1)S(1)}, u32[]{:S(2)}, u32[]{:S(2)}) %collective-permute-start.5) | collective-permute-done | bytes 16416 | tf_op jit(solution)/shard_map/ppermute | solution.py:272
  79.1 1.2 %last.1 = bf16[32,512]{1,0:T(8,128)(2,1)} custom-call(bf16[8,64,128]{2,1,0:T(8,128)(2,1)S(1)} %all-to-all-done.3.recv_ref, bf16[32,128]{1,0:T(8,128)(2,1)S(1)} %pad_maximum_fusion.3.two_ref, bf16[32,128]{1,0:T(8,128)(2,1)S(1)} %collective-permute-done.4.four_ref, bf16[32,256]{1,0:T(8,128)(2,1)S(1)} %collective-permute-done.5.eight_ref, ...), custom_call_target="tpu_custom_call" | custom-call | tf_op jit(solution)/shard_map/last/pallas_call | solution.py:345
  (24 shorter events, 0.1 us)
Async XLA Ops:
  3.4 15.1 %all-to-all-start = ((bf16[8,272,128]{2,1,0:T(8,128)(2,1)}), bf16[8,272,128]{2,1,0:T(8,128)(2,1)S(1)}, u32[]{:S(2)}, u32[]{:S(2)}) async-start(bf16[8,272,128]{2,1,0:T(8,128)(2,1)} %get-tuple-element.20), calls=%async_computation | async-start | bytes 1114112 | tf_op jit(solution)/shard_map/all_to_all | solution.py:309
  9.7 3.2 %collective-permute-start = (bf16[80,640]{1,0:T(8,128)(2,1)S(1)}, bf16[80,640]{1,0:T(8,128)(2,1)S(1)}, u32[]{:S(2)}, u32[]{:S(2)}) collective-permute-start(bf16[80,640]{1,0:T(8,128)(2,1)S(1)} %get-tuple-element.21), channel_id=1, source_target_pairs={{0,1},{1,0},{2,3},{3,2},{4,5},{5,4},{6,7},{7,6},{8,9},{9,8},{10,11... | collective-permute-start | bytes 307208 | tf_op jit(solution)/shard_map/ppermute | solution.py:272
  12.9 2.8 %copy-start.5 = (f32[7,512]{1,0:T(8,128)S(1)}, f32[7,512]{1,0:T(8,128)}, u32[]{:S(2)}) copy-start(f32[7,512]{1,0:T(8,128)} %own_ref.1) | copy-start | bytes 43012
  12.9 2.8 %copy-start.7 = (s32[4,8]{1,0:T(4,128)S(1)}, s32[4,8]{1,0:T(4,128)}, u32[]{:S(2)}) copy-start(s32[4,8]{1,0:T(4,128)} %mask_ref.1) | copy-start | bytes 388
  12.9 5.5 %collective-permute-start.1 = (bf16[32,128]{1,0:T(8,128)(2,1)S(1)}, bf16[32,128]{1,0:T(8,128)(2,1)S(1)}, u32[]{:S(2)}, u32[]{:S(2)}) collective-permute-start(bf16[32,128]{1,0:T(8,128)(2,1)S(1)} %pad_maximum_fusion.2.two_ref), channel_id=1, source_target_pairs={{0,2},{2,0},{4,6},{6,4},{1,3},{3,1},{5,7},{7,5},{8,10},{10,8},{12,... | collective-permute-start | bytes 24584 | tf_op jit(solution)/shard_map/ppermute | solution.py:272
  18.5 19.2 %copy-start.8 = (bf16[1,512,64]{1,2,0:T(8,128)(2,1)S(1)}, bf16[1,512,64]{1,2,0:T(8,128)(2,1)}, u32[]{:S(2)}) copy-start(bf16[1,512,64]{1,2,0:T(8,128)(2,1)} %param.16) | copy-start | bytes 196612
  18.5 19.3 %copy-start.4 = (bf16[32,512]{1,0:T(8,128)(2,1)S(1)}, bf16[32,512]{1,0:T(8,128)(2,1)}, u32[]{:S(2)}) copy-start(bf16[32,512]{1,0:T(8,128)(2,1)} %value_ref.1) | copy-start | bytes 98308
  19.3 23.6 %copy-start = (bf16[64,64,64]{2,1,0:T(8,128)(2,1)S(1)}, bf16[64,64,64]{2,1,0:T(8,128)(2,1)}, u32[]{:S(2)}) copy-start(bf16[64,64,64]{2,1,0:T(8,128)(2,1)} %coupling_ref.1) | copy-start | bytes 1572868
  19.4 23.6 %all-to-all-start.1 = ((bf16[8,64,128]{2,1,0:T(8,128)(2,1)}), bf16[8,64,128]{2,1,0:T(8,128)(2,1)S(1)}, u32[]{:S(2)}, u32[]{:S(2)}) async-start(bf16[8,64,128]{2,1,0:T(8,128)(2,1)} %get-tuple-element.25), calls=%async_computation.1 | async-start | bytes 262144 | tf_op jit(solution)/shard_map/all_to_all | solution.py:330
  35.2 6.8 %collective-permute-start.2 = (bf16[32,256]{1,0:T(8,128)(2,1)S(1)}, bf16[32,256]{1,0:T(8,128)(2,1)S(1)}, u32[]{:S(2)}, u32[]{:S(2)}) collective-permute-start(bf16[32,256]{1,0:T(8,128)(2,1)S(1)} %pad_maximum_fusion), channel_id=1, source_target_pairs={{0,6},{2,4},{4,2},{6,0},{1,7},{3,5},{5,3},{7,1},{8,14},{10,12},{12... | collective-permute-start | bytes 49160 | tf_op jit(solution)/shard_map/ppermute | solution.py:272
  37.8 4.3 %copy-start.1 = (bf16[4,64,64]{2,1,0:T(8,128)(2,1)S(1)}, bf16[4,64,64]{2,1,0:T(8,128)(2,1)}, u32[]{:S(2)}) copy-start(bf16[4,64,64]{2,1,0:T(8,128)(2,1)} %transfer_ref.5) | copy-start | bytes 98308
  38.1 4.9 %copy-start.2 = (bf16[64,512]{1,0:T(8,128)(2,1)S(1)}, bf16[64,512]{1,0:T(8,128)(2,1)}, u32[]{:S(2)}) copy-start(bf16[64,512]{1,0:T(8,128)(2,1)} %target_ref.3) | copy-start | bytes 196612
  38.1 4.9 %copy-start.3 = (bf16[64,512]{1,0:T(8,128)(2,1)S(1)}, bf16[64,512]{1,0:T(8,128)(2,1)}, u32[]{:S(2)}) copy-start(bf16[64,512]{1,0:T(8,128)(2,1)} %basis_ref.1) | copy-start | bytes 196612
  45.2 14.1 %all-to-all-start.2 = ((bf16[8,256,128]{2,1,0:T(8,128)(2,1)}), bf16[8,256,128]{2,1,0:T(8,128)(2,1)S(1)}, u32[]{:S(2)}, u32[]{:S(2)}) async-start(bf16[8,256,128]{2,1,0:T(8,128)(2,1)} %get-tuple-element.29), calls=%async_computation.2 | async-start | bytes 1048576 | tf_op jit(solution)/shard_map/all_to_all | solution.py:309
  50.4 5.3 %copy-start.6 = (bf16[32,512]{1,0:T(8,128)(2,1)S(1)}, bf16[32,512]{1,0:T(8,128)(2,1)}, u32[]{:S(2)}) copy-start(bf16[32,512]{1,0:T(8,128)(2,1)} %get-tuple-element.18.value_ref) | copy-start | bytes 98308
  50.4 3.2 %collective-permute-start.3 = (bf16[32,640]{1,0:T(8,128)(2,1)S(1)}, bf16[32,640]{1,0:T(8,128)(2,1)S(1)}, u32[]{:S(2)}, u32[]{:S(2)}) collective-permute-start(bf16[32,640]{1,0:T(8,128)(2,1)S(1)} %get-tuple-element.30), channel_id=1, source_target_pairs={{0,1},{1,0},{2,3},{3,2},{4,5},{5,4},{6,7},{7,6},{8,9},{9,8},{10,11... | collective-permute-start | bytes 122888 | tf_op jit(solution)/shard_map/ppermute | solution.py:272
  53.8 5.5 %collective-permute-start.4 = (bf16[32,128]{1,0:T(8,128)(2,1)S(1)}, bf16[32,128]{1,0:T(8,128)(2,1)S(1)}, u32[]{:S(2)}, u32[]{:S(2)}) collective-permute-start(bf16[32,128]{1,0:T(8,128)(2,1)S(1)} %pad_maximum_fusion.3.two_ref), channel_id=1, source_target_pairs={{0,2},{2,0},{4,6},{6,4},{1,3},{3,1},{5,7},{7,5},{8,10},{10,8},{12,... | collective-permute-start | bytes 24584 | tf_op jit(solution)/shard_map/ppermute | solution.py:272
  60.2 18.9 %all-to-all-start.3 = ((bf16[8,64,128]{2,1,0:T(8,128)(2,1)}), bf16[8,64,128]{2,1,0:T(8,128)(2,1)S(1)}, u32[]{:S(2)}, u32[]{:S(2)}) async-start(bf16[8,64,128]{2,1,0:T(8,128)(2,1)} %merge.1), calls=%async_computation.3 | async-start | bytes 262144 | tf_op jit(solution)/shard_map/all_to_all | solution.py:330
  72.3 6.8 %collective-permute-start.5 = (bf16[32,256]{1,0:T(8,128)(2,1)S(1)}, bf16[32,256]{1,0:T(8,128)(2,1)S(1)}, u32[]{:S(2)}, u32[]{:S(2)}) collective-permute-start(bf16[32,256]{1,0:T(8,128)(2,1)S(1)} %pad_maximum_fusion.1), channel_id=1, source_target_pairs={{0,6},{2,4},{4,2},{6,0},{1,7},{3,5},{5,3},{7,1},{8,14},{10,12},{12... | collective-permute-start | bytes 49160 | tf_op jit(solution)/shard_map/ppermute | solution.py:272

commit v10 on v9

--- a/solution.py
+++ b/solution.py
@@ -238,10 +238,11 @@
 
 
 def middle_body(
-    recv_ref, spread_ref, base_ref, target_ref, place_ref, basis_ref, transfer_ref, coupling_ref,
+    recv_ref, two_ref, four_ref, eight_ref, rows_ref, base_ref, target_ref, place_ref, basis_ref, transfer_ref, coupling_ref,
     out_ref, send_ref, swap_ref, coeff_ref,
 ):
-    finish(recv_ref, spread_ref[...], base_ref, target_ref, out_ref)
+    spread = spread_blocks(two_ref, four_ref, eight_ref, rows_ref, transfer_ref)
+    finish(recv_ref, spread, base_ref, target_ref, out_ref)
     clear(send_ref)
     leaf_coeffs(out_ref, basis_ref, transfer_ref, swap_ref, coeff_ref)
     for block in range(OUTS):
@@ -338,8 +339,8 @@
     received, base, clusters, choice, kernel = couple(density, send, packet, None, None)
     first_pass, send, packet = call(
         middle_body, "middle", [values, shape(PEERS, CHUNK, 128), shape(RIGHT_SIDES, packet_width)],
-        [VM, VM, VM, VM, SM, VM, VM, VM], [coeff_work],
-    )(received, spreading(*clusters)[0], base, target_basis, place, source_basis, leaf_transfer, coupling)
+        [VM] * 7 + [SM] + [VM] * 3, [coeff_work],
+    )(received, *clusters[:4], base, target_basis, place, source_basis, leaf_transfer, coupling)
 
     received, base, clusters, choice, kernel = couple(first_pass, send, packet, choice, kernel)
     second_pass = call(last_body, "last", [values], [VM] * 8)(received, *clusters, base, target_basis)[0]

time: 81 us -> 81 us (level)
  the two profiles are of different devices: /device:TPU:14 before, /device:TPU:8 now
where the time goes in v10:
time: 81 us; the launch traced here: 80.3 us
  starting transfers between devices  56.9 us (70%)
  waiting for transfers between devices  11.5 us (14%)
  Pallas kernels  10.6 us (13%)
  between operations  0.83 us (1%)
    all_to_all x2, starting transfers between devices, couple(): lax.all_to_all(merged, 'a', 0, 0, axis_index_groups=[order], tiled=True)  24.9 us
    ppermute x6, starting transfers between devices, swap(): return lax.ppermute(block, axis, [(i, i ^ distance) for i in range(count)])  17.9 us
    all_to_all x2, starting transfers between devices, couple(): arrived = lax.all_to_all(send, ('b', 'y'), 0, 0, tiled=True)  14.1 us
    ppermute x6, waiting for transfers between devices, swap(): return lax.ppermute(block, axis, [(i, i ^ distance) for i in range(count)])  10.6 us
    pallas_call x1, Pallas kernels, shards(): first(*[pltpu.with_memory_space_constraint(array, pltpu.HBM) for array in...  2.74 us
    pallas_call x1, Pallas kernels, shards(): call(middle_body, 'middle', [values, shape(PEERS, CHUNK, 128), shape(RIGH...  2.6 us
    pallas_call x1, Pallas kernels, couple(): call(kernel_body, 'kernel', [shape(panels_here, 2 * panels_here)], [VM, V...  1.72 us
  transfers between devices with their start and end apart: 10, of which 7 were waited for; matrix products, arithmetic and copies ran while one was open for 1% of the time, Pallas kernels for 3%

profile of v10, /device:TPU:8, one launch (start us, length us, event | category | flops | bytes accessed | tf_op | source)
XLA Modules:
  0.0 80.3 jit_solution(7138590735838321028)
XLA Ops:
  0.6 2.7 %first.1 = (bf16[8,272,128]{2,1,0:T(8,128)(2,1)}, bf16[80,640]{1,0:T(8,128)(2,1)S(1)}, s32[128]{0:T(128)S(1)}) custom-call(s32[64]{0:T(128)} %leaf_hbm.1, s32[64]{0:T(128)} %bitcast.1, s32[64]{0:T(128)} %target_hbm.1, f32[7,512]{1,0:T(8,128)} %own_ref.1, bf16[32,512]{1,0:T(8,128)(2,1)} %value_ref.1, bf16[64,512]{1,0:T(8,128)(2,1)} %basis_ref.1, ...), custom_call_target="tpu_custom_call" | custom-call | tf_op jit(solution)/shard_map/first/pallas_call | solution.py:338
  3.4 9.3 %all-to-all-start = ((bf16[8,272,128]{2,1,0:T(8,128)(2,1)}), bf16[8,272,128]{2,1,0:T(8,128)(2,1)S(1)}, u32[]{:S(2)}, u32[]{:S(2)}) async-start(bf16[8,272,128]{2,1,0:T(8,128)(2,1)} %get-tuple-element.20), calls=%async_computation | async-start | bytes 1114112 | tf_op jit(solution)/shard_map/all_to_all | solution.py:310
  12.7 1.9 %collective-permute-start = (bf16[80,640]{1,0:T(8,128)(2,1)S(1)}, bf16[80,640]{1,0:T(8,128)(2,1)S(1)}, u32[]{:S(2)}, u32[]{:S(2)}) collective-permute-start(bf16[80,640]{1,0:T(8,128)(2,1)S(1)} %get-tuple-element.21), channel_id=1, source_target_pairs={{0,1},{1,0},{2,3},{3,2},{4,5},{5,4},{6,7},{7,6},{8,9},{9,8},{10,11... | collective-permute-start | bytes 307208 | tf_op jit(solution)/shard_map/ppermute | solution.py:273
  14.6 1.3 %collective-permute-done.packet_ref.other_ref = bf16[80,640]{1,0:T(8,128)(2,1)S(1)} collective-permute-done((bf16[80,640]{1,0:T(8,128)(2,1)S(1)}, bf16[80,640]{1,0:T(8,128)(2,1)S(1)}, u32[]{:S(2)}, u32[]{:S(2)}) %collective-permute-start) | collective-permute-done | bytes 102432 | tf_op jit(solution)/shard_map/ppermute | solution.py:273
  15.9 0.1 pad_maximum_fusion.2.two_ref
  15.9 1.9 %collective-permute-start.1 = (bf16[32,128]{1,0:T(8,128)(2,1)S(1)}, bf16[32,128]{1,0:T(8,128)(2,1)S(1)}, u32[]{:S(2)}, u32[]{:S(2)}) collective-permute-start(bf16[32,128]{1,0:T(8,128)(2,1)S(1)} %pad_maximum_fusion.2.two_ref), channel_id=1, source_target_pairs={{0,2},{2,0},{4,6},{6,4},{1,3},{3,1},{5,7},{7,5},{8,10},{10,8},{12,... | collective-permute-start | bytes 24584 | tf_op jit(solution)/shard_map/ppermute | solution.py:273
  17.9 0.0 copy-start.8
  17.9 1.7 %kernel.1.kernel_ref = bf16[512,1024]{1,0:T(8,128)(2,1)S(1)} custom-call(f32[7,512]{1,0:T(8,128)S(1)} %copy-done.5, bf16[80,640]{1,0:T(8,128)(2,1)S(1)} %collective-permute-done.packet_ref.other_ref, s32[4,8]{1,0:T(4,128)S(1)} %copy-done.7), custom_call_target="tpu_custom_call" | custom-call | tf_op jit(solution)/shard_map/kernel/pallas_call | solution.py:315
  19.6 0.0 copy-start
  19.6 1.8 %collective-permute-done.1.four_ref = bf16[32,128]{1,0:T(8,128)(2,1)S(1)} collective-permute-done((bf16[32,128]{1,0:T(8,128)(2,1)S(1)}, bf16[32,128]{1,0:T(8,128)(2,1)S(1)}, u32[]{:S(2)}, u32[]{:S(2)}) %collective-permute-start.1) | collective-permute-done | bytes 8224 | tf_op jit(solution)/shard_map/ppermute | solution.py:273
  21.5 0.9 %first_merge.1 = (bf16[8,64,128]{2,1,0:T(8,128)(2,1)}, bf16[8,64,256]{2,1,0:T(8,128)(2,1)S(1)}) custom-call(bf16[8,272,128]{2,1,0:T(8,128)(2,1)S(1)} %all-to-all-done.recv_ref), custom_call_target="tpu_custom_call" | custom-call | tf_op jit(solution)/shard_map/first_merge/pallas_call | solution.py:326
  22.3 12.7 %all-to-all-start.1 = ((bf16[8,64,128]{2,1,0:T(8,128)(2,1)}), bf16[8,64,128]{2,1,0:T(8,128)(2,1)S(1)}, u32[]{:S(2)}, u32[]{:S(2)}) async-start(bf16[8,64,128]{2,1,0:T(8,128)(2,1)} %get-tuple-element.25), calls=%async_computation.1 | async-start | bytes 262144 | tf_op jit(solution)/shard_map/all_to_all | solution.py:331
  35.0 0.1 pad_maximum_fusion
  35.1 4.7 %collective-permute-start.2 = (bf16[32,256]{1,0:T(8,128)(2,1)S(1)}, bf16[32,256]{1,0:T(8,128)(2,1)S(1)}, u32[]{:S(2)}, u32[]{:S(2)}) collective-permute-start(bf16[32,256]{1,0:T(8,128)(2,1)S(1)} %pad_maximum_fusion), channel_id=1, source_target_pairs={{0,6},{2,4},{4,2},{6,0},{1,7},{3,5},{5,3},{7,1},{8,14},{10,12},{12... | collective-permute-start | bytes 49160 | tf_op jit(solution)/shard_map/ppermute | solution.py:273
  39.8 0.1 copy.13.rows_ref
  40.0 0.3 nearby.2.base_ref
  40.3 1.7 %collective-permute-done.2.eight_ref = bf16[32,256]{1,0:T(8,128)(2,1)S(1)} collective-permute-done((bf16[32,256]{1,0:T(8,128)(2,1)S(1)}, bf16[32,256]{1,0:T(8,128)(2,1)S(1)}, u32[]{:S(2)}, u32[]{:S(2)}) %collective-permute-start.2) | collective-permute-done | bytes 16416 | tf_op jit(solution)/shard_map/ppermute | solution.py:273
  41.9 0.9 %all-to-all-done.1.recv_ref = bf16[8,64,128]{2,1,0:T(8,128)(2,1)S(1)} async-done(((bf16[8,64,128]{2,1,0:T(8,128)(2,1)}), bf16[8,64,128]{2,1,0:T(8,128)(2,1)S(1)}, u32[]{:S(2)}, u32[]{:S(2)}) %all-to-all-start.1) | async-done | bytes 131104 | tf_op jit(solution)/shard_map/all_to_all | solution.py:331
  42.9 2.6 %middle.1 = (bf16[32,512]{1,0:T(8,128)(2,1)}, bf16[8,256,128]{2,1,0:T(8,128)(2,1)}, bf16[32,640]{1,0:T(8,128)(2,1)S(1)}) custom-call(bf16[8,64,128]{2,1,0:T(8,128)(2,1)S(1)} %all-to-all-done.1.recv_ref, bf16[32,128]{1,0:T(8,128)(2,1)S(1)} %pad_maximum_fusion.2.two_ref, bf16[32,128]{1,0:T(8,128)(2,1)S(1)} %collective-permute-done.1.four_ref, ...), custom_call_target="tpu_custom_call" | custom-call | tf_op jit(solution)/shard_map/middle/pallas_call | solution.py:340
  45.5 4.8 %all-to-all-start.2 = ((bf16[8,256,128]{2,1,0:T(8,128)(2,1)}), bf16[8,256,128]{2,1,0:T(8,128)(2,1)S(1)}, u32[]{:S(2)}, u32[]{:S(2)}) async-start(bf16[8,256,128]{2,1,0:T(8,128)(2,1)} %get-tuple-element.29), calls=%async_computation.2 | async-start | bytes 1048576 | tf_op jit(solution)/shard_map/all_to_all | solution.py:310
  50.3 2.0 %collective-permute-start.3 = (bf16[32,640]{1,0:T(8,128)(2,1)S(1)}, bf16[32,640]{1,0:T(8,128)(2,1)S(1)}, u32[]{:S(2)}, u32[]{:S(2)}) collective-permute-start(bf16[32,640]{1,0:T(8,128)(2,1)S(1)} %get-tuple-element.30), channel_id=1, source_target_pairs={{0,1},{1,0},{2,3},{3,2},{4,5},{5,4},{6,7},{7,6},{8,9},{9,8},{10,11... | collective-permute-start | bytes 122888 | tf_op jit(solution)/shard_map/ppermute | solution.py:273
  52.3 1.2 %collective-permute-done.3.other_ref = bf16[32,640]{1,0:T(8,128)(2,1)S(1)} collective-permute-done((bf16[32,640]{1,0:T(8,128)(2,1)S(1)}, bf16[32,640]{1,0:T(8,128)(2,1)S(1)}, u32[]{:S(2)}, u32[]{:S(2)}) %collective-permute-start.3) | collective-permute-done | bytes 40992 | tf_op jit(solution)/shard_map/ppermute | solution.py:273
  53.5 0.1 pad_maximum_fusion.3.two_ref
  53.6 2.9 %collective-permute-start.4 = (bf16[32,128]{1,0:T(8,128)(2,1)S(1)}, bf16[32,128]{1,0:T(8,128)(2,1)S(1)}, u32[]{:S(2)}, u32[]{:S(2)}) collective-permute-start(bf16[32,128]{1,0:T(8,128)(2,1)S(1)} %pad_maximum_fusion.3.two_ref), channel_id=1, source_target_pairs={{0,2},{2,0},{4,6},{6,4},{1,3},{3,1},{5,7},{7,5},{8,10},{10,8},{12,... | collective-permute-start | bytes 24584 | tf_op jit(solution)/shard_map/ppermute | solution.py:273
  56.5 0.3 nearby.3.base_ref
  56.9 2.3 %collective-permute-done.4.four_ref = bf16[32,128]{1,0:T(8,128)(2,1)S(1)} collective-permute-done((bf16[32,128]{1,0:T(8,128)(2,1)S(1)}, bf16[32,128]{1,0:T(8,128)(2,1)S(1)}, u32[]{:S(2)}, u32[]{:S(2)}) %collective-permute-start.4) | collective-permute-done | bytes 8224 | tf_op jit(solution)/shard_map/ppermute | solution.py:273
  59.1 0.9 %merge.1 = bf16[8,64,128]{2,1,0:T(8,128)(2,1)} custom-call(bf16[8,256,128]{2,1,0:T(8,128)(2,1)S(1)} %all-to-all-done.2.recv_ref, bf16[8,64,256]{2,1,0:T(8,128)(2,1)S(1)} %get-tuple-element.33.choice_ref), custom_call_target="tpu_custom_call" | custom-call | tf_op jit(solution)/shard_map/merge/pallas_call | solution.py:329
  60.0 12.2 %all-to-all-start.3 = ((bf16[8,64,128]{2,1,0:T(8,128)(2,1)}), bf16[8,64,128]{2,1,0:T(8,128)(2,1)S(1)}, u32[]{:S(2)}, u32[]{:S(2)}) async-start(bf16[8,64,128]{2,1,0:T(8,128)(2,1)} %merge.1), calls=%async_computation.3 | async-start | bytes 262144 | tf_op jit(solution)/shard_map/all_to_all | solution.py:331
  72.2 0.1 pad_maximum_fusion.1
  72.3 4.5 %collective-permute-start.5 = (bf16[32,256]{1,0:T(8,128)(2,1)S(1)}, bf16[32,256]{1,0:T(8,128)(2,1)S(1)}, u32[]{:S(2)}, u32[]{:S(2)}) collective-permute-start(bf16[32,256]{1,0:T(8,128)(2,1)S(1)} %pad_maximum_fusion.1), channel_id=1, source_target_pairs={{0,6},{2,4},{4,2},{6,0},{1,7},{3,5},{5,3},{7,1},{8,14},{10,12},{12... | collective-permute-start | bytes 49160 | tf_op jit(solution)/shard_map/ppermute | solution.py:273
  76.8 2.4 %collective-permute-done.5.eight_ref = bf16[32,256]{1,0:T(8,128)(2,1)S(1)} collective-permute-done((bf16[32,256]{1,0:T(8,128)(2,1)S(1)}, bf16[32,256]{1,0:T(8,128)(2,1)S(1)}, u32[]{:S(2)}, u32[]{:S(2)}) %collective-permute-start.5) | collective-permute-done | bytes 16416 | tf_op jit(solution)/shard_map/ppermute | solution.py:273
  79.1 1.2 %last.1 = bf16[32,512]{1,0:T(8,128)(2,1)} custom-call(bf16[8,64,128]{2,1,0:T(8,128)(2,1)S(1)} %all-to-all-done.3.recv_ref, bf16[32,128]{1,0:T(8,128)(2,1)S(1)} %pad_maximum_fusion.3.two_ref, bf16[32,128]{1,0:T(8,128)(2,1)S(1)} %collective-permute-done.4.four_ref, bf16[32,256]{1,0:T(8,128)(2,1)S(1)} %collective-permute-done.5.eight_ref, ...), custom_call_target="tpu_custom_call" | custom-call | tf_op jit(solution)/shard_map/last/pallas_call | solution.py:346
  (23 shorter events, 0.1 us)
Async XLA Ops:
  3.4 18.1 %all-to-all-start = ((bf16[8,272,128]{2,1,0:T(8,128)(2,1)}), bf16[8,272,128]{2,1,0:T(8,128)(2,1)S(1)}, u32[]{:S(2)}, u32[]{:S(2)}) async-start(bf16[8,272,128]{2,1,0:T(8,128)(2,1)} %get-tuple-element.20), calls=%async_computation | async-start | bytes 1114112 | tf_op jit(solution)/shard_map/all_to_all | solution.py:310
  12.7 3.2 %collective-permute-start = (bf16[80,640]{1,0:T(8,128)(2,1)S(1)}, bf16[80,640]{1,0:T(8,128)(2,1)S(1)}, u32[]{:S(2)}, u32[]{:S(2)}) collective-permute-start(bf16[80,640]{1,0:T(8,128)(2,1)S(1)} %get-tuple-element.21), channel_id=1, source_target_pairs={{0,1},{1,0},{2,3},{3,2},{4,5},{5,4},{6,7},{7,6},{8,9},{9,8},{10,11... | collective-permute-start | bytes 307208 | tf_op jit(solution)/shard_map/ppermute | solution.py:273
  15.8 2.0 %copy-start.5 = (f32[7,512]{1,0:T(8,128)S(1)}, f32[7,512]{1,0:T(8,128)}, u32[]{:S(2)}) copy-start(f32[7,512]{1,0:T(8,128)} %own_ref.1) | copy-start | bytes 43012
  15.9 2.0 %copy-start.7 = (s32[4,8]{1,0:T(4,128)S(1)}, s32[4,8]{1,0:T(4,128)}, u32[]{:S(2)}) copy-start(s32[4,8]{1,0:T(4,128)} %mask_ref.1) | copy-start | bytes 388
  15.9 5.5 %collective-permute-start.1 = (bf16[32,128]{1,0:T(8,128)(2,1)S(1)}, bf16[32,128]{1,0:T(8,128)(2,1)S(1)}, u32[]{:S(2)}, u32[]{:S(2)}) collective-permute-start(bf16[32,128]{1,0:T(8,128)(2,1)S(1)} %pad_maximum_fusion.2.two_ref), channel_id=1, source_target_pairs={{0,2},{2,0},{4,6},{6,4},{1,3},{3,1},{5,7},{7,5},{8,10},{10,8},{12,... | collective-permute-start | bytes 24584 | tf_op jit(solution)/shard_map/ppermute | solution.py:273
  17.9 21.9 %copy-start.8 = (bf16[1,512,64]{1,2,0:T(8,128)(2,1)S(1)}, bf16[1,512,64]{1,2,0:T(8,128)(2,1)}, u32[]{:S(2)}) copy-start(bf16[1,512,64]{1,2,0:T(8,128)(2,1)} %param.16) | copy-start | bytes 196612
  17.9 22.0 %copy-start.4 = (bf16[32,512]{1,0:T(8,128)(2,1)S(1)}, bf16[32,512]{1,0:T(8,128)(2,1)}, u32[]{:S(2)}) copy-start(bf16[32,512]{1,0:T(8,128)(2,1)} %value_ref.1) | copy-start | bytes 98308
  19.6 23.2 %copy-start = (bf16[64,64,64]{2,1,0:T(8,128)(2,1)S(1)}, bf16[64,64,64]{2,1,0:T(8,128)(2,1)}, u32[]{:S(2)}) copy-start(bf16[64,64,64]{2,1,0:T(8,128)(2,1)} %coupling_ref.1) | copy-start | bytes 1572868
  22.3 20.5 %all-to-all-start.1 = ((bf16[8,64,128]{2,1,0:T(8,128)(2,1)}), bf16[8,64,128]{2,1,0:T(8,128)(2,1)S(1)}, u32[]{:S(2)}, u32[]{:S(2)}) async-start(bf16[8,64,128]{2,1,0:T(8,128)(2,1)} %get-tuple-element.25), calls=%async_computation.1 | async-start | bytes 262144 | tf_op jit(solution)/shard_map/all_to_all | solution.py:331
  35.1 6.8 %collective-permute-start.2 = (bf16[32,256]{1,0:T(8,128)(2,1)S(1)}, bf16[32,256]{1,0:T(8,128)(2,1)S(1)}, u32[]{:S(2)}, u32[]{:S(2)}) collective-permute-start(bf16[32,256]{1,0:T(8,128)(2,1)S(1)} %pad_maximum_fusion), channel_id=1, source_target_pairs={{0,6},{2,4},{4,2},{6,0},{1,7},{3,5},{5,3},{7,1},{8,14},{10,12},{12... | collective-permute-start | bytes 49160 | tf_op jit(solution)/shard_map/ppermute | solution.py:273
  39.9 3.0 %copy-start.1 = (bf16[4,64,64]{2,1,0:T(8,128)(2,1)S(1)}, bf16[4,64,64]{2,1,0:T(8,128)(2,1)}, u32[]{:S(2)}) copy-start(bf16[4,64,64]{2,1,0:T(8,128)(2,1)} %transfer_ref.3) | copy-start | bytes 98308
  39.9 2.9 %copy-start.2 = (bf16[64,512]{1,0:T(8,128)(2,1)S(1)}, bf16[64,512]{1,0:T(8,128)(2,1)}, u32[]{:S(2)}) copy-start(bf16[64,512]{1,0:T(8,128)(2,1)} %target_ref.3) | copy-start | bytes 196612
  39.9 2.9 %copy-start.3 = (bf16[64,512]{1,0:T(8,128)(2,1)S(1)}, bf16[64,512]{1,0:T(8,128)(2,1)}, u32[]{:S(2)}) copy-start(bf16[64,512]{1,0:T(8,128)(2,1)} %basis_ref.1) | copy-start | bytes 196612
  45.5 13.7 %all-to-all-start.2 = ((bf16[8,256,128]{2,1,0:T(8,128)(2,1)}), bf16[8,256,128]{2,1,0:T(8,128)(2,1)S(1)}, u32[]{:S(2)}, u32[]{:S(2)}) async-start(bf16[8,256,128]{2,1,0:T(8,128)(2,1)} %get-tuple-element.29), calls=%async_computation.2 | async-start | bytes 1048576 | tf_op jit(solution)/shard_map/all_to_all | solution.py:310
  50.3 6.3 %copy-start.6 = (bf16[32,512]{1,0:T(8,128)(2,1)S(1)}, bf16[32,512]{1,0:T(8,128)(2,1)}, u32[]{:S(2)}) copy-start(bf16[32,512]{1,0:T(8,128)(2,1)} %get-tuple-element.18.value_ref) | copy-start | bytes 98308
  50.3 3.2 %collective-permute-start.3 = (bf16[32,640]{1,0:T(8,128)(2,1)S(1)}, bf16[32,640]{1,0:T(8,128)(2,1)S(1)}, u32[]{:S(2)}, u32[]{:S(2)}) collective-permute-start(bf16[32,640]{1,0:T(8,128)(2,1)S(1)} %get-tuple-element.30), channel_id=1, source_target_pairs={{0,1},{1,0},{2,3},{3,2},{4,5},{5,4},{6,7},{7,6},{8,9},{9,8},{10,11... | collective-permute-start | bytes 122888 | tf_op jit(solution)/shard_map/ppermute | solution.py:273
  53.6 5.5 %collective-permute-start.4 = (bf16[32,128]{1,0:T(8,128)(2,1)S(1)}, bf16[32,128]{1,0:T(8,128)(2,1)S(1)}, u32[]{:S(2)}, u32[]{:S(2)}) collective-permute-start(bf16[32,128]{1,0:T(8,128)(2,1)S(1)} %pad_maximum_fusion.3.two_ref), channel_id=1, source_target_pairs={{0,2},{2,0},{4,6},{6,4},{1,3},{3,1},{5,7},{7,5},{8,10},{10,8},{12,... | collective-permute-start | bytes 24584 | tf_op jit(solution)/shard_map/ppermute | solution.py:273
  60.0 19.1 %all-to-all-start.3 = ((bf16[8,64,128]{2,1,0:T(8,128)(2,1)}), bf16[8,64,128]{2,1,0:T(8,128)(2,1)S(1)}, u32[]{:S(2)}, u32[]{:S(2)}) async-start(bf16[8,64,128]{2,1,0:T(8,128)(2,1)} %merge.1), calls=%async_computation.3 | async-start | bytes 262144 | tf_op jit(solution)/shard_map/all_to_all | solution.py:331
  72.3 6.8 %collective-permute-start.5 = (bf16[32,256]{1,0:T(8,128)(2,1)S(1)}, bf16[32,256]{1,0:T(8,128)(2,1)S(1)}, u32[]{:S(2)}, u32[]{:S(2)}) collective-permute-start(bf16[32,256]{1,0:T(8,128)(2,1)S(1)} %pad_maximum_fusion.1), channel_id=1, source_target_pairs={{0,6},{2,4},{4,2},{6,0},{1,7},{3,5},{5,3},{7,1},{8,14},{10,12},{12... | collective-permute-start | bytes 49160 | tf_op jit(solution)/shard_map/ppermute | solution.py:273

commit v11 on v10

--- a/solution.py
+++ b/solution.py
@@ -105,6 +105,7 @@
     for wide in range(NA * PEERS):
         count_ref[wide] = 0
     clear(send_ref)
+    swap_ref[RIGHT_SIDES:, LEAVES * LEAF_SIZE :] = jnp.zeros((PARTS * ROWS, 128), BF16)
     for copy in copies[:3]:
         copy.wait()
     row_ref[...] = jnp.zeros((2 * PEERS * NA, 128), F32)
@@ -126,7 +127,6 @@
     for copy in copies[3:7]:
         copy.wait()
     leaf_coeffs(value_ref, basis_ref, transfer_ref, swap_ref, coeff_ref)
-    swap_ref[RIGHT_SIDES:, :] = jnp.zeros((PARTS * ROWS, LEAVES * LEAF_SIZE + 128), BF16)
     panel = jnp.concatenate([panel_ref[...], jnp.zeros((ROWS - 7, LEAVES * LEAF_SIZE), F32)], axis=0)
     for part, rows in enumerate(split_parts(panel)):
         start = RIGHT_SIDES + part * ROWS

time: 81 us -> 81 us (level)
  no operation moved by 1% of the time
where the time goes in v11:
time: 81 us; the launch traced here: 80.3 us
  starting transfers between devices  56.9 us (70%)
  waiting for transfers between devices  11.5 us (14%)
  Pallas kernels  10.6 us (13%)
  between operations  0.83 us (1%)
    all_to_all x2, starting transfers between devices, couple(): lax.all_to_all(merged, 'a', 0, 0, axis_index_groups=[order], tiled=True)  24.9 us
    ppermute x6, starting transfers between devices, swap(): return lax.ppermute(block, axis, [(i, i ^ distance) for i in range(count)])  17.9 us
    all_to_all x2, starting transfers between devices, couple(): arrived = lax.all_to_all(send, ('b', 'y'), 0, 0, tiled=True)  14.1 us
    ppermute x6, waiting for transfers between devices, swap(): return lax.ppermute(block, axis, [(i, i ^ distance) for i in range(count)])  10.6 us
    pallas_call x1, Pallas kernels, shards(): first(*[pltpu.with_memory_space_constraint(array, pltpu.HBM) for array in...  2.75 us
    pallas_call x1, Pallas kernels, shards(): call(middle_body, 'middle', [values, shape(PEERS, CHUNK, 128), shape(RIGH...  2.6 us
    pallas_call x1, Pallas kernels, couple(): call(kernel_body, 'kernel', [shape(panels_here, 2 * panels_here)], [VM, V...  1.72 us
  transfers between devices with their start and end apart: 10, of which 7 were waited for; matrix products, arithmetic and copies ran while one was open for 1% of the time, Pallas kernels for 3%

profile of v11, /device:TPU:8, one launch (start us, length us, event | category | flops | bytes accessed | tf_op | source)
XLA Modules:
  0.0 80.3 jit_solution(17641547662070617637)
XLA Ops:
  0.6 2.7 %first.1 = (bf16[8,272,128]{2,1,0:T(8,128)(2,1)}, bf16[80,640]{1,0:T(8,128)(2,1)S(1)}, s32[128]{0:T(128)S(1)}) custom-call(s32[64]{0:T(128)} %leaf_hbm.1, s32[64]{0:T(128)} %bitcast.1, s32[64]{0:T(128)} %target_hbm.1, f32[7,512]{1,0:T(8,128)} %own_ref.1, bf16[32,512]{1,0:T(8,128)(2,1)} %value_ref.1, bf16[64,512]{1,0:T(8,128)(2,1)} %basis_ref.1, ...), custom_call_target="tpu_custom_call" | custom-call | tf_op jit(solution)/shard_map/first/pallas_call | solution.py:338
  3.4 9.3 %all-to-all-start = ((bf16[8,272,128]{2,1,0:T(8,128)(2,1)}), bf16[8,272,128]{2,1,0:T(8,128)(2,1)S(1)}, u32[]{:S(2)}, u32[]{:S(2)}) async-start(bf16[8,272,128]{2,1,0:T(8,128)(2,1)} %get-tuple-element.20), calls=%async_computation | async-start | bytes 1114112 | tf_op jit(solution)/shard_map/all_to_all | solution.py:310
  12.7 1.9 %collective-permute-start = (bf16[80,640]{1,0:T(8,128)(2,1)S(1)}, bf16[80,640]{1,0:T(8,128)(2,1)S(1)}, u32[]{:S(2)}, u32[]{:S(2)}) collective-permute-start(bf16[80,640]{1,0:T(8,128)(2,1)S(1)} %get-tuple-element.21), channel_id=1, source_target_pairs={{0,1},{1,0},{2,3},{3,2},{4,5},{5,4},{6,7},{7,6},{8,9},{9,8},{10,11... | collective-permute-start | bytes 307208 | tf_op jit(solution)/shard_map/ppermute | solution.py:273
  14.6 1.3 %collective-permute-done.packet_ref.other_ref = bf16[80,640]{1,0:T(8,128)(2,1)S(1)} collective-permute-done((bf16[80,640]{1,0:T(8,128)(2,1)S(1)}, bf16[80,640]{1,0:T(8,128)(2,1)S(1)}, u32[]{:S(2)}, u32[]{:S(2)}) %collective-permute-start) | collective-permute-done | bytes 102432 | tf_op jit(solution)/shard_map/ppermute | solution.py:273
  15.9 0.1 pad_maximum_fusion.2.two_ref
  15.9 1.9 %collective-permute-start.1 = (bf16[32,128]{1,0:T(8,128)(2,1)S(1)}, bf16[32,128]{1,0:T(8,128)(2,1)S(1)}, u32[]{:S(2)}, u32[]{:S(2)}) collective-permute-start(bf16[32,128]{1,0:T(8,128)(2,1)S(1)} %pad_maximum_fusion.2.two_ref), channel_id=1, source_target_pairs={{0,2},{2,0},{4,6},{6,4},{1,3},{3,1},{5,7},{7,5},{8,10},{10,8},{12,... | collective-permute-start | bytes 24584 | tf_op jit(solution)/shard_map/ppermute | solution.py:273
  17.9 0.0 copy-start.4
  17.9 1.7 %kernel.1.kernel_ref = bf16[512,1024]{1,0:T(8,128)(2,1)S(1)} custom-call(f32[7,512]{1,0:T(8,128)S(1)} %copy-done.5, bf16[80,640]{1,0:T(8,128)(2,1)S(1)} %collective-permute-done.packet_ref.other_ref, s32[4,8]{1,0:T(4,128)S(1)} %copy-done.7), custom_call_target="tpu_custom_call" | custom-call | tf_op jit(solution)/shard_map/kernel/pallas_call | solution.py:315
  19.6 0.0 copy-start
  19.6 1.8 %collective-permute-done.1.four_ref = bf16[32,128]{1,0:T(8,128)(2,1)S(1)} collective-permute-done((bf16[32,128]{1,0:T(8,128)(2,1)S(1)}, bf16[32,128]{1,0:T(8,128)(2,1)S(1)}, u32[]{:S(2)}, u32[]{:S(2)}) %collective-permute-start.1) | collective-permute-done | bytes 8224 | tf_op jit(solution)/shard_map/ppermute | solution.py:273
  21.5 0.9 %first_merge.1 = (bf16[8,64,128]{2,1,0:T(8,128)(2,1)}, bf16[8,64,256]{2,1,0:T(8,128)(2,1)S(1)}) custom-call(bf16[8,272,128]{2,1,0:T(8,128)(2,1)S(1)} %all-to-all-done.recv_ref), custom_call_target="tpu_custom_call" | custom-call | tf_op jit(solution)/shard_map/first_merge/pallas_call | solution.py:326
  22.3 12.7 %all-to-all-start.1 = ((bf16[8,64,128]{2,1,0:T(8,128)(2,1)}), bf16[8,64,128]{2,1,0:T(8,128)(2,1)S(1)}, u32[]{:S(2)}, u32[]{:S(2)}) async-start(bf16[8,64,128]{2,1,0:T(8,128)(2,1)} %get-tuple-element.25), calls=%async_computation.1 | async-start | bytes 262144 | tf_op jit(solution)/shard_map/all_to_all | solution.py:331
  35.0 0.1 pad_maximum_fusion
  35.1 4.7 %collective-permute-start.2 = (bf16[32,256]{1,0:T(8,128)(2,1)S(1)}, bf16[32,256]{1,0:T(8,128)(2,1)S(1)}, u32[]{:S(2)}, u32[]{:S(2)}) collective-permute-start(bf16[32,256]{1,0:T(8,128)(2,1)S(1)} %pad_maximum_fusion), channel_id=1, source_target_pairs={{0,6},{2,4},{4,2},{6,0},{1,7},{3,5},{5,3},{7,1},{8,14},{10,12},{12... | collective-permute-start | bytes 49160 | tf_op jit(solution)/shard_map/ppermute | solution.py:273
  39.8 0.1 copy.13.rows_ref
  40.0 0.3 nearby.2.base_ref
  40.3 1.7 %collective-permute-done.2.eight_ref = bf16[32,256]{1,0:T(8,128)(2,1)S(1)} collective-permute-done((bf16[32,256]{1,0:T(8,128)(2,1)S(1)}, bf16[32,256]{1,0:T(8,128)(2,1)S(1)}, u32[]{:S(2)}, u32[]{:S(2)}) %collective-permute-start.2) | collective-permute-done | bytes 16416 | tf_op jit(solution)/shard_map/ppermute | solution.py:273
  41.9 0.9 %all-to-all-done.1.recv_ref = bf16[8,64,128]{2,1,0:T(8,128)(2,1)S(1)} async-done(((bf16[8,64,128]{2,1,0:T(8,128)(2,1)}), bf16[8,64,128]{2,1,0:T(8,128)(2,1)S(1)}, u32[]{:S(2)}, u32[]{:S(2)}) %all-to-all-start.1) | async-done | bytes 131104 | tf_op jit(solution)/shard_map/all_to_all | solution.py:331
  42.9 2.6 %middle.1 = (bf16[32,512]{1,0:T(8,128)(2,1)}, bf16[8,256,128]{2,1,0:T(8,128)(2,1)}, bf16[32,640]{1,0:T(8,128)(2,1)S(1)}) custom-call(bf16[8,64,128]{2,1,0:T(8,128)(2,1)S(1)} %all-to-all-done.1.recv_ref, bf16[32,128]{1,0:T(8,128)(2,1)S(1)} %pad_maximum_fusion.2.two_ref, bf16[32,128]{1,0:T(8,128)(2,1)S(1)} %collective-permute-done.1.four_ref, ...), custom_call_target="tpu_custom_call" | custom-call | tf_op jit(solution)/shard_map/middle/pallas_call | solution.py:340
  45.5 4.8 %all-to-all-start.2 = ((bf16[8,256,128]{2,1,0:T(8,128)(2,1)}), bf16[8,256,128]{2,1,0:T(8,128)(2,1)S(1)}, u32[]{:S(2)}, u32[]{:S(2)}) async-start(bf16[8,256,128]{2,1,0:T(8,128)(2,1)} %get-tuple-element.29), calls=%async_computation.2 | async-start | bytes 1048576 | tf_op jit(solution)/shard_map/all_to_all | solution.py:310
  50.3 2.0 %collective-permute-start.3 = (bf16[32,640]{1,0:T(8,128)(2,1)S(1)}, bf16[32,640]{1,0:T(8,128)(2,1)S(1)}, u32[]{:S(2)}, u32[]{:S(2)}) collective-permute-start(bf16[32,640]{1,0:T(8,128)(2,1)S(1)} %get-tuple-element.30), channel_id=1, source_target_pairs={{0,1},{1,0},{2,3},{3,2},{4,5},{5,4},{6,7},{7,6},{8,9},{9,8},{10,11... | collective-permute-start | bytes 122888 | tf_op jit(solution)/shard_map/ppermute | solution.py:273
  52.3 1.2 %collective-permute-done.3.other_ref = bf16[32,640]{1,0:T(8,128)(2,1)S(1)} collective-permute-done((bf16[32,640]{1,0:T(8,128)(2,1)S(1)}, bf16[32,640]{1,0:T(8,128)(2,1)S(1)}, u32[]{:S(2)}, u32[]{:S(2)}) %collective-permute-start.3) | collective-permute-done | bytes 40992 | tf_op jit(solution)/shard_map/ppermute | solution.py:273
  53.5 0.1 pad_maximum_fusion.3.two_ref
  53.6 2.9 %collective-permute-start.4 = (bf16[32,128]{1,0:T(8,128)(2,1)S(1)}, bf16[32,128]{1,0:T(8,128)(2,1)S(1)}, u32[]{:S(2)}, u32[]{:S(2)}) collective-permute-start(bf16[32,128]{1,0:T(8,128)(2,1)S(1)} %pad_maximum_fusion.3.two_ref), channel_id=1, source_target_pairs={{0,2},{2,0},{4,6},{6,4},{1,3},{3,1},{5,7},{7,5},{8,10},{10,8},{12,... | collective-permute-start | bytes 24584 | tf_op jit(solution)/shard_map/ppermute | solution.py:273
  56.5 0.3 nearby.3.base_ref
  56.9 2.3 %collective-permute-done.4.four_ref = bf16[32,128]{1,0:T(8,128)(2,1)S(1)} collective-permute-done((bf16[32,128]{1,0:T(8,128)(2,1)S(1)}, bf16[32,128]{1,0:T(8,128)(2,1)S(1)}, u32[]{:S(2)}, u32[]{:S(2)}) %collective-permute-start.4) | collective-permute-done | bytes 8224 | tf_op jit(solution)/shard_map/ppermute | solution.py:273
  59.1 0.9 %merge.1 = bf16[8,64,128]{2,1,0:T(8,128)(2,1)} custom-call(bf16[8,256,128]{2,1,0:T(8,128)(2,1)S(1)} %all-to-all-done.2.recv_ref, bf16[8,64,256]{2,1,0:T(8,128)(2,1)S(1)} %get-tuple-element.33.choice_ref), custom_call_target="tpu_custom_call" | custom-call | tf_op jit(solution)/shard_map/merge/pallas_call | solution.py:329
  60.0 12.2 %all-to-all-start.3 = ((bf16[8,64,128]{2,1,0:T(8,128)(2,1)}), bf16[8,64,128]{2,1,0:T(8,128)(2,1)S(1)}, u32[]{:S(2)}, u32[]{:S(2)}) async-start(bf16[8,64,128]{2,1,0:T(8,128)(2,1)} %merge.1), calls=%async_computation.3 | async-start | bytes 262144 | tf_op jit(solution)/shard_map/all_to_all | solution.py:331
  72.2 0.1 pad_maximum_fusion.1
  72.3 4.5 %collective-permute-start.5 = (bf16[32,256]{1,0:T(8,128)(2,1)S(1)}, bf16[32,256]{1,0:T(8,128)(2,1)S(1)}, u32[]{:S(2)}, u32[]{:S(2)}) collective-permute-start(bf16[32,256]{1,0:T(8,128)(2,1)S(1)} %pad_maximum_fusion.1), channel_id=1, source_target_pairs={{0,6},{2,4},{4,2},{6,0},{1,7},{3,5},{5,3},{7,1},{8,14},{10,12},{12... | collective-permute-start | bytes 49160 | tf_op jit(solution)/shard_map/ppermute | solution.py:273
  76.8 2.4 %collective-permute-done.5.eight_ref = bf16[32,256]{1,0:T(8,128)(2,1)S(1)} collective-permute-done((bf16[32,256]{1,0:T(8,128)(2,1)S(1)}, bf16[32,256]{1,0:T(8,128)(2,1)S(1)}, u32[]{:S(2)}, u32[]{:S(2)}) %collective-permute-start.5) | collective-permute-done | bytes 16416 | tf_op jit(solution)/shard_map/ppermute | solution.py:273
  79.1 1.2 %last.1 = bf16[32,512]{1,0:T(8,128)(2,1)} custom-call(bf16[8,64,128]{2,1,0:T(8,128)(2,1)S(1)} %all-to-all-done.3.recv_ref, bf16[32,128]{1,0:T(8,128)(2,1)S(1)} %pad_maximum_fusion.3.two_ref, bf16[32,128]{1,0:T(8,128)(2,1)S(1)} %collective-permute-done.4.four_ref, bf16[32,256]{1,0:T(8,128)(2,1)S(1)} %collective-permute-done.5.eight_ref, ...), custom_call_target="tpu_custom_call" | custom-call | tf_op jit(solution)/shard_map/last/pallas_call | solution.py:346
  (23 shorter events, 0.1 us)
Async XLA Ops:
  3.4 18.1 %all-to-all-start = ((bf16[8,272,128]{2,1,0:T(8,128)(2,1)}), bf16[8,272,128]{2,1,0:T(8,128)(2,1)S(1)}, u32[]{:S(2)}, u32[]{:S(2)}) async-start(bf16[8,272,128]{2,1,0:T(8,128)(2,1)} %get-tuple-element.20), calls=%async_computation | async-start | bytes 1114112 | tf_op jit(solution)/shard_map/all_to_all | solution.py:310
  12.7 3.2 %collective-permute-start = (bf16[80,640]{1,0:T(8,128)(2,1)S(1)}, bf16[80,640]{1,0:T(8,128)(2,1)S(1)}, u32[]{:S(2)}, u32[]{:S(2)}) collective-permute-start(bf16[80,640]{1,0:T(8,128)(2,1)S(1)} %get-tuple-element.21), channel_id=1, source_target_pairs={{0,1},{1,0},{2,3},{3,2},{4,5},{5,4},{6,7},{7,6},{8,9},{9,8},{10,11... | collective-permute-start | bytes 307208 | tf_op jit(solution)/shard_map/ppermute | solution.py:273
  15.8 2.0 %copy-start.5 = (f32[7,512]{1,0:T(8,128)S(1)}, f32[7,512]{1,0:T(8,128)}, u32[]{:S(2)}) copy-start(f32[7,512]{1,0:T(8,128)} %own_ref.1) | copy-start | bytes 43012
  15.9 2.0 %copy-start.7 = (s32[4,8]{1,0:T(4,128)S(1)}, s32[4,8]{1,0:T(4,128)}, u32[]{:S(2)}) copy-start(s32[4,8]{1,0:T(4,128)} %mask_ref.1) | copy-start | bytes 388
  15.9 5.5 %collective-permute-start.1 = (bf16[32,128]{1,0:T(8,128)(2,1)S(1)}, bf16[32,128]{1,0:T(8,128)(2,1)S(1)}, u32[]{:S(2)}, u32[]{:S(2)}) collective-permute-start(bf16[32,128]{1,0:T(8,128)(2,1)S(1)} %pad_maximum_fusion.2.two_ref), channel_id=1, source_target_pairs={{0,2},{2,0},{4,6},{6,4},{1,3},{3,1},{5,7},{7,5},{8,10},{10,8},{12,... | collective-permute-start | bytes 24584 | tf_op jit(solution)/shard_map/ppermute | solution.py:273
  17.9 21.9 %copy-start.8 = (bf16[1,512,64]{1,2,0:T(8,128)(2,1)S(1)}, bf16[1,512,64]{1,2,0:T(8,128)(2,1)}, u32[]{:S(2)}) copy-start(bf16[1,512,64]{1,2,0:T(8,128)(2,1)} %param.16) | copy-start | bytes 196612
  17.9 22.0 %copy-start.4 = (bf16[32,512]{1,0:T(8,128)(2,1)S(1)}, bf16[32,512]{1,0:T(8,128)(2,1)}, u32[]{:S(2)}) copy-start(bf16[32,512]{1,0:T(8,128)(2,1)} %value_ref.1) | copy-start | bytes 98308
  19.6 23.2 %copy-start = (bf16[64,64,64]{2,1,0:T(8,128)(2,1)S(1)}, bf16[64,64,64]{2,1,0:T(8,128)(2,1)}, u32[]{:S(2)}) copy-start(bf16[64,64,64]{2,1,0:T(8,128)(2,1)} %coupling_ref.1) | copy-start | bytes 1572868
  22.3 20.5 %all-to-all-start.1 = ((bf16[8,64,128]{2,1,0:T(8,128)(2,1)}), bf16[8,64,128]{2,1,0:T(8,128)(2,1)S(1)}, u32[]{:S(2)}, u32[]{:S(2)}) async-start(bf16[8,64,128]{2,1,0:T(8,128)(2,1)} %get-tuple-element.25), calls=%async_computation.1 | async-start | bytes 262144 | tf_op jit(solution)/shard_map/all_to_all | solution.py:331
  35.1 6.8 %collective-permute-start.2 = (bf16[32,256]{1,0:T(8,128)(2,1)S(1)}, bf16[32,256]{1,0:T(8,128)(2,1)S(1)}, u32[]{:S(2)}, u32[]{:S(2)}) collective-permute-start(bf16[32,256]{1,0:T(8,128)(2,1)S(1)} %pad_maximum_fusion), channel_id=1, source_target_pairs={{0,6},{2,4},{4,2},{6,0},{1,7},{3,5},{5,3},{7,1},{8,14},{10,12},{12... | collective-permute-start | bytes 49160 | tf_op jit(solution)/shard_map/ppermute | solution.py:273
  39.9 3.0 %copy-start.1 = (bf16[4,64,64]{2,1,0:T(8,128)(2,1)S(1)}, bf16[4,64,64]{2,1,0:T(8,128)(2,1)}, u32[]{:S(2)}) copy-start(bf16[4,64,64]{2,1,0:T(8,128)(2,1)} %transfer_ref.3) | copy-start | bytes 98308
  39.9 2.9 %copy-start.2 = (bf16[64,512]{1,0:T(8,128)(2,1)S(1)}, bf16[64,512]{1,0:T(8,128)(2,1)}, u32[]{:S(2)}) copy-start(bf16[64,512]{1,0:T(8,128)(2,1)} %target_ref.3) | copy-start | bytes 196612
  39.9 2.9 %copy-start.3 = (bf16[64,512]{1,0:T(8,128)(2,1)S(1)}, bf16[64,512]{1,0:T(8,128)(2,1)}, u32[]{:S(2)}) copy-start(bf16[64,512]{1,0:T(8,128)(2,1)} %basis_ref.1) | copy-start | bytes 196612
  45.5 13.7 %all-to-all-start.2 = ((bf16[8,256,128]{2,1,0:T(8,128)(2,1)}), bf16[8,256,128]{2,1,0:T(8,128)(2,1)S(1)}, u32[]{:S(2)}, u32[]{:S(2)}) async-start(bf16[8,256,128]{2,1,0:T(8,128)(2,1)} %get-tuple-element.29), calls=%async_computation.2 | async-start | bytes 1048576 | tf_op jit(solution)/shard_map/all_to_all | solution.py:310
  50.3 6.3 %copy-start.6 = (bf16[32,512]{1,0:T(8,128)(2,1)S(1)}, bf16[32,512]{1,0:T(8,128)(2,1)}, u32[]{:S(2)}) copy-start(bf16[32,512]{1,0:T(8,128)(2,1)} %get-tuple-element.18.value_ref) | copy-start | bytes 98308
  50.3 3.2 %collective-permute-start.3 = (bf16[32,640]{1,0:T(8,128)(2,1)S(1)}, bf16[32,640]{1,0:T(8,128)(2,1)S(1)}, u32[]{:S(2)}, u32[]{:S(2)}) collective-permute-start(bf16[32,640]{1,0:T(8,128)(2,1)S(1)} %get-tuple-element.30), channel_id=1, source_target_pairs={{0,1},{1,0},{2,3},{3,2},{4,5},{5,4},{6,7},{7,6},{8,9},{9,8},{10,11... | collective-permute-start | bytes 122888 | tf_op jit(solution)/shard_map/ppermute | solution.py:273
  53.6 5.5 %collective-permute-start.4 = (bf16[32,128]{1,0:T(8,128)(2,1)S(1)}, bf16[32,128]{1,0:T(8,128)(2,1)S(1)}, u32[]{:S(2)}, u32[]{:S(2)}) collective-permute-start(bf16[32,128]{1,0:T(8,128)(2,1)S(1)} %pad_maximum_fusion.3.two_ref), channel_id=1, source_target_pairs={{0,2},{2,0},{4,6},{6,4},{1,3},{3,1},{5,7},{7,5},{8,10},{10,8},{12,... | collective-permute-start | bytes 24584 | tf_op jit(solution)/shard_map/ppermute | solution.py:273
  60.0 19.1 %all-to-all-start.3 = ((bf16[8,64,128]{2,1,0:T(8,128)(2,1)}), bf16[8,64,128]{2,1,0:T(8,128)(2,1)S(1)}, u32[]{:S(2)}, u32[]{:S(2)}) async-start(bf16[8,64,128]{2,1,0:T(8,128)(2,1)} %merge.1), calls=%async_computation.3 | async-start | bytes 262144 | tf_op jit(solution)/shard_map/all_to_all | solution.py:331
  72.3 6.8 %collective-permute-start.5 = (bf16[32,256]{1,0:T(8,128)(2,1)S(1)}, bf16[32,256]{1,0:T(8,128)(2,1)S(1)}, u32[]{:S(2)}, u32[]{:S(2)}) collective-permute-start(bf16[32,256]{1,0:T(8,128)(2,1)S(1)} %pad_maximum_fusion.1), channel_id=1, source_target_pairs={{0,6},{2,4},{4,2},{6,0},{1,7},{3,5},{5,3},{7,1},{8,14},{10,12},{12... | collective-permute-start | bytes 49160 | tf_op jit(solution)/shard_map/ppermute | solution.py:273
